TPU v7x, 32 devices: a whole 2x2x4 slice. The times are simulated.
32 devices in a mesh: dp: 8 (over y, x, core), seq: 4 (over z).
Axes of the slice: x: 2, y: 2, z: 4, core: 2. Of those that a mesh axis runs over, the one named last changes fastest.
Arguments:
- inputs: bfloat16 [8, 1024, 2048], P('dp', 'seq'), may hold values from -6 to 6
- lengths: int32 [8], P('dp'), may hold values from 769 to 1024, as said below
- positions: int32 [8, 1024], P('dp', 'seq'), may hold values from 0 to 4093, as said below
- attn_gain: bfloat16 [2048], P(('dp', 'seq')), may hold values from 0.5 to 1.5
- w_query: bfloat16 [2048, 2048], P(('dp', 'seq')), may hold values from -0.125 to 0.125
- w_key: bfloat16 [2048, 512], P(('dp', 'seq')), may hold values from -0.125 to 0.125
- w_value: bfloat16 [2048, 512], P(('dp', 'seq')), may hold values from -0.125 to 0.125
- w_output: bfloat16 [2048, 2048], P(('dp', 'seq')), may hold values from -3 to 3
- ffn_gain: bfloat16 [2048], P(('dp', 'seq')), may hold values from 0.5 to 1.5
- w_gate: bfloat16 [2048, 8192], P(('dp', 'seq')), may hold values from -0.125 to 0.125
- w_up: bfloat16 [2048, 8192], P(('dp', 'seq')), may hold values from -0.125 to 0.125
- w_down: bfloat16 [2048, 8192], P(('dp', 'seq')), may hold values from -0.0625 to 0.0625
- out_grad: bfloat16 [8, 1024, 2048], P('dp', 'seq'), may hold values from -6 to 6
Outputs:
- output: bfloat16 [8, 1024, 2048], P('dp', 'seq')
- input_grad: bfloat16 [8, 1024, 2048], P('dp', 'seq')
- attn_gain_grad: float32 [2048], P(('dp', 'seq'))
- w_query_grad: float32 [2048, 2048], P(('dp', 'seq'))
- w_key_grad: float32 [2048, 512], P(('dp', 'seq'))
- w_value_grad: float32 [2048, 512], P(('dp', 'seq'))
- w_output_grad: float32 [2048, 2048], P(('dp', 'seq'))
- ffn_gain_grad: float32 [2048], P(('dp', 'seq'))
- w_gate_grad: float32 [2048, 8192], P(('dp', 'seq'))
- w_up_grad: float32 [2048, 8192], P(('dp', 'seq'))
- w_down_grad: float32 [2048, 8192], P(('dp', 'seq'))
Inputs may be any that keep to these rules, and one draw needn't show every extreme that they name: Each sequence's valid tokens are the first lengths slots; in every draw at least one sequence fills all 1024 slots. Within a sequence, positions rise by 1 or 2 from each slot to the next; a sequence's first position lies from 0 to 2047; in every draw some sequence starts at 0, and another starts at 2047 and rises by 2 at every slot.
All inputs are finite; a program needn't handle non-finite values.
Results may differ from a plain program's by a relative error of at most 0.014.
Values may be sent and summed in bfloat16 or wider, within the bound.
A program may use at most 704 MiB of HBM per device.

v0:
```python
import math

import jax
import jax.numpy as jnp
from jax import lax
from jax.sharding import PartitionSpec as P

QUERY_HEADS = 32
KEY_VALUE_HEADS = 8
HEAD_SIZE = 64


epsilon = 1e-05
rope_base = 500000.0
scale_factor = 32.0
high_factor = 4.0
initial_context = 8192.0
masked_score = -1e30


def rope_tables(positions):
    halves_index = jnp.arange(HEAD_SIZE // 2, dtype=jnp.float32)
    frequency = 1.0 / rope_base ** (2.0 * halves_index / HEAD_SIZE)
    wavelength = 2.0 * math.pi / frequency
    blending = (initial_context / wavelength - 1.0) / (high_factor - 1.0)
    middle = (1.0 - blending) * frequency / scale_factor + blending * frequency
    scaled = jnp.where(
        wavelength < initial_context / high_factor,
        frequency,
        jnp.where(wavelength > initial_context, frequency / scale_factor, middle),
    )
    angles = positions.astype(jnp.float32)[..., None] * scaled
    angles = jnp.concatenate([angles, angles], axis=-1)
    return (jnp.cos(angles), jnp.sin(angles))


def apply_rotary(vector, cos_table, sin_table):
    first_half, second_half = jnp.split(vector, 2, axis=-1)
    return vector * cos_table + jnp.concatenate([-second_half, first_half], axis=-1) * sin_table


def apply_rotary_back(gradient, cos_table, sin_table):
    turned = gradient * sin_table
    first_half, second_half = jnp.split(turned, 2, axis=-1)
    return gradient * cos_table + jnp.concatenate([second_half, -first_half], axis=-1)


def rms_norm(values, scaling):
    return values * lax.rsqrt(jnp.mean(values * values, axis=-1, keepdims=True) + epsilon) * scaling


def to_query_heads(flattened, query_group_width):
    batch_inputs, token_rows, width = flattened.shape
    reshaped_rows = flattened.reshape(
        batch_inputs, token_rows, KEY_VALUE_HEADS, query_group_width, HEAD_SIZE
    ).transpose(2, 0, 3, 1, 4)
    return reshaped_rows.reshape(
        KEY_VALUE_HEADS, batch_inputs, query_group_width * token_rows, HEAD_SIZE
    )


def from_query_heads(heads, query_group_width):
    count, batch_inputs, token_rows, depth = heads.shape
    reshaped_rows = heads.reshape(
        count, batch_inputs, query_group_width, token_rows // query_group_width, depth
    ).transpose(1, 3, 0, 2, 4)
    return reshaped_rows.reshape(
        batch_inputs, token_rows // query_group_width, count * query_group_width * depth
    )


def to_key_heads(flattened):
    batch_inputs, token_rows, width = flattened.shape
    return flattened.reshape(batch_inputs, token_rows, KEY_VALUE_HEADS, HEAD_SIZE).transpose(
        2, 0, 1, 3
    )


def from_key_heads(heads):
    count, batch_inputs, token_rows, depth = heads.shape
    return heads.transpose(1, 2, 0, 3).reshape(batch_inputs, token_rows, count * depth)


def attention_rows(query_heads, key_heads, value_heads, allowed):

    def one_head(operands):
        query_single, key_single, value_single = operands
        raw_scores = jnp.einsum(
            "fyj,fpj->fyp", query_single, key_single, preferred_element_type=jnp.float32
        ) * HEAD_SIZE ** (-0.5)
        scores = jnp.where(allowed, raw_scores, masked_score)
        row_peak = jnp.max(scores, axis=-1, keepdims=True)
        exponent = jnp.exp(scores - row_peak)
        row_total = jnp.sum(exponent, axis=-1, keepdims=True)
        attention_probabilities = (exponent / row_total).astype(jnp.bfloat16)
        attended_rows = jnp.einsum(
            "uil,ult->uit",
            attention_probabilities,
            value_single,
            preferred_element_type=jnp.float32,
        )
        return (attended_rows, row_peak[..., 0] + jnp.log(row_total[..., 0]))

    return lax.map(one_head, (query_heads, key_heads, value_heads))


def attention_back(query_heads, key_heads, value_heads, grad_heads, log_totals, allowed):

    def one_head(operands):
        query_single, key_single, value_single, grad_single, log_one = operands
        raw_scores = jnp.einsum(
            "fyj,fpj->fyp", query_single, key_single, preferred_element_type=jnp.float32
        ) * HEAD_SIZE ** (-0.5)
        scores = jnp.where(allowed, raw_scores, masked_score)
        probs_full = jnp.exp(scores - log_one[..., None])
        probabilities_lower = probs_full.astype(jnp.bfloat16)
        value_grad = jnp.einsum(
            "ain,aiv->anv", probabilities_lower, grad_single, preferred_element_type=jnp.float32
        )
        prob_grad = jnp.einsum(
            "fyj,fpj->fyp", grad_single, value_single, preferred_element_type=jnp.float32
        )
        inner = jnp.sum(probs_full * prob_grad, axis=-1, keepdims=True)
        grad_score_matrix = (probs_full * (prob_grad - inner)).astype(jnp.bfloat16)
        query_grad = jnp.einsum(
            "uil,ult->uit", grad_score_matrix, key_single, preferred_element_type=jnp.float32
        ) * HEAD_SIZE ** (-0.5)
        key_grad = jnp.einsum(
            "ain,aiv->anv", grad_score_matrix, query_single, preferred_element_type=jnp.float32
        ) * HEAD_SIZE ** (-0.5)
        return (query_grad, key_grad, value_grad)

    return lax.map(one_head, (query_heads, key_heads, value_heads, grad_heads, log_totals))


def local(
    inputs,
    lengths,
    positions,
    attn_gain,
    w_query,
    w_key,
    w_value,
    w_output,
    ffn_gain,
    w_gate,
    w_up,
    w_down,
    out_grad,
):
    sequence_count, sequence_rows, width = inputs.shape
    seq_parts = lax.axis_size("seq")
    offset = lax.axis_index("seq") * sequence_rows
    slot_total = sequence_rows * seq_parts
    query_group_width = QUERY_HEADS // KEY_VALUE_HEADS
    slot_ids = offset + jnp.arange(sequence_rows, dtype=jnp.int32)
    valid = (slot_ids[None, :] < lengths[:, None])[..., None]
    cos_table, sin_table = rope_tables(positions)
    cosine_heads = cos_table[:, :, None, :]
    sine_heads = sin_table[:, :, None, :]
    query_slot = jnp.tile(slot_ids, query_group_width)
    key_slot = jnp.arange(slot_total, dtype=jnp.int32)
    allowed = (key_slot[None, None, :] <= query_slot[None, :, None]) & (
        key_slot[None, None, :] < lengths[:, None, None]
    )
    attn_full = (
        lax.all_gather(attn_gain, ("dp", "seq"), axis=0, tiled=True),
        lax.all_gather(ffn_gain, ("dp", "seq"), axis=0, tiled=True),
        lax.all_gather(w_query, ("dp", "seq"), axis=0, tiled=True),
        lax.all_gather(w_key, ("dp", "seq"), axis=0, tiled=True),
        lax.all_gather(w_value, ("dp", "seq"), axis=0, tiled=True),
        lax.all_gather(w_output, ("dp", "seq"), axis=0, tiled=True),
    )
    ffn_gain_full = attn_full[1].astype(jnp.float32)
    inputs_f = inputs.astype(jnp.float32)
    normed_attn = rms_norm(inputs_f, attn_full[0].astype(jnp.float32)).astype(jnp.bfloat16)
    query_pre = jnp.dot(normed_attn, attn_full[2], preferred_element_type=jnp.float32)
    key_projected = jnp.dot(normed_attn, attn_full[3], preferred_element_type=jnp.float32)
    value_lower = jnp.dot(normed_attn, attn_full[4], preferred_element_type=jnp.float32).astype(
        jnp.bfloat16
    )
    query_rotated = apply_rotary(
        query_pre.reshape(sequence_count, sequence_rows, QUERY_HEADS, HEAD_SIZE),
        cosine_heads,
        sine_heads,
    )
    query_rotated = query_rotated.reshape(
        sequence_count, sequence_rows, QUERY_HEADS * HEAD_SIZE
    ).astype(jnp.bfloat16)
    key_rotated = apply_rotary(
        key_projected.reshape(sequence_count, sequence_rows, KEY_VALUE_HEADS, HEAD_SIZE),
        cosine_heads,
        sine_heads,
    )
    key_rotated = key_rotated.reshape(
        sequence_count, sequence_rows, KEY_VALUE_HEADS * HEAD_SIZE
    ).astype(jnp.bfloat16)
    key_whole, value_whole = (
        lax.all_gather(key_rotated, "seq", axis=1, tiled=True),
        lax.all_gather(value_lower, "seq", axis=1, tiled=True),
    )
    query_heads = to_query_heads(query_rotated, query_group_width)
    key_heads = to_key_heads(key_whole)
    value_heads = to_key_heads(value_whole)
    attended_heads, log_totals = attention_rows(query_heads, key_heads, value_heads, allowed)
    attended_rows = from_query_heads(attended_heads, query_group_width).astype(jnp.bfloat16)
    hidden_res = inputs_f + jnp.dot(attended_rows, attn_full[5], preferred_element_type=jnp.float32)
    normed_ffn = rms_norm(hidden_res, ffn_gain_full).astype(jnp.bfloat16)
    pieces = (
        lax.all_gather(w_gate, ("dp", "seq"), axis=0, tiled=True),
        lax.all_gather(w_up, ("dp", "seq"), axis=0, tiled=True),
    )
    normed_rows = normed_ffn
    gate_part = jnp.einsum(
        "btd,df->btf", normed_rows, pieces[0], preferred_element_type=jnp.float32
    )
    up_part = jnp.einsum("btd,df->btf", normed_rows, pieces[1], preferred_element_type=jnp.float32)
    gate_pre = gate_part
    upward = up_part
    activated = (jax.nn.silu(gate_pre) * upward).astype(jnp.bfloat16)
    down_out = jnp.einsum(
        "btf,df->btd",
        activated,
        lax.all_gather(w_down, ("dp", "seq"), axis=0, tiled=True),
        preferred_element_type=jnp.float32,
    )
    output = jnp.where(valid, hidden_res + down_out, 0.0).astype(jnp.bfloat16)
    grad_out = jnp.where(valid, out_grad.astype(jnp.float32), 0.0)
    grad_ffn = grad_out.astype(jnp.bfloat16)
    grad_rows = grad_ffn
    grad_act = jnp.einsum(
        "btd,df->btf",
        grad_rows,
        lax.all_gather(w_down, ("dp", "seq"), axis=0, tiled=True),
        preferred_element_type=jnp.float32,
    )
    unused_value, silu_back = jax.vjp(
        lambda gate_in, up_in: jax.nn.silu(gate_in) * up_in, gate_pre, upward
    )
    grad_gate, grad_up = silu_back(grad_act)
    grad_gate = grad_gate.astype(jnp.bfloat16)
    grad_up = grad_up.astype(jnp.bfloat16)
    pieces = (
        lax.all_gather(w_gate, ("dp", "seq"), axis=0, tiled=True),
        lax.all_gather(w_up, ("dp", "seq"), axis=0, tiled=True),
    )
    part = jnp.einsum("btf,df->btd", grad_gate, pieces[0], preferred_element_type=jnp.float32)
    part = part + jnp.einsum("btf,df->btd", grad_up, pieces[1], preferred_element_type=jnp.float32)
    unused_norm, norm_back = jax.vjp(rms_norm, hidden_res, ffn_gain_full)
    grad_hidden_norm, ffn_gain_term = norm_back(part)
    grad_hidden = grad_out + grad_hidden_norm
    normed_rows = normed_ffn
    gate_part = jnp.einsum(
        "btd,btf->df", normed_rows, grad_gate, preferred_element_type=jnp.float32
    )
    up_part = jnp.einsum("btd,btf->df", normed_rows, grad_up, preferred_element_type=jnp.float32)
    both = jnp.stack([gate_part, up_part], axis=1)
    grad_rows = grad_ffn
    ffn_summed = lax.psum_scatter(
        jnp.concatenate(
            [
                both,
                jnp.einsum("btd,btf->df", grad_rows, activated, preferred_element_type=jnp.float32)[
                    :, None, :
                ],
            ],
            axis=1,
        ),
        ("dp", "seq"),
        scatter_dimension=0,
        tiled=True,
    )
    gate_grad = ffn_summed[:, 0, :]
    up_grad = ffn_summed[:, 1, :]
    down_grad = ffn_summed[:, 2, :]
    attn_back = (
        lax.all_gather(attn_gain, ("dp", "seq"), axis=0, tiled=True),
        lax.all_gather(w_query, ("dp", "seq"), axis=0, tiled=True),
        lax.all_gather(w_key, ("dp", "seq"), axis=0, tiled=True),
        lax.all_gather(w_value, ("dp", "seq"), axis=0, tiled=True),
        lax.all_gather(w_output, ("dp", "seq"), axis=0, tiled=True),
    )
    grad_branch = grad_hidden.astype(jnp.bfloat16)
    output_term = jnp.einsum(
        "btq,btd->qd", attended_rows, grad_branch, preferred_element_type=jnp.float32
    )
    grad_attended = jnp.einsum(
        "btd,qd->btq", grad_branch, attn_back[4], preferred_element_type=jnp.float32
    )
    grad_heads = to_query_heads(grad_attended.astype(jnp.bfloat16), query_group_width)
    query_grad, key_grad, value_grad = attention_back(
        query_heads, key_heads, value_heads, grad_heads, log_totals, allowed
    )
    key_grad_total, value_sum = (
        lax.psum_scatter(from_key_heads(key_grad), "seq", scatter_dimension=1, tiled=True),
        lax.psum_scatter(from_key_heads(value_grad), "seq", scatter_dimension=1, tiled=True),
    )
    grad_query_flat = from_query_heads(query_grad, query_group_width).reshape(
        sequence_count, sequence_rows, QUERY_HEADS, HEAD_SIZE
    )
    grad_qpre = (
        apply_rotary_back(grad_query_flat, cosine_heads, sine_heads)
        .reshape(sequence_count, sequence_rows, QUERY_HEADS * HEAD_SIZE)
        .astype(jnp.bfloat16)
    )
    grad_key_projected = apply_rotary_back(
        key_grad_total.reshape(sequence_count, sequence_rows, KEY_VALUE_HEADS, HEAD_SIZE),
        cosine_heads,
        sine_heads,
    )
    grad_key_projected = grad_key_projected.reshape(
        sequence_count, sequence_rows, KEY_VALUE_HEADS * HEAD_SIZE
    ).astype(jnp.bfloat16)
    grad_vpre = value_sum.astype(jnp.bfloat16)
    grad_nattn = jnp.einsum(
        "btq,dq->btd", grad_qpre, attn_back[1], preferred_element_type=jnp.float32
    )
    grad_nattn = grad_nattn + jnp.einsum(
        "btk,dk->btd", grad_key_projected, attn_back[2], preferred_element_type=jnp.float32
    )
    grad_nattn = grad_nattn + jnp.einsum(
        "btk,dk->btd", grad_vpre, attn_back[3], preferred_element_type=jnp.float32
    )
    unused_attn, norm_back_attn = jax.vjp(rms_norm, inputs_f, attn_back[0].astype(jnp.float32))
    grad_input_norm, attn_gain_term = norm_back_attn(grad_nattn)
    input_grad = (grad_hidden + grad_input_norm).astype(jnp.bfloat16)
    query_term = jnp.einsum(
        "btd,btq->dq", normed_attn, grad_qpre, preferred_element_type=jnp.float32
    )
    key_term = jnp.einsum(
        "btd,btk->dk", normed_attn, grad_key_projected, preferred_element_type=jnp.float32
    )
    value_term = jnp.einsum(
        "btd,btk->dk", normed_attn, grad_vpre, preferred_element_type=jnp.float32
    )
    attn_grads = (
        lax.psum_scatter(attn_gain_term, ("dp", "seq"), scatter_dimension=0, tiled=True),
        lax.psum_scatter(ffn_gain_term, ("dp", "seq"), scatter_dimension=0, tiled=True),
        lax.psum_scatter(query_term, ("dp", "seq"), scatter_dimension=0, tiled=True),
        lax.psum_scatter(key_term, ("dp", "seq"), scatter_dimension=0, tiled=True),
        lax.psum_scatter(value_term, ("dp", "seq"), scatter_dimension=0, tiled=True),
        lax.psum_scatter(output_term, ("dp", "seq"), scatter_dimension=0, tiled=True),
    )
    return (
        output,
        input_grad,
        attn_grads[0],
        attn_grads[2],
        attn_grads[3],
        attn_grads[4],
        attn_grads[5],
        attn_grads[1],
        gate_grad,
        up_grad,
        down_grad,
    )


def solution(mesh):
    placed = (
        P("dp", "seq", None),
        P("dp"),
        P("dp", "seq"),
        P(("dp", "seq")),
        P(("dp", "seq"), None),
        P(("dp", "seq"), None),
        P(("dp", "seq"), None),
        P(("dp", "seq"), None),
        P(("dp", "seq")),
        P(("dp", "seq"), None),
        P(("dp", "seq"), None),
        P(("dp", "seq"), None),
        P("dp", "seq", None),
    )
    return jax.shard_map(
        local,
        mesh=mesh,
        in_specs=placed,
        out_specs=(
            P("dp", "seq", None),
            P("dp", "seq", None),
            P(("dp", "seq")),
            P(("dp", "seq"), None),
            P(("dp", "seq"), None),
            P(("dp", "seq"), None),
            P(("dp", "seq"), None),
            P(("dp", "seq")),
            P(("dp", "seq"), None),
            P(("dp", "seq"), None),
            P(("dp", "seq"), None),
        ),
        check_vma=False,
    )
```

profile of v0, /device:TPU:0, one launch (start us, length us, event | category | flops | bytes accessed | tf_op | source)
XLA Modules:
  0.0 6564.9 jit_solution(4141006341169578825)
XLA Ops:
  11.1 42.1 all-reduce.5
  54.3 15.9 all-gather.14.cloned.1.call-done
  75.8 52.6 all-gather.16.cloned.1.call-done
  128.5 3.0 convolution_convert_fusion.1
  141.2 16.3 all-gather.26.cloned.1.call-done
  160.7 26.2 all-gather.28.cloned.1.call-done
  190.2 76.4 %all-gather.12.cloned.1.call-done = bf16[2048,2048]{1,0:T(8,128)(2,1)} async-done(((bf16[64,2048]{1,0:T(8,128)(2,1)}), bf16[2048,2048]{1,0:T(8,128)(2,1)}) %all-gather.12.cloned.1.call-update) | async-done | bytes 8388624 | tf_op jit(solution)/shard_map/all_gather | solution.py:169
  266.6 7.1 fusion.109
  277.9 4.1 add_convert_fusion.1
  285.4 59.9 while.30
  289.4 3.4 fusion.182
  296.9 3.4 fusion.182
  304.4 3.4 fusion.182
  311.8 3.4 fusion.182
  319.4 3.4 fusion.182
  326.8 3.4 fusion.182
  334.3 3.4 fusion.182
  341.8 3.5 fusion.182
  345.3 3.3 convert_element_type.139
  351.0 6.2 multiply_reduce_fusion.1
  357.5 184.3 %all-gather.22.cloned.1.call-done = bf16[2048,8192]{1,0:T(8,128)(2,1)} async-done(((bf16[64,8192]{1,0:T(8,128)(2,1)}), bf16[2048,8192]{1,0:T(8,128)(2,1)}) %all-gather.22.cloned.1.call-update) | async-done | bytes 33554448 | tf_op jit(solution)/shard_map/all_gather | solution.py:211
  541.8 17.8 fusion.114
  559.6 178.1 %all-gather.20.cloned.1.call-done = bf16[2048,8192]{1,0:T(8,128)(2,1)} async-done(((bf16[64,8192]{1,0:T(8,128)(2,1)}), bf16[2048,8192]{1,0:T(8,128)(2,1)}) %all-gather.20.cloned.1.call-update) | async-done | bytes 33554448 | tf_op jit(solution)/shard_map/all_gather | solution.py:210
  737.7 17.9 fusion.113
  755.6 178.1 %all-gather.24.cloned.1.call-done = bf16[2048,8192]{1,0:T(8,128)(2,1)} async-done(((bf16[64,8192]{1,0:T(8,128)(2,1)}), bf16[2048,8192]{1,0:T(8,128)(2,1)}) %all-gather.24.cloned.1.call-update) | async-done | bytes 33554448 | tf_op jit(solution)/shard_map/all_gather | solution.py:224
  933.6 25.1 multiply_convert_fusion.1
  958.8 16.9 fusion.115
  975.7 16.6 fusion.72
  994.3 5.7 convolution_convert_fusion
  1003.4 96.4 %while.31 = (s32[]{:T(128)}, f32[8,1,1024,64]{2,3,1,0:T(8,128)}, f32[8,1,1024,64]{2,3,1,0:T(8,128)}, f32[8,1,1024,64]{2,3,1,0:T(8,128)}, bf16[8,1,1024,64]{3,2,1...) while((s32[]{:T(128)}, f32[8,1,1024,64]{2,3,1,0:T(8,128)}, ...), condition=%wide.region_9.10_spmd.clone.clone, body=%wide.region_7.9_spmd.clone.sunk.clone | while | flops 682753024 | bytes 34109560 | solution.py:133
  1005.2 3.1 multiply_reduce_fusion.4
  1017.2 3.1 multiply_reduce_fusion.4
  1023.0 2.4 fusion.193
  1029.3 3.1 multiply_reduce_fusion.4
  1035.0 2.4 fusion.193
  1041.3 3.1 multiply_reduce_fusion.4
  1047.1 2.4 fusion.193
  1053.3 3.1 multiply_reduce_fusion.4
  1059.1 2.4 fusion.193
  1065.4 3.1 multiply_reduce_fusion.4
  1071.1 2.4 fusion.193
  1077.4 3.1 multiply_reduce_fusion.4
  1083.1 2.4 fusion.193
  1089.4 3.1 multiply_reduce_fusion.4
  1099.8 25.6 convolution_bitcast_fusion.1
  1125.5 25.5 convolution_bitcast_fusion.2
  1151.0 25.4 convolution_bitcast_fusion
  1176.5 131.2 %pad_maximum_fusion = f32[2048,3,8192]{2,0,1:T(8,128)} fusion(f32[2048,1,8192]{2,0,1:T(8,128)} %convolution_bitcast_fusion, f32[2048,1,8192]{2,0,1:T(8,128)} %convolution_bitcast_fusion.1, f32[2048,1,8192]{2,0,1:T(8,128)} %convolution_bitcast_fusion.2), kind=kLoop, calls=%fused_computation.63 | loop fusion | flops 100663296 | bytes 402653184 | tf_op jit(solution)/shard_map/concatenate | solution.py:260
  1308.9 4.3 fusion.88
  1315.5 2.9 fusion.91
  1319.9 9.4 fusion.79
  1337.0 8.3 fusion.104
  1347.2 7.2 fusion.116
  1354.5 17.0 fusion.62
  1371.5 3.2 convolution_add_fusion.1
  1374.8 2.5 fusion.66
  1377.3 46.7 all-reduce.4
  1425.2 3.2 fusion.69
  1428.3 4098.0 %reduce-scatter.20.cloned.1.call-done = f32[64,3,8192]{2,0,1:T(8,128)} async-done(((f32[2048,3,8192]{2,0,1:T(8,128)}), f32[64,3,8192]{2,0,1:T(8,128)}) %reduce-scatter.20.cloned.1.call-update) | async-done | bytes 6291472 | tf_op jit(solution)/shard_map/reduce_scatter | solution.py:259
  5526.3 5.7 slice_bitcast_fusion
  5532.0 145.9 %reduce-scatter.16.cloned.1.call-done = f32[64,512]{1,0:T(8,128)} async-done(((f32[2048,512]{1,0:T(8,128)}), f32[64,512]{1,0:T(8,128)}) %reduce-scatter.16.cloned.1.call-update) | async-done | bytes 131088 | tf_op jit(solution)/shard_map/reduce_scatter | solution.py:341
  5677.9 149.0 %reduce-scatter.14.cloned.1.call-done = f32[64,512]{1,0:T(8,128)} async-done(((f32[2048,512]{1,0:T(8,128)}), f32[64,512]{1,0:T(8,128)}) %reduce-scatter.14.cloned.1.call-update) | async-done | bytes 131088 | tf_op jit(solution)/shard_map/reduce_scatter | solution.py:340
  5826.9 366.1 %reduce-scatter.18.cloned.1.call-done = f32[64,2048]{1,0:T(8,128)} async-done(((f32[2048,2048]{1,0:T(8,128)}), f32[64,2048]{1,0:T(8,128)}) %reduce-scatter.18.cloned.1.call-update) | async-done | bytes 524304 | tf_op jit(solution)/shard_map/reduce_scatter | solution.py:342
  6193.1 365.0 %reduce-scatter.12.cloned.1.call-done = f32[64,2048]{1,0:T(8,128)} async-done(((f32[2048,2048]{1,0:T(8,128)}), f32[64,2048]{1,0:T(8,128)}) %reduce-scatter.12.cloned.1.call-update) | async-done | bytes 524304 | tf_op jit(solution)/shard_map/reduce_scatter | solution.py:339
  (229 shorter events, 145.9 us)
Async XLA Ops:
  7.2 46.8 copy-start
  7.2 63.0 all-gather.14.cloned.1.call-start
  7.9 120.6 %all-gather.16.cloned.1.call-start = ((), (), s32[]{:S(2)}) async-start(), calls=%async_computation.9 | async-start | bytes 2162688 | tf_op jit(solution)/shard_map/all_gather | solution.py:171
  8.7 148.8 %all-gather.26.cloned.1.call-start = ((), (), s32[]{:S(2)}) async-start(), calls=%async_computation.21 | async-start | bytes 1310720 | tf_op jit(solution)/shard_map/all_gather | solution.py:199
  53.2 213.4 %copy-start.18 = (f32[2048]{0:T(1024)}, f32[2048]{0:T(1024)S(1)}, u32[]{:S(2)}) copy-start(f32[2048]{0:T(1024)S(1)} %convert_element_type.130) | copy-start | bytes 24580
  53.4 82.5 %copy-start.16 = (f32[256,64]{0,1:T(8,128)}, f32[256,64]{0,1:T(8,128)S(1)}, u32[]{:S(2)}) copy-start(f32[256,64]{0,1:T(8,128)S(1)} %get-tuple-element.297) | copy-start | bytes 196612
  53.5 84.5 %copy-start.10 = (f32[256,64]{0,1:T(8,128)}, f32[256,64]{0,1:T(8,128)S(1)}, u32[]{:S(2)}) copy-start(f32[256,64]{0,1:T(8,128)S(1)} %get-tuple-element.296) | copy-start | bytes 196612
  54.3 18.3 copy-start.24
  54.3 212.3 %copy-start.20 = (f32[256]{0:T(256)}, f32[256]{0:T(256)S(1)}, u32[]{:S(2)}) copy-start(f32[256]{0:T(256)S(1)} %fusion.98) | copy-start | bytes 3076
  75.8 111.1 %all-gather.28.cloned.1.call-start = ((), (), s32[]{:S(2)}) async-start(), calls=%async_computation.22 | async-start | bytes 1310720 | tf_op jit(solution)/shard_map/all_gather | solution.py:200
  131.6 135.0 %all-gather.12.cloned.1.call-start = ((), (), s32[]{:S(2)}) async-start(), calls=%async_computation.7 | async-start | bytes 8650752 | tf_op jit(solution)/shard_map/all_gather | solution.py:169
  132.1 218.9 %all-gather.18.cloned.1.call-start = ((), (), s32[]{:S(2)}) async-start(), calls=%async_computation.10 | async-start | bytes 8650752 | tf_op jit(solution)/shard_map/all_gather | solution.py:172
  132.7 409.1 %all-gather.22.cloned.1.call-start = ((), (), s32[]{:S(2)}) async-start(), calls=%async_computation.12 | async-start | bytes 34603008 | tf_op jit(solution)/shard_map/all_gather | solution.py:211
  133.5 604.2 %all-gather.20.cloned.1.call-start = ((), (), s32[]{:S(2)}) async-start(), calls=%async_computation.11 | async-start | bytes 34603008 | tf_op jit(solution)/shard_map/all_gather | solution.py:210
  134.2 799.4 %all-gather.24.cloned.1.call-start = ((), (), s32[]{:S(2)}) async-start(), calls=%async_computation.13 | async-start | bytes 34603008 | tf_op jit(solution)/shard_map/all_gather | solution.py:224
  135.0 1172.9 %reduce-scatter.10.cloned.1.call-start = ((), (), s32[]{:S(2)}) async-start(), calls=%async_computation.15 | async-start | bytes 2621440 | tf_op jit(solution)/shard_map/reduce_scatter | solution.py:296
  140.1 1010.9 %copy-start.22 = (pred[256]{0:T(512)(128)(4,1)}, pred[256]{0:T(512)(128)(4,1)S(1)}, u32[]{:S(2)}) copy-start(pred[256]{0:T(512)(128)(4,1)S(1)} %broadcast_compare_fusion) | copy-start | bytes 772
  345.3 5.8 copy-start.7
  357.2 635.1 %copy-start.5 = (f32[1,256,2048]{2,1,0:T(8,128)}, f32[1,256,2048]{2,1,0:T(8,128)S(1)}, u32[]{:S(2)}) copy-start(f32[1,256,2048]{2,1,0:T(8,128)S(1)} %get-tuple-element.299) | copy-start | bytes 6291460
  975.7 16.7 copy-start.8
  993.0 1.3 copy-start.2
  1099.8 213.6 %reduce-scatter.8.cloned.1.call-start = ((), (), s32[]{:S(2)}) async-start(), calls=%async_computation.14 | async-start | bytes 2621440 | tf_op jit(solution)/shard_map/reduce_scatter | solution.py:295
  1125.5 25.5 copy-start.9
  1176.4 4349.9 %reduce-scatter.20.cloned.1.call-start = ((), (), s32[]{:S(2)}) async-start(), calls=%async_computation.20 | async-start | bytes 207618048 | tf_op jit(solution)/shard_map/reduce_scatter | solution.py:259
  1307.7 1.2 copy-start.1
  1307.7 1.2 copy-start.19
  1307.7 1.2 copy-start.21
  1307.8 4370.1 %reduce-scatter.16.cloned.1.call-start = ((), (), s32[]{:S(2)}) async-start(), calls=%async_computation.18 | async-start | bytes 4325376 | tf_op jit(solution)/shard_map/reduce_scatter | solution.py:341
  1313.3 0.9 copy-start.17
  1313.3 2.0 copy-start.11
  1313.3 4513.6 %reduce-scatter.14.cloned.1.call-start = ((), (), s32[]{:S(2)}) async-start(), calls=%async_computation.17 | async-start | bytes 4325376 | tf_op jit(solution)/shard_map/reduce_scatter | solution.py:340
  1313.4 2.0 copy-start.15
  1318.3 1.6 copy-start.3
  1318.4 4874.7 %reduce-scatter.18.cloned.1.call-start = ((), (), s32[]{:S(2)}) async-start(), calls=%async_computation.19 | async-start | bytes 17301504 | tf_op jit(solution)/shard_map/reduce_scatter | solution.py:342
  1329.3 1.6 copy-start.14
  1329.4 5228.7 %reduce-scatter.12.cloned.1.call-start = ((), (), s32[]{:S(2)}) async-start(), calls=%async_computation.16 | async-start | bytes 17301504 | tf_op jit(solution)/shard_map/reduce_scatter | solution.py:339
  1347.2 7.3 copy-start.6
  1347.2 7.3 copy-start.23
  1371.5 3.2 copy-start.12
  1371.5 3.3 copy-start.13
  1374.7 2.5 copy-start.26
  1374.7 50.4 copy-start.25
  1374.8 50.4 copy-start.4
Sparse Core Ops, SparseCore 0:
  11.0 59.1 all-gather.13
  73.1 55.3 all-gather.15
  130.6 26.7 all-gather.25
  159.4 27.4 all-gather.27
  189.7 76.8 all-gather.11
  269.4 76.0 all-gather.17
  348.4 193.3 all-gather.21
  544.7 192.9 all-gather.19
  740.6 192.9 all-gather.23
  1099.9 42.0 reduce-scatter.9
  1176.5 42.4 reduce-scatter.7
  1307.9 4218.3 reduce-scatter.19
  5529.3 148.5 reduce-scatter.15
  5680.7 146.1 reduce-scatter.13
  5829.8 363.2 reduce-scatter.17
  6195.9 362.1 reduce-scatter.11
where the time goes:
time: 6570 us; the launch traced here: 6560 us
  waiting for transfers between devices  5860 us (89%)
  matrix products  382 us (6%)
  other arithmetic  173 us (3%)
  blocking collectives  88.8 us (1%)
    reduce_scatter x1, waiting for transfers between devices, local(): lax.psum_scatter(jnp.concatenate([both, jnp.einsum('btd,btf->df', grad_ro...  4100 us
    reduce_scatter x1, waiting for transfers between devices, local(): lax.psum_scatter(output_term, ('dp', 'seq'), scatter_dimension=0, tiled=T...  366 us
    reduce_scatter x1, waiting for transfers between devices, local(): lax.psum_scatter(query_term, ('dp', 'seq'), scatter_dimension=0, tiled=True)  365 us
    all_gather x1, waiting for transfers between devices, local(): lax.all_gather(w_up, ('dp', 'seq'), axis=0, tiled=True)  184 us
    all_gather x1, waiting for transfers between devices, local(): lax.all_gather(w_gate, ('dp', 'seq'), axis=0, tiled=True)  178 us
    all_gather x1, waiting for transfers between devices, local(): lax.all_gather(w_down, ('dp', 'seq'), axis=0, tiled=True)  178 us
    reduce_scatter x1, waiting for transfers between devices, local(): lax.psum_scatter(key_term, ('dp', 'seq'), scatter_dimension=0, tiled=True)  149 us
    reduce_scatter x1, waiting for transfers between devices, local(): lax.psum_scatter(value_term, ('dp', 'seq'), scatter_dimension=0, tiled=True)  146 us
  transfers between devices with their start and end apart: 16, of which 13 were waited for; matrix products, arithmetic and copies ran while one was open for 7% of the time, Pallas kernels for 0%

commit v1 on v0

v1 whole, which is shorter than its diff:
```python
import functools
import math

import jax
import jax.numpy as jnp
from jax import lax
from jax.experimental import pallas as pl
from jax.experimental.pallas import tpu as pltpu
from jax.sharding import Mesh
from jax.sharding import PartitionSpec as P

HEADS = 32
GROUPS = 8
SIZE = 64
SHARE = HEADS // GROUPS
EPS = 1e-05
TEAM = ("b", "c", "l")
EVERY = ("a", "b", "c", "h", "l")
BF = jnp.bfloat16
F32 = jnp.float32


def rope_tables(positions):
    index = jnp.arange(SIZE // 2, dtype=F32)
    frequency = 1.0 / 500000.0 ** (2.0 * index / SIZE)
    wavelength = 2.0 * math.pi / frequency
    blending = (8192.0 / wavelength - 1.0) / (4.0 - 1.0)
    middle = (1.0 - blending) * frequency / 32.0 + blending * frequency
    scaled = jnp.where(
        wavelength < 8192.0 / 4.0,
        frequency,
        jnp.where(wavelength > 8192.0, frequency / 32.0, middle),
    )
    angles = positions.astype(F32)[..., None] * scaled
    angles = jnp.concatenate([angles, angles], axis=-1)
    return jnp.cos(angles), jnp.sin(angles)


def rotate(v, cosine, sine):
    first, second = jnp.split(v, 2, axis=-1)
    return v * cosine + jnp.concatenate([-second, first], axis=-1) * sine


def rotate_back(v, cosine, sine):
    turned = v * sine
    first, second = jnp.split(turned, 2, axis=-1)
    return v * cosine + jnp.concatenate([second, -first], axis=-1)


def shift(value, axis, step):
    n = lax.axis_size(axis)
    return lax.ppermute(value, axis, [(i, (i + step) % n) for i in range(n)])


def scatter_step(value, axis, dim):
    n = lax.axis_size(axis)
    me = lax.axis_index(axis)
    kept = lax.dynamic_index_in_dim(value, me, dim, keepdims=False)
    for s in range(1, n):
        sent = lax.dynamic_index_in_dim(value, lax.rem(me + s, n), dim, keepdims=False)
        kept = kept + shift(sent.astype(BF), axis, s).astype(F32)
    return kept


def team_scatter(partial):
    width = partial.shape[-1]
    view = partial.reshape(2, 2, 2, -1, width)
    view = scatter_step(view, "c", 1)
    left = scatter_step(view[..., : width // 2], "l", 1)
    left = scatter_step(left, "b", 0)
    right = scatter_step(view[..., width // 2 :], "b", 0)
    right = scatter_step(right, "l", 0)
    return jnp.concatenate([left, right], axis=-1)


def slices_of(weight, rows):
    return weight.reshape(rows, 8, -1)


def gather_slices(local):
    rows, _, width = local.shape
    n_a, n_h = lax.axis_size("a"), lax.axis_size("h")
    a, h = lax.axis_index("a"), lax.axis_index("h")
    piece = lax.all_to_all(local.transpose(1, 0, 2), TEAM, 0, 0, tiled=True)
    whole = jnp.zeros((n_a, 4, n_h, 2 * rows, width), local.dtype)
    for dh in range(n_h):
        from_h = shift(piece, "h", -dh) if dh else piece
        for da in range(n_a):
            block = shift(from_h, "a", -da) if da else from_h
            whole = lax.dynamic_update_slice(
                whole,
                block.reshape(1, 4, 1, 2 * rows, width),
                (lax.rem(a + da, n_a), 0, lax.rem(h + dh, n_h), 0, 0),
            )
    return whole.reshape(-1, width)


def scatter_slices(partial, rows):
    width = partial.shape[-1]
    view = partial.reshape(lax.axis_size("a"), 4, lax.axis_size("h"), 2 * rows, width)
    view = scatter_step(view, "a", 0)
    view = scatter_step(view, "h", 1)
    owned = lax.all_to_all(view.reshape(8, rows, width).astype(BF), TEAM, 0, 0, tiled=True)
    return owned.transpose(1, 0, 2).astype(F32)


def rows_scatter(partial, rows):
    view = partial.reshape(lax.axis_size("a"), 2, 2, lax.axis_size("h"), 2, rows, -1)
    view = scatter_step(view, "c", 2)
    view = scatter_step(view, "b", 1)
    view = scatter_step(view, "l", 2)
    view = scatter_step(view, "a", 0)
    return scatter_step(view, "h", 0)


def dot(a, b, over):
    return lax.dot_general(a, b, ((over[0], over[1]), ((), ())), preferred_element_type=F32)


NN = ((1,), (0,))
NT = ((1,), (1,))
TN = ((0,), (0,))


def softmax_parts(late, length, q, keys, early_keys):
    rows = q.shape[0]
    slot = late * rows + lax.broadcasted_iota(jnp.int32, (rows, rows), 0)
    key_slot = late * rows + lax.broadcasted_iota(jnp.int32, (rows, rows), 1)
    allowed = (key_slot <= slot) & (key_slot < length)
    own = jnp.where(allowed, dot(q, keys, NT) * SIZE**-0.5, -1e30)
    early_slot = lax.broadcasted_iota(jnp.int32, (rows, rows), 1)
    early = jnp.where(
        (early_slot < late * rows) & (early_slot < length), dot(q, early_keys, NT) * SIZE**-0.5, -1e30
    )
    peak = jnp.maximum(
        jnp.max(own, axis=-1, keepdims=True), jnp.max(early, axis=-1, keepdims=True)
    )
    own, early = jnp.exp(own - peak), jnp.exp(early - peak)
    total = jnp.sum(own, axis=-1, keepdims=True) + jnp.sum(early, axis=-1, keepdims=True)
    part = 1.0 / total
    return own * part, early * part


def forward_kernel(late_ref, length_ref, q_ref, k_ref, v_ref, ek_ref, ev_ref, o_ref):
    late, length = late_ref[0], length_ref[pl.program_id(0)]
    outs = []
    for head in range(SHARE):
        q = q_ref[0, :, head * SIZE : (head + 1) * SIZE]
        own, early = softmax_parts(late, length, q, k_ref[0], ek_ref[0])
        outs.append(dot(own.astype(BF), v_ref[0], NN) + dot(early.astype(BF), ev_ref[0], NN))
    o_ref[0] = jnp.concatenate(outs, axis=-1).astype(BF)


def backward_kernel(
    late_ref, length_ref, q_ref, k_ref, v_ref, ek_ref, ev_ref, g_ref, dq_ref, dk_ref, dv_ref, edk_ref, edv_ref
):
    late, length = late_ref[0], length_ref[pl.program_id(0)]
    scale = SIZE**-0.5
    dqs = []
    dk = dv = edk = edv = 0.0
    for head in range(SHARE):
        q = q_ref[0, :, head * SIZE : (head + 1) * SIZE]
        g = g_ref[0, :, head * SIZE : (head + 1) * SIZE]
        own, early = softmax_parts(late, length, q, k_ref[0], ek_ref[0])
        dp, edp = dot(g, v_ref[0], NT), dot(g, ev_ref[0], NT)
        inner = jnp.sum(own * dp, axis=-1, keepdims=True) + jnp.sum(
            early * edp, axis=-1, keepdims=True
        )
        ds = (own * (dp - inner)).astype(BF)
        eds = (early * (edp - inner)).astype(BF)
        dqs.append((dot(ds, k_ref[0], NN) + dot(eds, ek_ref[0], NN)) * scale)
        dv = dv + dot(own.astype(BF), g, TN)
        edv = edv + dot(early.astype(BF), g, TN)
        dk = dk + dot(ds, q, TN)
        edk = edk + dot(eds, q, TN)
    dq_ref[0] = jnp.concatenate(dqs, axis=-1)
    dk_ref[0], dv_ref[0] = dk * scale, dv
    edk_ref[0], edv_ref[0] = (edk * scale).astype(BF), edv.astype(BF)


def attention_call(kernel, late, lengths, arrays, outs, flops):
    count, rows, _ = arrays[0].shape

    def spec(width):
        return pl.BlockSpec((1, rows, width), lambda s, *_: (s, 0, 0))

    return pl.pallas_call(
        kernel,
        grid_spec=pltpu.PrefetchScalarGridSpec(
            num_scalar_prefetch=2,
            grid=(count,),
            in_specs=[spec(x.shape[-1]) for x in arrays],
            out_specs=[spec(width) for width, _ in outs],
        ),
        out_shape=[jax.ShapeDtypeStruct((count, rows, width), kind) for width, kind in outs],
        compiler_params=pltpu.CompilerParams(vmem_limit_bytes=48 * 2**20),
        cost_estimate=pl.CostEstimate(flops=flops, bytes_accessed=8 * 2**20, transcendentals=2**23),
    )(late, lengths, *arrays)


def norm_parts(value):
    return lax.rsqrt(jnp.mean(value * value, axis=-1, keepdims=True) + EPS)


def norm_back(value, gain, grad):
    r = norm_parts(value)
    hat = value * r
    scaled = grad * gain
    return r * (scaled - hat * jnp.mean(scaled * hat, axis=-1, keepdims=True)), hat


def local(
    inputs,
    lengths,
    positions,
    attn_gain,
    w_query,
    w_key,
    w_value,
    w_output,
    ffn_gain,
    w_gate,
    w_up,
    w_down,
    out_grad,
):
    _, slots, width = inputs.shape
    rows = w_gate.shape[0]
    h, l = lax.axis_index("h"), lax.axis_index("l")
    half = 2 * slots
    own_slot = (h * 2 + l) * slots + jnp.arange(slots, dtype=jnp.int32)
    valid = (own_slot < lengths[0])[:, None]
    own = inputs[0]
    grad_out = jnp.where(valid, out_grad[0], jnp.zeros((), BF))

    gains = lax.all_gather(jnp.stack([attn_gain, ffn_gain]), EVERY, axis=1, tiled=True).astype(F32)
    attn_gain_full, ffn_gain_full = gains[0], gains[1]
    team_inputs = lax.all_gather(own, TEAM, axis=0, tiled=True)
    team_positions = lax.all_gather(positions[0], TEAM, axis=0, tiled=True)
    team_lengths = lax.all_gather(lengths, ("b", "c"), axis=0, tiled=True)
    w_qkv = gather_slices(
        jnp.concatenate([slices_of(w, rows) for w in (w_query, w_key, w_value)], axis=-1)
    )
    cosine, sine = rope_tables(team_positions)

    team_f = team_inputs.astype(F32)
    normed_attn = (team_f * norm_parts(team_f) * attn_gain_full).astype(BF)
    qkv = dot(normed_attn, w_qkv, NN)
    q_width = SHARE * SIZE
    tokens = qkv.shape[0]
    query = rotate(
        qkv[:, :q_width].reshape(tokens, SHARE, SIZE), cosine[:, None], sine[:, None]
    ).astype(BF)
    query = query.reshape(4, half, q_width)
    keys = rotate(qkv[:, q_width : q_width + SIZE], cosine, sine).astype(BF).reshape(4, half, SIZE)
    values = qkv[:, q_width + SIZE :].astype(BF).reshape(4, half, SIZE)
    early = lax.ppermute(jnp.stack([keys, values]), "h", [(0, 1)])
    attention_in = (query, keys, values, early[0], early[1])
    late = h.astype(jnp.int32).reshape(1)
    attended = attention_call(
        forward_kernel, late, team_lengths, attention_in, [(q_width, BF)], 3 * 10**9
    )[0]
    attended = lax.all_to_all(attended.reshape(8, slots, q_width), TEAM, 0, 0, tiled=True)
    attended = attended.transpose(1, 0, 2).reshape(slots, HEADS * SIZE)

    w_out = lax.all_gather(w_output, EVERY, axis=0, tiled=True)
    hidden = own.astype(F32) + dot(attended, w_out, NN)
    normed_ffn = (hidden * norm_parts(hidden) * ffn_gain_full).astype(BF)

    team_grad = lax.all_gather(grad_out, TEAM, axis=0, tiled=True)
    gate_w = gather_slices(slices_of(w_gate, rows))
    up_w = gather_slices(slices_of(w_up, rows))
    down_w = gather_slices(slices_of(w_down, rows))
    team_ffn = lax.all_gather(normed_ffn, TEAM, axis=0, tiled=True)
    gate = dot(team_ffn, gate_w, NN)
    up = dot(team_ffn, up_w, NN)
    sigmoid = jax.nn.sigmoid(gate)
    silu = gate * sigmoid
    activated = (silu * up).astype(BF)
    grad_act = dot(team_grad, down_w, NN)
    grad_gate = (grad_act * up * sigmoid * (1.0 + gate * (1.0 - sigmoid))).astype(BF)
    grad_up = (grad_act * silu).astype(BF)
    grad_nffn = team_scatter(dot(grad_gate, gate_w, NT) + dot(grad_up, up_w, NT))
    down_out = team_scatter(dot(activated, down_w, NT))
    output = jnp.where(valid, hidden + down_out, 0.0).astype(BF)
    gate_grad = scatter_slices(dot(team_ffn, grad_gate, TN), rows).reshape(rows, -1)
    up_grad = scatter_slices(dot(team_ffn, grad_up, TN), rows).reshape(rows, -1)
    down_grad = scatter_slices(dot(team_grad, activated, TN), rows).reshape(rows, -1)

    grad_hidden, hat = norm_back(hidden, ffn_gain_full, grad_nffn)
    grad_hidden = grad_hidden + grad_out.astype(F32)
    ffn_gain_term = jnp.sum(grad_nffn * hat, axis=0)

    grad_branch = grad_hidden.astype(BF)
    output_grad = rows_scatter(dot(attended, grad_branch, TN), rows)
    grad_attended = dot(grad_branch, w_out, NT).astype(BF)
    grad_heads = lax.all_to_all(
        grad_attended.reshape(slots, 8, q_width).transpose(1, 0, 2), TEAM, 0, 0, tiled=True
    ).reshape(4, half, q_width)
    grad_query, grad_keys, grad_values, grad_ek, grad_ev = attention_call(
        backward_kernel,
        late,
        team_lengths,
        attention_in + (grad_heads,),
        [(q_width, F32), (SIZE, F32), (SIZE, F32), (SIZE, BF), (SIZE, BF)],
        8 * 10**9,
    )
    back = lax.ppermute(jnp.stack([grad_ek, grad_ev]), "h", [(1, 0)]).astype(F32)
    grad_q = rotate_back(
        grad_query.reshape(tokens, SHARE, SIZE), cosine[:, None], sine[:, None]
    ).reshape(tokens, q_width)
    grad_k = rotate_back((grad_keys + back[0]).reshape(tokens, SIZE), cosine, sine)
    grad_v = (grad_values + back[1]).reshape(tokens, SIZE)
    grad_qkv = jnp.concatenate([grad_q, grad_k, grad_v], axis=-1).astype(BF)
    partial = dot(grad_qkv, w_qkv, NT)
    qkv_grad = scatter_slices(dot(normed_attn, grad_qkv, TN), rows)
    grad_nattn = team_scatter(partial)
    grad_input, hat = norm_back(own.astype(F32), attn_gain_full, grad_nattn)
    input_grad = (grad_hidden + grad_input).astype(BF)
    attn_gain_term = jnp.sum(grad_nattn * hat, axis=0)
    gain_grads = lax.psum_scatter(
        jnp.stack([attn_gain_term, ffn_gain_term]), EVERY, scatter_dimension=1, tiled=True
    )
    return (
        output[None],
        input_grad[None],
        gain_grads[0],
        qkv_grad[:, :, :q_width].reshape(rows, -1),
        qkv_grad[:, :, q_width : q_width + SIZE].reshape(rows, -1),
        qkv_grad[:, :, q_width + SIZE :].reshape(rows, -1),
        output_grad,
        gain_grads[1],
        gate_grad,
        up_grad,
        down_grad,
    )


def solution(mesh):
    n_dp, n_seq = mesh.shape["dp"], mesh.shape["seq"]
    fine = Mesh(mesh.devices.reshape(n_dp // 4, 2, 2, n_seq // 2, 2), EVERY)
    tokens = P(("a", "b", "c"), ("h", "l"), None)
    matrix = P(EVERY, None)
    vector = P(EVERY)
    placed = (
        tokens,
        P(("a", "b", "c")),
        P(("a", "b", "c"), ("h", "l")),
        vector,
        matrix,
        matrix,
        matrix,
        matrix,
        vector,
        matrix,
        matrix,
        matrix,
        tokens,
    )
    return jax.shard_map(
        local,
        mesh=fine,
        in_specs=placed,
        out_specs=(
            tokens, tokens, vector, matrix, matrix, matrix, matrix, vector, matrix, matrix, matrix
        ),
        check_vma=False,
    )
```

time: 6570 us -> 1270 us (0.19)
  waiting for transfers between devices: 5860 us -> 557 us
  matrix products: 382 us -> 157 us
  local copies, waits for them, and re-layouts: 47.2 us -> 196 us
  starting transfers between devices: 1.02 us -> 88.4 us
    reduce_scatter x7 -> x0, waiting for transfers between devices: 5120 us -> none  [the longest x1 4100 us: local(): lax.psum_scatter(jnp.concatenate([both, jnp.einsum('btd,btf->df', grad_ro...]
    all_gather x9 -> x4, waiting for transfers between devices: 728 us -> 0.04 us  [the longest x1 0.02 us: local(): team_inputs = lax.all_gather(own, TEAM, axis=0, tiled=True)]
    ppermute x0 -> x42, waiting for transfers between devices: none -> 327 us  [the longest x40 322 us: shift(): return lax.ppermute(value, axis, [(i, (i + step) % n) for i in range(n)])]
    dot_general x77 -> x15, matrix products: 382 us -> 157 us  [dot(): lax.dot_general(a, b, ((over[0], over[1]), ((), ())), preferred_element_t...]
    concatenate x4 -> x1, other arithmetic: 132 us -> 3.09 us  [rotate_back(): return v * cosine + jnp.concatenate([second, -first], axis=-1)]
    unnamed x16 -> x6, waiting for transfers between devices: 4.65 us -> 131 us
    all_to_all x0 -> x10, waiting for transfers between devices: none -> 99.5 us  [the longest x4 66.2 us: gather_slices(): piece = lax.all_to_all(local.transpose(1, 0, 2), TEAM, 0, 0, tiled=True)]
    unnamed x2 -> x1, blocking collectives: 88.8 us -> 4.35 us
  transfers between devices with their start and end apart: 16 -> 57, of which waited for: 13 -> 26; matrix products, arithmetic and copies ran while one was open for 7% -> 29% of each run, Pallas kernels for 0% -> 4%
where the time goes in v1:
time: 1270 us
  waiting for transfers between devices  557 us (44%)
  local copies, waits for them, and re-layouts  196 us (15%)
  matrix products  157 us (12%)
  other arithmetic  112 us (9%)
  starting transfers between devices  88.4 us (7%)
  blocking collectives  86.6 us (7%)
  Pallas kernels  52.2 us (4%)
  between operations  16.4 us (1%)
    ppermute x40, waiting for transfers between devices, shift(): return lax.ppermute(value, axis, [(i, (i + step) % n) for i in range(n)])  322 us
    dot_general x15, matrix products, dot(): lax.dot_general(a, b, ((over[0], over[1]), ((), ())), preferred_element_t...  157 us
    unnamed x6, waiting for transfers between devices  131 us
    all_gather x1, blocking collectives, local(): lax.all_gather(jnp.stack([attn_gain, ffn_gain]), EVERY, axis=1, tiled=True)  69.2 us
    all_to_all x4, waiting for transfers between devices, gather_slices(): piece = lax.all_to_all(local.transpose(1, 0, 2), TEAM, 0, 0, tiled=True)  66.2 us
    unnamed x185, local copies, waits for them, and re-layouts  58.3 us
    pallas_call x2, Pallas kernels, attention_call(): pl.pallas_call(kernel, grid_spec=pltpu.PrefetchScalarGridSpec(num_scalar_...  52.2 us
    add x24, other arithmetic, scatter_step(): kept = kept + shift(sent.astype(BF), axis, s).astype(F32)  48.9 us
  transfers between devices with their start and end apart: 57, of which 26 were waited for; matrix products, arithmetic and copies ran while one was open for 29% of the time, Pallas kernels for 4%

profile of v1, /device:TPU:0, one launch (start us, length us, event | category | flops | bytes accessed | tf_op | source)
XLA Modules:
  0.0 1265.4 jit_solution(16807571530390596697)
XLA Ops:
  13.1 5.2 all-to-all-start
  18.4 69.2 %all-gather.2 = bf16[32,64,2]{1,2,0:T(2,128)(2,1)S(1)} all-gather(bf16[1,64,2]{1,2,0:T(2,128)(2,1)S(1)} %maximum_bitcast_fusion.1), channel_id=1, replica_groups=mesh['a'=2,'b'=2,'c'=2,'h'=2,'l'=2] {'a','b','c','h','l'}, dimensions={0}, use_global_device_ids=true | all-gather | bytes 8448 | tf_op jit(solution)/shard_map/all_gather | solution.py:236
  87.7 13.0 %all-gather.1 = s32[1,2048]{1,0:T(1,128)S(1)} all-gather(s32[1,256]{1,0:T(1,128)S(1)} %copy-done.73), channel_id=3, replica_groups=mesh['a'=2,'b'=2,'c'=2,'h'=2,'l'=2] {'b','c','l'}, dimensions={1}, use_global_device_ids=true | all-gather | bytes 9216 | tf_op jit(solution)/shard_map/all_gather | solution.py:239
  103.3 24.1 %collective-permute-done.1 = bf16[8,64,384]{2,1,0:T(8,128)(2,1)S(1)} collective-permute-done((bf16[8,64,384]{2,1,0:T(8,128)(2,1)S(1)}, bf16[8,64,384]{2,1,0:T(8,128)(2,1)S(1)}, u32[]{:S(2)}, u32[]{:S(2)}) %collective-permute-start.1) | collective-permute-done | bytes 393248 | tf_op jit(solution)/shard_map/ppermute | solution.py:52
  128.6 4.4 all-reduce.length_ref
  134.4 13.1 %collective-permute-done.2 = bf16[8,64,384]{2,1,0:T(8,128)(2,1)S(1)} collective-permute-done((bf16[8,64,384]{2,1,0:T(8,128)(2,1)S(1)}, bf16[8,64,384]{2,1,0:T(8,128)(2,1)S(1)}, u32[]{:S(2)}, u32[]{:S(2)}) %collective-permute-start.2) | collective-permute-done | bytes 393248 | tf_op jit(solution)/shard_map/ppermute | solution.py:52
  147.6 5.7 fusion
  192.4 17.1 %shard_map.212 = bf16[4,512,256]{2,1,0:T(8,128)(2,1)S(1)} custom-call(s32[1]{0:T(128)} %bitcast.2.late_ref, s32[4]{0:T(128)S(1)} %all-reduce.length_ref, bf16[4,512,256]{2,1,0:T(8,128)(2,1)S(1)} %add_convert_fusion.1.q_ref, bf16[4,512,64]{2,1,0:T(8,128)(2,1)S(1)} %bitcast.374, bf16[4,512,64]{2,1,0:T(8,128)(2,1)S(1)} %bitcast.376, ...), custom_call_target="tpu_custom_call" | custom-call | flops 3000000000 | bytes 8388608 | tf_op jit(solution)/shard_map/pallas_call | solution.py:187
  214.4 14.8 %all-to-all-done.1 = bf16[8,256,256]{1,2,0:T(8,128)(2,1)S(1)} async-done(((bf16[8,256,256]{1,2,0:T(8,128)(2,1)}), bf16[8,256,256]{1,2,0:T(8,128)(2,1)S(1)}, u32[]{:S(2)}, u32[]{:S(2)}) %all-to-all-start.1) | async-done | bytes 1048608 | tf_op jit(solution)/shard_map/all_to_all | solution.py:263
  229.2 6.2 multiply_reduce_fusion.2
  247.5 15.2 %all-to-all-done.4 = bf16[8,64,1024]{2,1,0:T(8,128)(2,1)S(1)} async-done(((bf16[8,64,1024]{2,1,0:T(8,128)(2,1)}), bf16[8,64,1024]{2,1,0:T(8,128)(2,1)S(1)}, u32[]{:S(2)}, u32[]{:S(2)}) %all-to-all-start.4) | async-done | bytes 1048608 | tf_op jit(solution)/shard_map/all_to_all | solution.py:84
  269.7 17.2 %all-to-all-done.2 = bf16[8,64,1024]{2,1,0:T(8,128)(2,1)S(1)} async-done(((bf16[8,64,1024]{2,1,0:T(8,128)(2,1)}), bf16[8,64,1024]{2,1,0:T(8,128)(2,1)S(1)}, u32[]{:S(2)}, u32[]{:S(2)}) %all-to-all-start.2) | async-done | bytes 1048608 | tf_op jit(solution)/shard_map/all_to_all | solution.py:84
  287.0 4.2 all-to-all-start.3
  292.2 6.2 collective-permute-start.5
  298.5 33.7 %all-to-all-done.3 = bf16[8,64,1024]{2,1,0:T(8,128)(2,1)} async-done(((bf16[8,64,1024]{2,1,0:T(8,128)(2,1)}), bf16[8,64,1024]{2,1,0:T(8,128)(2,1)}, u32[]{:S(2)}, u32[]{:S(2)}) %all-to-all-start.3) | async-done | bytes 1048608 | tf_op jit(solution)/shard_map/all_to_all | solution.py:84
  348.1 64.7 %collective-permute-done.8 = bf16[8,64,1024]{2,1,0:T(8,128)(2,1)} collective-permute-done((bf16[8,64,1024]{2,1,0:T(8,128)(2,1)}, bf16[8,64,1024]{2,1,0:T(8,128)(2,1)}, u32[]{:S(2)}, u32[]{:S(2)}) %collective-permute-start.8) | collective-permute-done | bytes 1048608 | tf_op jit(solution)/shard_map/ppermute | solution.py:52
  415.0 20.2 %collective-permute-done.11 = bf16[8,64,1024]{2,1,0:T(8,128)(2,1)} collective-permute-done((bf16[8,64,1024]{2,1,0:T(8,128)(2,1)S(1)}, bf16[8,64,1024]{2,1,0:T(8,128)(2,1)}, u32[]{:S(2)}, u32[]{:S(2)}) %collective-permute-start.11) | collective-permute-done | bytes 1048608 | tf_op jit(solution)/shard_map/ppermute | solution.py:52
  455.6 5.6 collective-permute-done.12
  462.8 14.4 %fusion.95 = f32[2048,1024]{1,0:T(8,128)} fusion(bf16[2048,2048]{1,0:T(8,128)(2,1)} %all-gather.12.cloned.1.call-done, bf16[2048,1024]{1,0:T(8,128)(2,1)} %bitcast.63), kind=kOutput, calls=%fused_computation.227 | convolution fusion | flops 8589934592 | bytes 20971520 | tf_op jit(solution)/shard_map/dot_general | solution.py:117
  477.2 14.5 %fusion.93 = f32[2048,1024]{1,0:T(8,128)} fusion(bf16[2048,2048]{1,0:T(8,128)(2,1)} %all-gather.10.cloned.1.call-done, bf16[2048,1024]{1,0:T(8,128)(2,1)} %bitcast.52), kind=kOutput, calls=%fused_computation.225 | convolution fusion | flops 8589934592 | bytes 20971520 | tf_op jit(solution)/shard_map/dot_general | solution.py:117
  491.8 21.6 %multiply_convert_fusion.1 = (bf16[2048,1024]{1,0:T(8,128)(2,1)}, bf16[2048,1024]{1,0:T(8,128)(2,1)}, bf16[2048,1024]{1,0:T(8,128)(2,1)S(1)}) fusion(f32[2048,1024]{1,0:T(8,128)} %fusion.95, f32[2048,1024]{1,0:T(8,128)} %fusion.93, bf16[2048,2048]{1,0:T(8,128)(2,1)} %all-gather.10.cloned.1.call-done, bf16[2048,1024]{1,0:T(8,128)(2,1)} %bitcast.42), kind=kOutput, calls=%fused_computation.14 | convolution fusion | flops 8621391872 | bytes 41943040 | tf_op jit(solution)/shard_map/dot_general | solution.py:117
  513.4 13.1 %fusion.99 = f32[2048,1024]{1,0:T(8,128)S(1)} fusion(bf16[2048,2048]{1,0:T(8,128)(2,1)} %all-gather.12.cloned.1.call-done, bf16[2048,1024]{1,0:T(8,128)(2,1)S(1)} %get-tuple-element.27), kind=kOutput, calls=%fused_computation.231 | convolution fusion | flops 8589934592 | bytes 20971520 | tf_op jit(solution)/shard_map/dot_general | solution.py:117
  526.6 4.2 copy-done.44
  533.8 14.7 %fusion.96 = f32[2048,2048]{1,0:T(8,128)} fusion(bf16[2048,1024]{1,0:T(8,128)(2,1)S(1)} %copy-done.79, bf16[2048,1024]{1,0:T(8,128)(2,1)} %bitcast.52), kind=kOutput, calls=%fused_computation.228 | convolution fusion | flops 8589934592 | bytes 25165824 | tf_op jit(solution)/shard_map/dot_general | solution.py:117
  548.5 9.1 fusion.98
  561.5 12.2 fusion.94
  573.7 5.8 copy-done.35
  582.1 17.6 %convolution_add_fusion = f32[2048,2048]{1,0:T(8,128)} fusion(f32[2048,2048]{1,0:T(8,128)} %fusion.96, bf16[2048,1024]{1,0:T(8,128)(2,1)} %get-tuple-element.25, bf16[2048,1024]{1,0:T(8,128)(2,1)} %bitcast.42), kind=kOutput, calls=%fused_computation.18 | convolution fusion | flops 8594128896 | bytes 41943040 | tf_op jit(solution)/shard_map/dot_general | solution.py:117
  599.8 6.2 fusion.5
  606.5 11.7 fusion.97
  628.2 4.6 copy.271
  638.6 4.2 bitcast_add_fusion.5
  644.7 26.5 %collective-permute-done.36 = bf16[4,2,128,1024]{3,2,1,0:T(8,128)(2,1)} collective-permute-done((bf16[4,2,128,1024]{3,2,1,0:T(8,128)(2,1)}, bf16[4,2,128,1024]{3,2,1,0:T(8,128)(2,1)}, u32[]{:S(2)}, u32[]{:S(2)}) %collective-permute-start.36) | collective-permute-done | bytes 2097184 | tf_op jit(solution)/shard_map/ppermute | solution.py:52
  676.2 5.9 bitcast_add_fusion.3
  687.4 5.9 bitcast_add_fusion.2
  693.4 4.3 fusion.85
  700.5 28.1 %collective-permute-done.41 = bf16[4,128,1024]{2,1,0:T(8,128)(2,1)S(1)} collective-permute-done((bf16[4,128,1024]{2,1,0:T(8,128)(2,1)S(1)}, bf16[4,128,1024]{2,1,0:T(8,128)(2,1)S(1)}, u32[]{:S(2)}, u32[]{:S(2)}) %collective-permute-start.41) | collective-permute-done | bytes 1048608 | tf_op jit(solution)/shard_map/ppermute | solution.py:52
  731.7 19.4 %collective-permute-done.39 = bf16[4,128,1024]{2,1,0:T(8,128)(2,1)S(1)} collective-permute-done((bf16[4,128,1024]{2,1,0:T(8,128)(2,1)S(1)}, bf16[4,128,1024]{2,1,0:T(8,128)(2,1)S(1)}, u32[]{:S(2)}, u32[]{:S(2)}) %collective-permute-start.39) | collective-permute-done | bytes 1048608 | tf_op jit(solution)/shard_map/ppermute | solution.py:52
  754.2 25.8 %collective-permute-done.14 = bf16[2,256,1024]{2,1,0:T(8,128)(2,1)} collective-permute-done((bf16[2,256,1024]{2,1,0:T(8,128)(2,1)}, bf16[2,256,1024]{2,1,0:T(8,128)(2,1)}, u32[]{:S(2)}, u32[]{:S(2)}) %collective-permute-start.14) | collective-permute-done | bytes 1048608 | tf_op jit(solution)/shard_map/ppermute | solution.py:52
  782.4 18.1 %collective-permute-done.19 = bf16[2,256,1024]{2,1,0:T(8,128)(2,1)S(1)} collective-permute-done((bf16[2,256,1024]{2,1,0:T(8,128)(2,1)S(1)}, bf16[2,256,1024]{2,1,0:T(8,128)(2,1)S(1)}, u32[]{:S(2)}, u32[]{:S(2)}) %collective-permute-start.19) | collective-permute-done | bytes 1048608 | tf_op jit(solution)/shard_map/ppermute | solution.py:52
  804.1 9.0 collective-permute-done.20
  817.5 7.3 collective-permute-done.17
  830.9 4.2 all-to-all-start.5
  840.8 5.8 copy-done.9
  850.1 4.2 all-to-all-start.9
  856.4 35.1 %shard_map.213 = (f32[4,512,256]{2,1,0:T(8,128)}, f32[4,512,64]{2,1,0:T(8,128)S(1)}, f32[4,512,64]{2,1,0:T(8,128)S(1)}, bf16[4,512,64]{2,1,0:T(8,128)(2,1)S(1)}, bf16[4,512,64]{2,1,0:T(8,128)(2,1)S(1)}) custom-call(s32[1]{0:T(128)} %bitcast.2.late_ref, s32[4]{0:T(128)S(1)} %all-reduce.length_ref, bf16[4,512,256]{2,1,0:T(8,128)(2,1)} %copy-done, ...), custom_call_target="tpu_custom_call" | custom-call | flops 8000000000 | bytes 8388608 | tf_op jit(solution)/shard_map/pallas_call | solution.py:187
  912.4 4.0 concatenate.66
  920.0 4.1 copy.273
  924.1 4.2 add_convert_fusion
  928.4 4.8 collective-permute-done.23
  942.7 8.9 fusion.11
  955.0 4.4 all-to-all-start.8
  959.4 5.5 fusion.59
  964.9 4.6 fusion.32
  969.5 5.8 copy-done.10
  984.1 5.9 bitcast_add_fusion
  997.5 19.9 %collective-permute-done.30 = bf16[4,128,384]{2,1,0:T(8,128)(2,1)S(1)} collective-permute-done((bf16[4,128,384]{2,1,0:T(8,128)(2,1)S(1)}, bf16[4,128,384]{2,1,0:T(8,128)(2,1)S(1)}, u32[]{:S(2)}, u32[]{:S(2)}) %collective-permute-start.30) | collective-permute-done | bytes 393248 | tf_op jit(solution)/shard_map/ppermute | solution.py:52
  1029.5 18.0 %all-to-all-done.6 = bf16[8,64,384]{2,1,0:T(8,128)(2,1)S(1)} async-done(((bf16[8,64,384]{2,1,0:T(8,128)(2,1)}), bf16[8,64,384]{2,1,0:T(8,128)(2,1)S(1)}, u32[]{:S(2)}, u32[]{:S(2)}) %all-to-all-start.6) | async-done | bytes 393248 | tf_op jit(solution)/shard_map/all_to_all | solution.py:103
  1053.9 5.9 bitcast_add_fusion.1
  1073.9 4.4 collective-permute-done.33
  1081.9 17.5 %collective-permute-done.25 = bf16[2,256,1024]{2,1,0:T(8,128)(2,1)} collective-permute-done((bf16[2,256,1024]{2,1,0:T(8,128)(2,1)S(1)}, bf16[2,256,1024]{2,1,0:T(8,128)(2,1)}, u32[]{:S(2)}, u32[]{:S(2)}) %collective-permute-start.25) | collective-permute-done | bytes 1048608 | tf_op jit(solution)/shard_map/ppermute | solution.py:52
  1105.6 8.4 collective-permute-done.26
  1114.1 6.5 collective-permute-done.28
  1127.4 129.1 %reduce-scatter.4.cloned.1.call-done = f32[64,2]{1,0:T(8,128)} async-done(((f32[2048,2]{1,0:T(8,128)}), f32[64,2]{1,0:T(8,128)}) %reduce-scatter.4.cloned.1.call-update) | async-done | bytes 528
  (435 shorter events, 293.4 us)
Async XLA Ops:
  7.2 94.1 %copy-start.77 = (u32[32]{0:T(128)S(1)}, u32[32]{0:T(128)}, u32[]{:S(2)}) copy-start(u32[32]{0:T(128)} %constant.227) | copy-start | bytes 388
  7.2 80.4 %copy-start.73 = (s32[1,256]{1,0:T(1,128)S(1)}, s32[1,256]{1,0:T(1,128)}, u32[]{:S(2)}) copy-start(s32[1,256]{1,0:T(1,128)} %param.15) | copy-start | bytes 3076
  7.3 140.3 %all-gather.14.cloned.1.call-start = ((), (), s32[]{:S(2)}) async-start(), calls=%async_computation.14 | async-start | bytes 9437184 | tf_op jit(solution)/shard_map/all_gather | solution.py:238
  8.0 206.5 %all-gather.8.cloned.1.call-start = ((), (), s32[]{:S(2)}) async-start(), calls=%async_computation.11 | async-start | bytes 8650752 | tf_op jit(solution)/shard_map/all_gather | solution.py:266
  8.7 454.1 %all-gather.12.cloned.1.call-start = ((), (), s32[]{:S(2)}) async-start(), calls=%async_computation.13 | async-start | bytes 9437184 | tf_op jit(solution)/shard_map/all_gather | solution.py:270
  9.5 119.1 %copy-start.69 = (pred[256]{0:T(512)(128)(4,1)}, pred[256]{0:T(512)(128)(4,1)S(1)}, u32[]{:S(2)}) copy-start(pred[256]{0:T(512)(128)(4,1)S(1)} %add_compare_fusion) | copy-start | bytes 772
  13.1 89.6 %all-to-all-start = ((bf16[8,64,384]{2,1,0:T(8,128)(2,1)}), bf16[8,64,384]{2,1,0:T(8,128)(2,1)S(1)}, u32[]{:S(2)}, u32[]{:S(2)}) async-start(bf16[8,64,384]{2,1,0:T(8,128)(2,1)} %copy.238), calls=%async_computation | async-start | bytes 786432 | tf_op jit(solution)/shard_map/all_to_all | solution.py:84
  102.7 50.6 %copy-start.71 = (f32[32]{0:T(128)}, f32[32]{0:T(128)S(1)}, u32[]{:S(2)}) copy-start(f32[32]{0:T(128)S(1)} %compare_select_fusion.1) | copy-start | bytes 388
  102.7 24.7 %collective-permute-start.1 = (bf16[8,64,384]{2,1,0:T(8,128)(2,1)S(1)}, bf16[8,64,384]{2,1,0:T(8,128)(2,1)S(1)}, u32[]{:S(2)}, u32[]{:S(2)}) collective-permute-start(bf16[8,64,384]{2,1,0:T(8,128)(2,1)S(1)} %all-to-all-done), channel_id=1, source_target_pairs={{0,2},{2,0},{1,3},{3,1},{4,6},{6,4},{5,7},{7,5},{8,10},{10,8},{9,1... | collective-permute-start | bytes 1179656 | tf_op jit(solution)/shard_map/ppermute | solution.py:52
  102.9 55.4 %copy-start.50 = (f32[2048,32]{0,1:T(8,128)}, f32[2048,32]{0,1:T(8,128)S(1)}, u32[]{:S(2)}) copy-start(f32[2048,32]{0,1:T(8,128)S(1)} %broadcast_multiply_fusion.2) | copy-start | bytes 786436
  102.9 30.4 %collective-permute-start = (bf16[8,64,384]{2,1,0:T(8,128)(2,1)S(1)}, bf16[8,64,384]{2,1,0:T(8,128)(2,1)}, u32[]{:S(2)}, u32[]{:S(2)}) collective-permute-start(bf16[8,64,384]{2,1,0:T(8,128)(2,1)S(1)} %all-to-all-done), channel_id=1, source_target_pairs={{0,16},{16,0},{1,17},{17,1},{2,18},{18,2},{3,19},{19,3},{4,20},{20... | collective-permute-start | bytes 1179656 | tf_op jit(solution)/shard_map/ppermute | solution.py:52
  127.4 20.1 %collective-permute-start.2 = (bf16[8,64,384]{2,1,0:T(8,128)(2,1)S(1)}, bf16[8,64,384]{2,1,0:T(8,128)(2,1)S(1)}, u32[]{:S(2)}, u32[]{:S(2)}) collective-permute-start(bf16[8,64,384]{2,1,0:T(8,128)(2,1)S(1)} %collective-permute-done.1), channel_id=1, source_target_pairs={{0,16},{16,0},{1,17},{17,1},{2,18},{18,2},{3,19},{19,3},{4,20},{20... | collective-permute-start | bytes 1179656 | tf_op jit(solution)/shard_map/ppermute | solution.py:52
  128.6 106.9 %copy-start.57 = (f32[1,2048]{1,0:T(1,128)}, f32[1,2048]{1,0:T(1,128)S(1)}, u32[]{:S(2)}) copy-start(f32[1,2048]{1,0:T(1,128)S(1)} %get-tuple-element.55) | copy-start | bytes 24580
  164.0 22.8 %collective-permute-start.3 = (bf16[2,4,512,64]{2,3,1,0:T(8,128)(2,1)}, bf16[2,4,512,64]{2,3,1,0:T(8,128)(2,1)}, u32[]{:S(2)}, u32[]{:S(2)}) collective-permute-start(bf16[2,4,512,64]{2,3,1,0:T(8,128)(2,1)} %pad_maximum_fusion.5), channel_id=1, source_target_pairs={{0,2},{1,3},{4,6},{5,7},{8,10},{9,11},{12,14},{13,15},{16,18},{17,... | collective-permute-start | bytes 1572872 | tf_op jit(solution)/shard_map/ppermute | solution.py:257
  210.8 18.4 %all-to-all-start.1 = ((bf16[8,256,256]{1,2,0:T(8,128)(2,1)}), bf16[8,256,256]{1,2,0:T(8,128)(2,1)S(1)}, u32[]{:S(2)}, u32[]{:S(2)}) async-start(bf16[8,256,256]{1,2,0:T(8,128)(2,1)} %copy.252), calls=%async_computation.1 | async-start | bytes 2097152 | tf_op jit(solution)/shard_map/all_to_all | solution.py:263
  214.4 262.9 %all-gather.10.cloned.1.call-start = ((), (), s32[]{:S(2)}) async-start(), calls=%async_computation.12 | async-start | bytes 9437184 | tf_op jit(solution)/shard_map/all_gather | solution.py:274
  240.2 22.6 %all-to-all-start.4 = ((bf16[8,64,1024]{2,1,0:T(8,128)(2,1)}), bf16[8,64,1024]{2,1,0:T(8,128)(2,1)S(1)}, u32[]{:S(2)}, u32[]{:S(2)}) async-start(bf16[8,64,1024]{2,1,0:T(8,128)(2,1)} %copy.263), calls=%async_computation.4 | async-start | bytes 2097152 | tf_op jit(solution)/shard_map/all_to_all | solution.py:84
  262.8 24.2 %all-to-all-start.2 = ((bf16[8,64,1024]{2,1,0:T(8,128)(2,1)}), bf16[8,64,1024]{2,1,0:T(8,128)(2,1)S(1)}, u32[]{:S(2)}, u32[]{:S(2)}) async-start(bf16[8,64,1024]{2,1,0:T(8,128)(2,1)} %copy.253), calls=%async_computation.2 | async-start | bytes 2097152 | tf_op jit(solution)/shard_map/all_to_all | solution.py:84
  287.0 45.2 %all-to-all-start.3 = ((bf16[8,64,1024]{2,1,0:T(8,128)(2,1)}), bf16[8,64,1024]{2,1,0:T(8,128)(2,1)}, u32[]{:S(2)}, u32[]{:S(2)}) async-start(bf16[8,64,1024]{2,1,0:T(8,128)(2,1)} %copy.258), calls=%async_computation.3 | async-start | bytes 2097152 | tf_op jit(solution)/shard_map/all_to_all | solution.py:84
  291.2 46.3 %collective-permute-start.10 = (bf16[8,64,1024]{2,1,0:T(8,128)(2,1)S(1)}, bf16[8,64,1024]{2,1,0:T(8,128)(2,1)}, u32[]{:S(2)}, u32[]{:S(2)}) collective-permute-start(bf16[8,64,1024]{2,1,0:T(8,128)(2,1)S(1)} %all-to-all-done.4), channel_id=1, source_target_pairs={{0,16},{16,0},{1,17},{17,1},{2,18},{18,2},{3,19},{19,3},{4,20},{20... | collective-permute-start | bytes 3145736 | tf_op jit(solution)/shard_map/ppermute | solution.py:52
  292.2 49.0 %collective-permute-start.5 = (bf16[8,64,1024]{2,1,0:T(8,128)(2,1)S(1)}, bf16[8,64,1024]{2,1,0:T(8,128)(2,1)}, u32[]{:S(2)}, u32[]{:S(2)}) collective-permute-start(bf16[8,64,1024]{2,1,0:T(8,128)(2,1)S(1)} %all-to-all-done.2), channel_id=1, source_target_pairs={{0,2},{2,0},{1,3},{3,1},{4,6},{6,4},{5,7},{7,5},{8,10},{10,8},{9,1... | collective-permute-start | bytes 3145736 | tf_op jit(solution)/shard_map/ppermute | solution.py:52
  332.2 80.5 %collective-permute-start.8 = (bf16[8,64,1024]{2,1,0:T(8,128)(2,1)}, bf16[8,64,1024]{2,1,0:T(8,128)(2,1)}, u32[]{:S(2)}, u32[]{:S(2)}) collective-permute-start(bf16[8,64,1024]{2,1,0:T(8,128)(2,1)} %all-to-all-done.3), channel_id=1, source_target_pairs={{0,2},{2,0},{1,3},{3,1},{4,6},{6,4},{5,7},{7,5},{8,10},{10,8},{9,1... | collective-permute-start | bytes 3145736 | tf_op jit(solution)/shard_map/ppermute | solution.py:52
  332.2 103.0 %collective-permute-start.11 = (bf16[8,64,1024]{2,1,0:T(8,128)(2,1)S(1)}, bf16[8,64,1024]{2,1,0:T(8,128)(2,1)}, u32[]{:S(2)}, u32[]{:S(2)}) collective-permute-start(bf16[8,64,1024]{2,1,0:T(8,128)(2,1)S(1)} %all-to-all-done.4), channel_id=1, source_target_pairs={{0,2},{2,0},{1,3},{3,1},{4,6},{6,4},{5,7},{7,5},{8,10},{10,8},{9,1... | collective-permute-start | bytes 3145736 | tf_op jit(solution)/shard_map/ppermute | solution.py:52
  335.2 110.3 %collective-permute-start.7 = (bf16[8,64,1024]{2,1,0:T(8,128)(2,1)}, bf16[8,64,1024]{2,1,0:T(8,128)(2,1)}, u32[]{:S(2)}, u32[]{:S(2)}) collective-permute-start(bf16[8,64,1024]{2,1,0:T(8,128)(2,1)} %all-to-all-done.3), channel_id=1, source_target_pairs={{0,16},{16,0},{1,17},{17,1},{2,18},{18,2},{3,19},{19,3},{4,20},{20... | collective-permute-start | bytes 3145736 | tf_op jit(solution)/shard_map/ppermute | solution.py:52
  337.5 112.5 %collective-permute-start.4 = (bf16[8,64,1024]{2,1,0:T(8,128)(2,1)S(1)}, bf16[8,64,1024]{2,1,0:T(8,128)(2,1)}, u32[]{:S(2)}, u32[]{:S(2)}) collective-permute-start(bf16[8,64,1024]{2,1,0:T(8,128)(2,1)S(1)} %all-to-all-done.2), channel_id=1, source_target_pairs={{0,16},{16,0},{1,17},{17,1},{2,18},{18,2},{3,19},{19,3},{4,20},{20... | collective-permute-start | bytes 3145736 | tf_op jit(solution)/shard_map/ppermute | solution.py:52
  341.2 113.3 %collective-permute-start.6 = (bf16[8,64,1024]{2,1,0:T(8,128)(2,1)}, bf16[8,64,1024]{2,1,0:T(8,128)(2,1)S(1)}, u32[]{:S(2)}, u32[]{:S(2)}) collective-permute-start(bf16[8,64,1024]{2,1,0:T(8,128)(2,1)} %collective-permute-done.5), channel_id=1, source_target_pairs={{0,16},{16,0},{1,17},{17,1},{2,18},{18,2},{3,19},{19,3},{4,20},{20... | collective-permute-start | bytes 3145736 | tf_op jit(solution)/shard_map/ppermute | solution.py:52
  412.7 42.9 %collective-permute-start.9 = (bf16[8,64,1024]{2,1,0:T(8,128)(2,1)}, bf16[8,64,1024]{2,1,0:T(8,128)(2,1)S(1)}, u32[]{:S(2)}, u32[]{:S(2)}) collective-permute-start(bf16[8,64,1024]{2,1,0:T(8,128)(2,1)} %collective-permute-done.8), channel_id=1, source_target_pairs={{0,16},{16,0},{1,17},{17,1},{2,18},{18,2},{3,19},{19,3},{4,20},{20... | collective-permute-start | bytes 3145736 | tf_op jit(solution)/shard_map/ppermute | solution.py:52
  435.2 26.0 %collective-permute-start.12 = (bf16[8,64,1024]{2,1,0:T(8,128)(2,1)}, bf16[8,64,1024]{2,1,0:T(8,128)(2,1)S(1)}, u32[]{:S(2)}, u32[]{:S(2)}) collective-permute-start(bf16[8,64,1024]{2,1,0:T(8,128)(2,1)} %collective-permute-done.11), channel_id=1, source_target_pairs={{0,16},{16,0},{1,17},{17,1},{2,18},{18,2},{3,19},{19,3},{4,20},{20... | collective-permute-start | bytes 3145736 | tf_op jit(solution)/shard_map/ppermute | solution.py:52
  532.4 100.4 %collective-permute-start.40 = (bf16[4,2,128,1024]{3,2,1,0:T(8,128)(2,1)}, bf16[4,2,128,1024]{3,2,1,0:T(8,128)(2,1)}, u32[]{:S(2)}, u32[]{:S(2)}) collective-permute-start(bf16[4,2,128,1024]{3,2,1,0:T(8,128)(2,1)} %fusion.25), channel_id=1, source_target_pairs={{0,16},{16,0},{1,17},{17,1},{2,18},{18,2},{3,19},{19,3},{4,20},{20... | collective-permute-start | bytes 6291464 | tf_op jit(solution)/shard_map/ppermute | solution.py:52
  559.5 79.1 %collective-permute-start.38 = (bf16[4,2,128,1024]{3,2,1,0:T(8,128)(2,1)}, bf16[4,2,128,1024]{3,2,1,0:T(8,128)(2,1)}, u32[]{:S(2)}, u32[]{:S(2)}) collective-permute-start(bf16[4,2,128,1024]{3,2,1,0:T(8,128)(2,1)} %fusion.24), channel_id=1, source_target_pairs={{0,16},{16,0},{1,17},{17,1},{2,18},{18,2},{3,19},{19,3},{4,20},{20... | collective-permute-start | bytes 6291464 | tf_op jit(solution)/shard_map/ppermute | solution.py:52
  582.1 94.1 %collective-permute-start.13 = (bf16[2,2,256,2048]{3,2,1,0:T(8,128)(2,1)}, bf16[2,2,256,2048]{3,2,1,0:T(8,128)(2,1)}, u32[]{:S(2)}, u32[]{:S(2)}) collective-permute-start(bf16[2,2,256,2048]{3,2,1,0:T(8,128)(2,1)} %fusion.7), channel_id=1, source_target_pairs={{0,4},{4,0},{1,5},{5,1},{2,6},{6,2},{3,7},{7,3},{8,12},{12,8},{9,1... | collective-permute-start | bytes 12582920 | tf_op jit(solution)/shard_map/ppermute | solution.py:52
  606.0 81.5 %collective-permute-start.18 = (bf16[2,2,256,2048]{3,2,1,0:T(8,128)(2,1)}, bf16[2,2,256,2048]{3,2,1,0:T(8,128)(2,1)}, u32[]{:S(2)}, u32[]{:S(2)}) collective-permute-start(bf16[2,2,256,2048]{3,2,1,0:T(8,128)(2,1)} %fusion.5), channel_id=1, source_target_pairs={{0,4},{4,0},{1,5},{5,1},{2,6},{6,2},{3,7},{7,3},{8,12},{12,8},{9,1... | collective-permute-start | bytes 12582920 | tf_op jit(solution)/shard_map/ppermute | solution.py:52
  623.4 47.9 %collective-permute-start.36 = (bf16[4,2,128,1024]{3,2,1,0:T(8,128)(2,1)}, bf16[4,2,128,1024]{3,2,1,0:T(8,128)(2,1)}, u32[]{:S(2)}, u32[]{:S(2)}) collective-permute-start(bf16[4,2,128,1024]{3,2,1,0:T(8,128)(2,1)} %fusion.23), channel_id=1, source_target_pairs={{0,16},{16,0},{1,17},{17,1},{2,18},{18,2},{3,19},{19,3},{4,20},{20... | collective-permute-start | bytes 6291464 | tf_op jit(solution)/shard_map/ppermute | solution.py:52
  636.7 91.9 %collective-permute-start.41 = (bf16[4,128,1024]{2,1,0:T(8,128)(2,1)S(1)}, bf16[4,128,1024]{2,1,0:T(8,128)(2,1)S(1)}, u32[]{:S(2)}, u32[]{:S(2)}) collective-permute-start(bf16[4,128,1024]{2,1,0:T(8,128)(2,1)S(1)} %fusion.52), channel_id=1, source_target_pairs={{0,2},{2,0},{1,3},{3,1},{4,6},{6,4},{5,7},{7,5},{8,10},{10,8},{9,1... | collective-permute-start | bytes 3145736 | tf_op jit(solution)/shard_map/ppermute | solution.py:52
  642.9 108.2 %collective-permute-start.39 = (bf16[4,128,1024]{2,1,0:T(8,128)(2,1)S(1)}, bf16[4,128,1024]{2,1,0:T(8,128)(2,1)S(1)}, u32[]{:S(2)}, u32[]{:S(2)}) collective-permute-start(bf16[4,128,1024]{2,1,0:T(8,128)(2,1)S(1)} %fusion.51), channel_id=1, source_target_pairs={{0,2},{2,0},{1,3},{3,1},{4,6},{6,4},{5,7},{7,5},{8,10},{10,8},{9,1... | collective-permute-start | bytes 3145736 | tf_op jit(solution)/shard_map/ppermute | solution.py:52
  675.2 160.0 %collective-permute-start.37 = (bf16[4,128,1024]{2,1,0:T(8,128)(2,1)}, bf16[4,128,1024]{2,1,0:T(8,128)(2,1)}, u32[]{:S(2)}, u32[]{:S(2)}) collective-permute-start(bf16[4,128,1024]{2,1,0:T(8,128)(2,1)} %fusion.50), channel_id=1, source_target_pairs={{0,2},{2,0},{1,3},{3,1},{4,6},{6,4},{5,7},{7,5},{8,10},{10,8},{9,1... | collective-permute-start | bytes 3145736 | tf_op jit(solution)/shard_map/ppermute | solution.py:52
  686.3 93.7 %collective-permute-start.14 = (bf16[2,256,1024]{2,1,0:T(8,128)(2,1)}, bf16[2,256,1024]{2,1,0:T(8,128)(2,1)}, u32[]{:S(2)}, u32[]{:S(2)}) collective-permute-start(bf16[2,256,1024]{2,1,0:T(8,128)(2,1)} %fusion.43), channel_id=1, source_target_pairs={{0,1},{1,0},{2,3},{3,2},{4,5},{5,4},{6,7},{7,6},{8,9},{9,8},{10,11... | collective-permute-start | bytes 3145736 | tf_op jit(solution)/shard_map/ppermute | solution.py:52
  697.7 53.4 %copy-start.22 = (f32[4,2,128,1024]{3,2,1,0:T(8,128)S(1)}, f32[4,2,128,1024]{3,2,1,0:T(8,128)}, u32[]{:S(2)}) copy-start(f32[4,2,128,1024]{3,2,1,0:T(8,128)} %copy-done.21) | copy-start | bytes 12582916
  699.6 101.0 %collective-permute-start.19 = (bf16[2,256,1024]{2,1,0:T(8,128)(2,1)S(1)}, bf16[2,256,1024]{2,1,0:T(8,128)(2,1)S(1)}, u32[]{:S(2)}, u32[]{:S(2)}) collective-permute-start(bf16[2,256,1024]{2,1,0:T(8,128)(2,1)S(1)} %fusion.45), channel_id=1, source_target_pairs={{0,1},{1,0},{2,3},{3,2},{4,5},{5,4},{6,7},{7,6},{8,9},{9,8},{10,11... | collective-permute-start | bytes 3145736 | tf_op jit(solution)/shard_map/ppermute | solution.py:52
  730.1 70.9 %collective-permute-start.21 = (bf16[2,256,1024]{2,1,0:T(8,128)(2,1)S(1)}, bf16[2,256,1024]{2,1,0:T(8,128)(2,1)S(1)}, u32[]{:S(2)}, u32[]{:S(2)}) collective-permute-start(bf16[2,256,1024]{2,1,0:T(8,128)(2,1)S(1)} %fusion.46), channel_id=1, source_target_pairs={{0,8},{8,0},{1,9},{9,1},{2,10},{10,2},{3,11},{11,3},{4,12},{12,4},... | collective-permute-start | bytes 3145736 | tf_op jit(solution)/shard_map/ppermute | solution.py:52
  752.6 48.9 %collective-permute-start.16 = (bf16[2,256,1024]{2,1,0:T(8,128)(2,1)S(1)}, bf16[2,256,1024]{2,1,0:T(8,128)(2,1)S(1)}, u32[]{:S(2)}, u32[]{:S(2)}) collective-permute-start(bf16[2,256,1024]{2,1,0:T(8,128)(2,1)S(1)} %fusion.44), channel_id=1, source_target_pairs={{0,8},{8,0},{1,9},{9,1},{2,10},{10,2},{3,11},{11,3},{4,12},{12,4},... | collective-permute-start | bytes 3145736 | tf_op jit(solution)/shard_map/ppermute | solution.py:52
  782.3 35.0 %collective-permute-start.15 = (bf16[256,1024]{1,0:T(8,128)(2,1)S(1)}, bf16[256,1024]{1,0:T(8,128)(2,1)S(1)}, u32[]{:S(2)}, u32[]{:S(2)}) collective-permute-start(bf16[256,1024]{1,0:T(8,128)(2,1)S(1)} %fusion.65), channel_id=1, source_target_pairs={{0,8},{8,0},{1,9},{9,1},{2,10},{10,2},{3,11},{11,3},{4,12},{12,4},... | collective-permute-start | bytes 1572872 | tf_op jit(solution)/shard_map/ppermute | solution.py:52
  800.9 12.1 collective-permute-start.20
  801.5 14.9 %collective-permute-start.22 = (bf16[256,1024]{1,0:T(8,128)(2,1)S(1)}, bf16[256,1024]{1,0:T(8,128)(2,1)S(1)}, u32[]{:S(2)}, u32[]{:S(2)}) collective-permute-start(bf16[256,1024]{1,0:T(8,128)(2,1)S(1)} %fusion.68), channel_id=1, source_target_pairs={{0,1},{1,0},{2,3},{3,2},{4,5},{5,4},{6,7},{7,6},{8,9},{9,8},{10,11... | collective-permute-start | bytes 1572872 | tf_op jit(solution)/shard_map/ppermute | solution.py:52
  802.0 22.8 %collective-permute-start.17 = (bf16[256,1024]{1,0:T(8,128)(2,1)S(1)}, bf16[256,1024]{1,0:T(8,128)(2,1)S(1)}, u32[]{:S(2)}, u32[]{:S(2)}) collective-permute-start(bf16[256,1024]{1,0:T(8,128)(2,1)S(1)} %fusion.66), channel_id=1, source_target_pairs={{0,1},{1,0},{2,3},{3,2},{4,5},{5,4},{6,7},{7,6},{8,9},{9,8},{10,11... | collective-permute-start | bytes 1572872 | tf_op jit(solution)/shard_map/ppermute | solution.py:52
  830.9 19.2 %all-to-all-start.5 = ((bf16[8,256,256]{2,1,0:T(8,128)(2,1)}), bf16[8,256,256]{2,1,0:T(8,128)(2,1)}, u32[]{:S(2)}, u32[]{:S(2)}) async-start(bf16[8,256,256]{2,1,0:T(8,128)(2,1)} %bitcast.410), calls=%async_computation.5 | async-start | bytes 2097152 | tf_op jit(solution)/shard_map/all_to_all | solution.py:297
  849.2 134.9 %collective-permute-start.31 = (bf16[2,2,2,2,64,2048]{5,4,3,2,1,0:T(8,128)(2,1)}, bf16[2,2,2,2,64,2048]{5,4,3,2,1,0:T(8,128)(2,1)}, u32[]{:S(2)}, u32[]{:S(2)}) collective-permute-start(bf16[2,2,2,2,64,2048]{5,4,3,2,1,0:T(8,128)(2,1)} %fusion.4), channel_id=1, source_target_pairs={{0,4},{4,0},{1,5},{5,1},{2,6},{6,2},{3,7},{7,3},{8,12},{12,8},{9,1... | collective-permute-start | bytes 12582920 | tf_op jit(solution)/shard_map/ppermute | solution.py:52
  850.1 104.9 %all-to-all-start.9 = ((bf16[8,64,1024]{2,1,0:T(8,128)(2,1)}), bf16[8,64,1024]{2,1,0:T(8,128)(2,1)}, u32[]{:S(2)}, u32[]{:S(2)}) async-start(bf16[8,64,1024]{2,1,0:T(8,128)(2,1)} %bitcast.164), calls=%async_computation.9 | async-start | bytes 2097152 | tf_op jit(solution)/shard_map/all_to_all | solution.py:103
  904.7 28.5 %collective-permute-start.23 = (bf16[2,4,512,64]{2,3,1,0:T(8,128)(2,1)}, bf16[2,4,512,64]{2,3,1,0:T(8,128)(2,1)}, u32[]{:S(2)}, u32[]{:S(2)}) collective-permute-start(bf16[2,4,512,64]{2,3,1,0:T(8,128)(2,1)} %copy.274), channel_id=1, source_target_pairs={{2,0},{3,1},{6,4},{7,5},{10,8},{11,9},{14,12},{15,13},{18,16},{19,... | collective-permute-start | bytes 1572872 | tf_op jit(solution)/shard_map/ppermute | solution.py:308
  954.3 28.0 %collective-permute-start.29 = (bf16[4,2,128,384]{3,2,1,0:T(8,128)(2,1)}, bf16[4,2,128,384]{3,2,1,0:T(8,128)(2,1)}, u32[]{:S(2)}, u32[]{:S(2)}) collective-permute-start(bf16[4,2,128,384]{3,2,1,0:T(8,128)(2,1)} %fusion.63), channel_id=1, source_target_pairs={{0,16},{16,0},{1,17},{17,1},{2,18},{18,2},{3,19},{19,3},{4,20},{20... | collective-permute-start | bytes 2359304 | tf_op jit(solution)/shard_map/ppermute | solution.py:52
  955.0 23.4 %all-to-all-start.8 = ((bf16[8,64,1024]{2,1,0:T(8,128)(2,1)}), bf16[8,64,1024]{2,1,0:T(8,128)(2,1)}, u32[]{:S(2)}, u32[]{:S(2)}) async-start(bf16[8,64,1024]{2,1,0:T(8,128)(2,1)} %bitcast.408), calls=%async_computation.8 | async-start | bytes 2097152 | tf_op jit(solution)/shard_map/all_to_all | solution.py:103
  977.9 75.9 %collective-permute-start.24 = (bf16[2,2,256,2048]{3,2,1,0:T(8,128)(2,1)}, bf16[2,2,256,2048]{3,2,1,0:T(8,128)(2,1)}, u32[]{:S(2)}, u32[]{:S(2)}) collective-permute-start(bf16[2,2,256,2048]{3,2,1,0:T(8,128)(2,1)} %fusion.6), channel_id=1, source_target_pairs={{0,4},{4,0},{1,5},{5,1},{2,6},{6,2},{3,7},{7,3},{8,12},{12,8},{9,1... | collective-permute-start | bytes 12582920 | tf_op jit(solution)/shard_map/ppermute | solution.py:52
  978.4 39.8 %all-to-all-start.7 = ((bf16[8,64,1024]{2,1,0:T(8,128)(2,1)}), bf16[8,64,1024]{2,1,0:T(8,128)(2,1)S(1)}, u32[]{:S(2)}, u32[]{:S(2)}) async-start(bf16[8,64,1024]{2,1,0:T(8,128)(2,1)} %bitcast.150), calls=%async_computation.7 | async-start | bytes 2097152 | tf_op jit(solution)/shard_map/all_to_all | solution.py:103
  995.0 53.4 %collective-permute-start.32 = (bf16[2,2,2,64,2048]{4,3,2,1,0:T(8,128)(2,1)}, bf16[2,2,2,64,2048]{4,3,2,1,0:T(8,128)(2,1)}, u32[]{:S(2)}, u32[]{:S(2)}) collective-permute-start(bf16[2,2,2,64,2048]{4,3,2,1,0:T(8,128)(2,1)} %fusion.22), channel_id=1, source_target_pairs={{0,8},{8,0},{1,9},{9,1},{2,10},{10,2},{3,11},{11,3},{4,12},{12,4},... | collective-permute-start | bytes 6291464 | tf_op jit(solution)/shard_map/ppermute | solution.py:52
  997.1 20.3 %collective-permute-start.30 = (bf16[4,128,384]{2,1,0:T(8,128)(2,1)S(1)}, bf16[4,128,384]{2,1,0:T(8,128)(2,1)S(1)}, u32[]{:S(2)}, u32[]{:S(2)}) collective-permute-start(bf16[4,128,384]{2,1,0:T(8,128)(2,1)S(1)} %fusion.79), channel_id=1, source_target_pairs={{0,2},{2,0},{1,3},{3,1},{4,6},{6,4},{5,7},{7,5},{8,10},{10,8},{9,1... | collective-permute-start | bytes 1179656 | tf_op jit(solution)/shard_map/ppermute | solution.py:52
  1018.2 29.3 %all-to-all-start.6 = ((bf16[8,64,384]{2,1,0:T(8,128)(2,1)}), bf16[8,64,384]{2,1,0:T(8,128)(2,1)S(1)}, u32[]{:S(2)}, u32[]{:S(2)}) async-start(bf16[8,64,384]{2,1,0:T(8,128)(2,1)} %bitcast.127), calls=%async_computation.6 | async-start | bytes 786432 | tf_op jit(solution)/shard_map/all_to_all | solution.py:103
  1021.7 234.9 %reduce-scatter.4.cloned.1.call-start = ((), (), s32[]{:S(2)}) async-start(), calls=%async_computation.15 | async-start | bytes 1081344
  1052.0 26.2 %collective-permute-start.33 = (bf16[2,2,64,2048]{3,2,1,0:T(8,128)(2,1)S(1)}, bf16[2,2,64,2048]{3,2,1,0:T(8,128)(2,1)}, u32[]{:S(2)}, u32[]{:S(2)}) collective-permute-start(bf16[2,2,64,2048]{3,2,1,0:T(8,128)(2,1)S(1)} %fusion.49), channel_id=1, source_target_pairs={{0,1},{1,0},{2,3},{3,2},{4,5},{5,4},{6,7},{7,6},{8,9},{9,8},{10,11... | collective-permute-start | bytes 3145736 | tf_op jit(solution)/shard_map/ppermute | solution.py:52
  1065.1 34.4 %collective-permute-start.25 = (bf16[2,256,1024]{2,1,0:T(8,128)(2,1)S(1)}, bf16[2,256,1024]{2,1,0:T(8,128)(2,1)}, u32[]{:S(2)}, u32[]{:S(2)}) collective-permute-start(bf16[2,256,1024]{2,1,0:T(8,128)(2,1)S(1)} %fusion.47), channel_id=1, source_target_pairs={{0,1},{1,0},{2,3},{3,2},{4,5},{5,4},{6,7},{7,6},{8,9},{9,8},{10,11... | collective-permute-start | bytes 3145736 | tf_op jit(solution)/shard_map/ppermute | solution.py:52
  1072.3 30.2 %collective-permute-start.27 = (bf16[2,256,1024]{2,1,0:T(8,128)(2,1)S(1)}, bf16[2,256,1024]{2,1,0:T(8,128)(2,1)S(1)}, u32[]{:S(2)}, u32[]{:S(2)}) collective-permute-start(bf16[2,256,1024]{2,1,0:T(8,128)(2,1)S(1)} %fusion.48), channel_id=1, source_target_pairs={{0,8},{8,0},{1,9},{9,1},{2,10},{10,2},{3,11},{11,3},{4,12},{12,4},... | collective-permute-start | bytes 3145736 | tf_op jit(solution)/shard_map/ppermute | solution.py:52
  1080.5 24.1 %collective-permute-start.34 = (bf16[2,64,2048]{2,1,0:T(8,128)(2,1)S(1)}, bf16[2,64,2048]{2,1,0:T(8,128)(2,1)S(1)}, u32[]{:S(2)}, u32[]{:S(2)}) collective-permute-start(bf16[2,64,2048]{2,1,0:T(8,128)(2,1)S(1)} %fusion.71), channel_id=1, source_target_pairs={{0,16},{16,0},{1,17},{17,1},{2,18},{18,2},{3,19},{19,3},{4,20},{20... | collective-permute-start | bytes 1572872 | tf_op jit(solution)/shard_map/ppermute | solution.py:52
  1101.2 12.7 %collective-permute-start.26 = (bf16[256,1024]{1,0:T(8,128)(2,1)S(1)}, bf16[256,1024]{1,0:T(8,128)(2,1)S(1)}, u32[]{:S(2)}, u32[]{:S(2)}) collective-permute-start(bf16[256,1024]{1,0:T(8,128)(2,1)S(1)} %fusion.69), channel_id=1, source_target_pairs={{0,8},{8,0},{1,9},{9,1},{2,10},{10,2},{3,11},{11,3},{4,12},{12,4},... | collective-permute-start | bytes 1572872 | tf_op jit(solution)/shard_map/ppermute | solution.py:52
  1103.1 17.6 %collective-permute-start.28 = (bf16[256,1024]{1,0:T(8,128)(2,1)S(1)}, bf16[256,1024]{1,0:T(8,128)(2,1)S(1)}, u32[]{:S(2)}, u32[]{:S(2)}) collective-permute-start(bf16[256,1024]{1,0:T(8,128)(2,1)S(1)} %fusion.70), channel_id=1, source_target_pairs={{0,1},{1,0},{2,3},{3,2},{4,5},{5,4},{6,7},{7,6},{8,9},{9,8},{10,11... | collective-permute-start | bytes 1572872 | tf_op jit(solution)/shard_map/ppermute | solution.py:52
  1105.5 21.0 %collective-permute-start.35 = (bf16[64,2048]{1,0:T(8,128)(2,1)}, bf16[64,2048]{1,0:T(8,128)(2,1)S(1)}, u32[]{:S(2)}, u32[]{:S(2)}) collective-permute-start(bf16[64,2048]{1,0:T(8,128)(2,1)} %fusion.80), channel_id=1, source_target_pairs={{0,2},{2,0},{1,3},{3,1},{4,6},{6,4},{5,7},{7,5},{8,10},{10,8},{9,1... | collective-permute-start | bytes 786440 | tf_op jit(solution)/shard_map/ppermute | solution.py:52
  (79 other events, 726.4 us)
Sparse Core Ops, SparseCore 0:
  9.6 55.5 all-gather.13
  68.1 95.8 all-gather.7
  166.2 50.6 all-gather.11
  238.1 110.6 all-gather.9
  1123.4 133.0 reduce-scatter.3

commit v2 on v1

--- a/solution.py
+++ b/solution.py
@@ -55,7 +55,7 @@
 def scatter_step(value, axis, dim):
     n = lax.axis_size(axis)
     me = lax.axis_index(axis)
-    kept = lax.dynamic_index_in_dim(value, me, dim, keepdims=False)
+    kept = lax.dynamic_index_in_dim(value, me, dim, keepdims=False).astype(F32)
     for s in range(1, n):
         sent = lax.dynamic_index_in_dim(value, lax.rem(me + s, n), dim, keepdims=False)
         kept = kept + shift(sent.astype(BF), axis, s).astype(F32)
@@ -102,6 +102,20 @@
     view = scatter_step(view, "h", 1)
     owned = lax.all_to_all(view.reshape(8, rows, width).astype(BF), TEAM, 0, 0, tiled=True)
     return owned.transpose(1, 0, 2).astype(F32)
+
+
+def relative_scatter(partial):
+    half = partial.shape[-1] // 2
+
+    def fold(value, axis, dim):
+        kept = lax.index_in_dim(value, 0, dim, keepdims=False).astype(F32)
+        sent = lax.index_in_dim(value, 1, dim, keepdims=False).astype(BF)
+        return kept + shift(sent, axis, 1).astype(F32)
+
+    view = fold(partial, "c", 2)
+    left = fold(fold(view[..., :half], "l", 0), "b", 0)
+    right = fold(fold(view[..., half:], "b", 1), "l", 0)
+    return jnp.concatenate([left, right], axis=-1)
 
 
 def rows_scatter(partial, rows):
@@ -198,6 +212,275 @@
     )(late, lengths, *arrays)
 
 
+MESH = pl.DeviceIdType.MESH
+
+
+def ffn_kernel(
+    own_ref,
+    grad_ref,
+    wg_ref,
+    wu_ref,
+    wd_ref,
+    gn_ref,
+    dn_ref,
+    dwg_ref,
+    dwu_ref,
+    dwd_ref,
+    wg,
+    wu,
+    wd,
+    xs,
+    gs,
+    act,
+    gg,
+    gu,
+    send_sib,
+    recv_sib,
+    send_own,
+    recv_own,
+    stage,
+    local_sem,
+    grad_sem,
+    ag_send,
+    ag_recv,
+    sib_send,
+    sib_recv,
+    own_send,
+    own_recv,
+    stage_sem,
+    credit,
+):
+    b, c, l = lax.axis_index("b"), lax.axis_index("c"), lax.axis_index("l")
+    rows, width = own_ref.shape
+    tile = wg.shape[1]
+    sibling = {"c": 1 - c}
+
+    def chip(k):
+        return {"b": lax.rem(b + lax.rem(k, 2), 2), "l": lax.rem(l + k // 2, 2)}
+
+    barrier = pltpu.get_barrier_semaphore()
+    for peer in (sibling, chip(1), chip(2), chip(3)):
+        pl.semaphore_signal(barrier, inc=1, device_id=peer, device_id_type=MESH)
+    pl.semaphore_wait(barrier, 4)
+
+    def part(slot):
+        return pl.ds(pl.multiple_of(slot * rows, rows), rows)
+
+    def gather_copy(source, slot, peer):
+        return pltpu.make_async_remote_copy(
+            src_ref=source,
+            dst_ref=xs.at[part(slot)],
+            send_sem=ag_send.at[slot],
+            recv_sem=ag_recv.at[slot],
+            device_id=peer,
+            device_id_type=MESH,
+        )
+
+    def forward_copy(k):
+        return gather_copy(xs.at[part(2 * k)], 2 * k + 1, sibling)
+
+    def sibling_copy(k):
+        spot = lax.rem(k, 2)
+        return pltpu.make_async_remote_copy(
+            src_ref=send_sib.at[spot],
+            dst_ref=recv_sib.at[spot],
+            send_sem=sib_send.at[spot],
+            recv_sem=sib_recv.at[spot],
+            device_id=sibling,
+            device_id_type=MESH,
+        )
+
+    def owner_copy(k):
+        return pltpu.make_async_remote_copy(
+            src_ref=send_own.at[k - 1],
+            dst_ref=recv_own.at[k - 1],
+            send_sem=own_send.at[k - 1],
+            recv_sem=own_recv.at[k - 1],
+            device_id=chip(k),
+            device_id_type=MESH,
+        )
+
+    def grad_copy(slot):
+        k, dc = slot // 2, lax.rem(slot, 2)
+        db, dl = lax.rem(k, 2), k // 2
+        source = (lax.rem(b + db, 2) * 2 + lax.rem(c + dc, 2)) * 2 + lax.rem(l + dl, 2)
+        return pltpu.make_async_copy(grad_ref.at[source], gs.at[part(slot)], grad_sem.at[slot])
+
+    def down_copy(spot, slot):
+        cols = pl.ds(spot * tile, tile)
+        return pltpu.make_async_copy(stage.at[spot], dn_ref.at[slot, :, cols], stage_sem.at[spot])
+
+    gather_copy(own_ref, 1, sibling).start()
+    for k in (1, 2, 3):
+        gather_copy(own_ref, 2 * k, chip(k)).start()
+    own_copy = pltpu.make_async_copy(own_ref, xs.at[part(0)], local_sem.at[0])
+    own_copy.start()
+    loads = [
+        pltpu.make_async_copy(source, target, local_sem.at[1 + j])
+        for j, (source, target) in enumerate(((wg_ref, wg), (wu_ref, wu), (wd_ref, wd)))
+    ]
+    for load in loads:
+        load.start()
+    for slot in range(8):
+        grad_copy(slot).start()
+    for load in loads:
+        load.wait()
+    own_copy.wait()
+
+    def block(i, carry):
+        k, second = i // 2, lax.rem(i, 2)
+        slot = 2 * k + 1 - second
+        spot = lax.rem(k, 2)
+        for at, ready in ((2, 1), (3, 2), (5, 3)):
+
+            @pl.when(i == at)
+            def _():
+                gather_copy(own_ref, 2 * ready, chip(ready)).wait_recv()
+                forward_copy(ready).start()
+
+        @pl.when(second == 0)
+        def _():
+            gather_copy(own_ref, slot, sibling).wait_recv()
+
+        grad_copy(slot).wait()
+        for piece in (slice(0, tile // 2), slice(tile // 2, tile)):
+            gate = dot(xs[part(slot), :], wg[:, piece], NN)
+            up = dot(xs[part(slot), :], wu[:, piece], NN)
+            grad_act = dot(gs[part(slot), :], wd[:, piece], NN)
+            sigmoid = jax.nn.sigmoid(gate)
+            silu = gate * sigmoid
+            act[part(slot), piece] = (silu * up).astype(BF)
+            gu[part(slot), piece] = (grad_act * silu).astype(BF)
+            slope = sigmoid * (1.0 + gate * (1.0 - sigmoid))
+            gg[part(slot), piece] = (grad_act * up * slope).astype(BF)
+
+        @pl.when((second == 0) & (k >= 2))
+        def _():
+            sibling_copy(k).wait_send()
+
+        @pl.when(second == 1)
+        def _():
+            sibling_copy(k).wait_recv()
+
+        for start in range(0, width, tile):
+            cols = slice(start, start + tile)
+            part_gn = dot(gg[part(slot), :], wg[cols, :], NT)
+            part_gn += dot(gu[part(slot), :], wu[cols, :], NT)
+
+            @pl.when(second == 0)
+            def _():
+                send_sib[spot, :, cols] = part_gn.astype(BF)
+
+            @pl.when(i == 1)
+            def _():
+                gn_ref[:, cols] = part_gn + recv_sib[spot, :, cols].astype(F32)
+
+            @pl.when((second == 1) & (k > 0))
+            def _():
+                send_own[k - 1, :, cols] = (part_gn + recv_sib[spot, :, cols].astype(F32)).astype(BF)
+
+        @pl.when((second == 0) & (k >= 2))
+        def _():
+            pl.semaphore_wait(credit, 1)
+
+        @pl.when(second == 0)
+        def _():
+            sibling_copy(k).start()
+
+        @pl.when((second == 1) & (k < 2))
+        def _():
+            pl.semaphore_signal(credit, inc=1, device_id=sibling, device_id_type=MESH)
+
+        @pl.when((second == 1) & (k > 0))
+        def _():
+            owner_copy(k).start()
+
+        for at in range(width // tile):
+            part_dn = dot(act[part(slot), :], wd[at * tile : (at + 1) * tile, :], NT)
+
+            @pl.when(i >= 1)
+            def _():
+                down_copy(at, slot).wait()
+
+            stage[at] = part_dn.astype(BF)
+            down_copy(at, slot).start()
+        return carry
+
+    lax.fori_loop(0, 8, block, 0)
+    for at in range(width // tile):
+        down_copy(at, 0).wait()
+
+    step = rows
+
+    def weight_copy(j, which, target):
+        return pltpu.make_async_copy(
+            stage.at[which],
+            target.at[pl.ds(pl.multiple_of(j * step, step), step)],
+            stage_sem.at[which],
+        )
+
+    def weights(j, carry):
+        cols = pl.ds(pl.multiple_of(j * step, step), step)
+        for which, (left, right, target) in enumerate(
+            ((xs, gg, dwg_ref), (xs, gu, dwu_ref), (gs, act, dwd_ref))
+        ):
+
+            @pl.when(j > 0)
+            def _():
+                weight_copy(j, which, target).wait()
+
+            stage[which] = dot(left[:, cols], right[...], TN).astype(BF)
+            weight_copy(j, which, target).start()
+        return carry
+
+    lax.fori_loop(0, width // step, weights, 0)
+
+    for k in (1, 2, 3):
+        owner_copy(k).wait_recv()
+        gn_ref[...] += recv_own[k - 1].astype(F32)
+    for which, target in enumerate((dwg_ref, dwu_ref, dwd_ref)):
+        weight_copy(0, which, target).wait()
+    for k in (0, 1):
+        sibling_copy(k).wait_send()
+    gather_copy(own_ref, 1, sibling).wait_send()
+    for k in (1, 2, 3):
+        gather_copy(own_ref, 2 * k, chip(k)).wait_send()
+        forward_copy(k).wait_send()
+        owner_copy(k).wait_send()
+
+
+def ffn_call(own, team_grad, gate_w, up_w, down_w):
+    rows, width = own.shape
+    hidden = gate_w.shape[1]
+    team = 8 * rows
+    anywhere = pl.BlockSpec(memory_space=pl.ANY)
+    stages = max(3, width // hidden)
+    return pl.pallas_call(
+        ffn_kernel,
+        in_specs=[anywhere] * 5,
+        out_specs=[pl.BlockSpec(memory_space=pltpu.VMEM)] + [anywhere] * 4,
+        out_shape=[
+            jax.ShapeDtypeStruct((rows, width), F32),
+            jax.ShapeDtypeStruct((8, rows, width), BF),
+        ]
+        + [jax.ShapeDtypeStruct((width, hidden), BF)] * 3,
+        scratch_shapes=[pltpu.VMEM((width, hidden), BF)] * 3
+        + [pltpu.VMEM((team, width), BF)] * 2
+        + [pltpu.VMEM((team, hidden), BF)] * 3
+        + [pltpu.VMEM((2, rows, width), BF)] * 2
+        + [pltpu.VMEM((3, rows, width), BF)] * 2
+        + [pltpu.VMEM((stages, rows, hidden), BF)]
+        + [pltpu.SemaphoreType.DMA((n,)) for n in (4, 8, 8, 8, 2, 2, 3, 3, stages)]
+        + [pltpu.SemaphoreType.REGULAR],
+        compiler_params=pltpu.CompilerParams(
+            collective_id=0, has_side_effects=True, vmem_limit_bytes=60 * 2**20
+        ),
+        cost_estimate=pl.CostEstimate(
+            flops=18 * team * width * hidden, bytes_accessed=60 * 2**20, transcendentals=team * hidden
+        ),
+    )(own, team_grad, gate_w, up_w, down_w)
+
+
 def norm_parts(value):
     return lax.rsqrt(jnp.mean(value * value, axis=-1, keepdims=True) + EPS)
 
@@ -271,21 +554,14 @@
     gate_w = gather_slices(slices_of(w_gate, rows))
     up_w = gather_slices(slices_of(w_up, rows))
     down_w = gather_slices(slices_of(w_down, rows))
-    team_ffn = lax.all_gather(normed_ffn, TEAM, axis=0, tiled=True)
-    gate = dot(team_ffn, gate_w, NN)
-    up = dot(team_ffn, up_w, NN)
-    sigmoid = jax.nn.sigmoid(gate)
-    silu = gate * sigmoid
-    activated = (silu * up).astype(BF)
-    grad_act = dot(team_grad, down_w, NN)
-    grad_gate = (grad_act * up * sigmoid * (1.0 + gate * (1.0 - sigmoid))).astype(BF)
-    grad_up = (grad_act * silu).astype(BF)
-    grad_nffn = team_scatter(dot(grad_gate, gate_w, NT) + dot(grad_up, up_w, NT))
-    down_out = team_scatter(dot(activated, down_w, NT))
+    grad_nffn, down_part, gate_dw, up_dw, down_dw = ffn_call(
+        normed_ffn, team_grad.reshape(8, slots, width), gate_w, up_w, down_w
+    )
+    down_out = relative_scatter(down_part.reshape(2, 2, 2, slots, width))
     output = jnp.where(valid, hidden + down_out, 0.0).astype(BF)
-    gate_grad = scatter_slices(dot(team_ffn, grad_gate, TN), rows).reshape(rows, -1)
-    up_grad = scatter_slices(dot(team_ffn, grad_up, TN), rows).reshape(rows, -1)
-    down_grad = scatter_slices(dot(team_grad, activated, TN), rows).reshape(rows, -1)
+    gate_grad = scatter_slices(gate_dw, rows).reshape(rows, -1)
+    up_grad = scatter_slices(up_dw, rows).reshape(rows, -1)
+    down_grad = scatter_slices(down_dw, rows).reshape(rows, -1)
 
     grad_hidden, hat = norm_back(hidden, ffn_gain_full, grad_nffn)
     grad_hidden = grad_hidden + grad_out.astype(F32)
@@ -313,23 +589,25 @@
     grad_v = (grad_values + back[1]).reshape(tokens, SIZE)
     grad_qkv = jnp.concatenate([grad_q, grad_k, grad_v], axis=-1).astype(BF)
     partial = dot(grad_qkv, w_qkv, NT)
-    qkv_grad = scatter_slices(dot(normed_attn, grad_qkv, TN), rows)
+    attn_gain_term = jnp.sum(partial * (team_f * norm_parts(team_f)), axis=0)
+    extra = jnp.stack([attn_gain_term, ffn_gain_term], axis=-1)
+    extra = jnp.pad(extra, ((0, 0), (0, 126)))
+    slab = jnp.concatenate([dot(normed_attn, grad_qkv, TN), extra], axis=-1)
+    qkv_grad = scatter_slices(slab, rows)
     grad_nattn = team_scatter(partial)
-    grad_input, hat = norm_back(own.astype(F32), attn_gain_full, grad_nattn)
+    grad_input, _ = norm_back(own.astype(F32), attn_gain_full, grad_nattn)
     input_grad = (grad_hidden + grad_input).astype(BF)
-    attn_gain_term = jnp.sum(grad_nattn * hat, axis=0)
-    gain_grads = lax.psum_scatter(
-        jnp.stack([attn_gain_term, ffn_gain_term]), EVERY, scatter_dimension=1, tiled=True
-    )
+    q_end, k_end, v_end = q_width, q_width + SIZE, q_width + 2 * SIZE
+    gain_grads = jnp.sum(qkv_grad[:, :, v_end : v_end + 2], axis=1)
     return (
         output[None],
         input_grad[None],
-        gain_grads[0],
-        qkv_grad[:, :, :q_width].reshape(rows, -1),
-        qkv_grad[:, :, q_width : q_width + SIZE].reshape(rows, -1),
-        qkv_grad[:, :, q_width + SIZE :].reshape(rows, -1),
+        gain_grads[:, 0],
+        qkv_grad[:, :, :q_end].reshape(rows, -1),
+        qkv_grad[:, :, q_end:k_end].reshape(rows, -1),
+        qkv_grad[:, :, k_end:v_end].reshape(rows, -1),
         output_grad,
-        gain_grads[1],
+        gain_grads[:, 1],
         gate_grad,
         up_grad,
         down_grad,

time: 1270 us -> 1100 us (0.87)
  waiting for transfers between devices: 557 us -> 410 us
  matrix products: 157 us -> 33.8 us
  Pallas kernels: 52.2 us -> 160 us
  starting transfers between devices: 88.4 us -> 126 us
  local copies, waits for them, and re-layouts: 196 us -> 161 us
  other arithmetic: 112 us -> 88.9 us
    unnamed x6 -> x3, waiting for transfers between devices: 131 us -> 1.39 us
    dot_general x15 -> x6, matrix products: 157 us -> 33.8 us  [dot(): lax.dot_general(a, b, ((over[0], over[1]), ((), ())), preferred_element_t...]
    pallas_call x0 -> x1, Pallas kernels: none -> 108 us  [ffn_call(): pl.pallas_call(ffn_kernel, in_specs=[anywhere] * 5, out_specs=[pl.BlockSp...]
    ppermute x1, waiting for transfers between devices: 0.01 us -> 46.8 us  [local(): early = lax.ppermute(jnp.stack([keys, values]), 'h', [(0, 1)])]
    ppermute x40 -> x35, waiting for transfers between devices: 322 us -> 283 us  [shift(): return lax.ppermute(value, axis, [(i, (i + step) % n) for i in range(n)])]
    all_to_all x4, waiting for transfers between devices: 66.2 us -> 28.4 us  [gather_slices(): piece = lax.all_to_all(local.transpose(1, 0, 2), TEAM, 0, 0, tiled=True)]
    all_to_all x1, starting transfers between devices: 3.56 us -> 39.9 us  [local(): lax.all_to_all(attended.reshape(8, slots, q_width), TEAM, 0, 0, tiled=True)]
    unnamed x185 -> x153, local copies, waits for them, and re-layouts: 58.3 us -> 31.9 us
  transfers between devices with their start and end apart: 57 -> 50, of which waited for: 26 -> 23; matrix products, arithmetic and copies ran while one was open for 29% -> 23% of each run, Pallas kernels for 4% -> 5%
where the time goes in v2:
time: 1100 us; the launch traced here: 1090 us
  waiting for transfers between devices  410 us (37%)
  local copies, waits for them, and re-layouts  161 us (15%)
  Pallas kernels  160 us (15%)
  starting transfers between devices  126 us (11%)
  blocking collectives  97.5 us (9%)
  other arithmetic  88.9 us (8%)
  matrix products  33.8 us (3%)
  between operations  15.9 us (1%)
    ppermute x35, waiting for transfers between devices, shift(): return lax.ppermute(value, axis, [(i, (i + step) % n) for i in range(n)])  283 us
    pallas_call x1, Pallas kernels, ffn_call(): pl.pallas_call(ffn_kernel, in_specs=[anywhere] * 5, out_specs=[pl.BlockSp...  108 us
    all_gather x1, blocking collectives, local(): lax.all_gather(jnp.stack([attn_gain, ffn_gain]), EVERY, axis=1, tiled=True)  79.8 us
    pallas_call x2, Pallas kernels, attention_call(): pl.pallas_call(kernel, grid_spec=pltpu.PrefetchScalarGridSpec(num_scalar_...  52 us
    ppermute x1, waiting for transfers between devices, local(): early = lax.ppermute(jnp.stack([keys, values]), 'h', [(0, 1)])  46.8 us
    ppermute x35, starting transfers between devices, shift(): return lax.ppermute(value, axis, [(i, (i + step) % n) for i in range(n)])  40.3 us
    all_to_all x1, starting transfers between devices, local(): lax.all_to_all(attended.reshape(8, slots, q_width), TEAM, 0, 0, tiled=True)  39.9 us
    dot_general x6, matrix products, dot(): lax.dot_general(a, b, ((over[0], over[1]), ((), ())), preferred_element_t...  33.8 us
  transfers between devices with their start and end apart: 50, of which 23 were waited for; matrix products, arithmetic and copies ran while one was open for 23% of the time, Pallas kernels for 5%

profile of v2, /device:TPU:0, one launch (start us, length us, event | category | flops | bytes accessed | tf_op | source)
XLA Modules:
  0.0 1092.5 jit_solution(11805796248474080661)
XLA Ops:
  13.6 5.2 all-to-all-start
  21.0 7.9 all-to-all-done
  28.9 4.2 all-to-all-start.2
  35.4 18.5 %all-to-all-done.2 = bf16[8,64,1024]{2,1,0:T(8,128)(2,1)} async-done(((bf16[8,64,1024]{2,1,0:T(8,128)(2,1)}), bf16[8,64,1024]{2,1,0:T(8,128)(2,1)}, u32[]{:S(2)}, u32[]{:S(2)}) %all-to-all-start.2) | async-done | bytes 1048608 | tf_op jit(solution)/shard_map/all_to_all | solution.py:84
  53.8 4.2 all-to-all-start.3
  58.1 79.8 %all-gather.2 = bf16[32,64,2]{1,2,0:T(2,128)(2,1)S(1)} all-gather(bf16[1,64,2]{1,2,0:T(2,128)(2,1)S(1)} %maximum_bitcast_fusion.1), channel_id=1, replica_groups=mesh['a'=2,'b'=2,'c'=2,'h'=2,'l'=2] {'a','b','c','h','l'}, dimensions={0}, use_global_device_ids=true | all-gather | bytes 8448 | tf_op jit(solution)/shard_map/all_gather | solution.py:519
  138.0 13.4 %all-gather.1 = s32[1,2048]{1,0:T(1,128)S(1)} all-gather(s32[1,256]{1,0:T(1,128)S(1)} %copy-done.65), channel_id=3, replica_groups=mesh['a'=2,'b'=2,'c'=2,'h'=2,'l'=2] {'b','c','l'}, dimensions={1}, use_global_device_ids=true | all-gather | bytes 9216 | tf_op jit(solution)/shard_map/all_gather | solution.py:522
  153.8 27.8 %collective-permute-done.1 = bf16[8,64,384]{2,1,0:T(8,128)(2,1)} collective-permute-done((bf16[8,64,384]{2,1,0:T(8,128)(2,1)S(1)}, bf16[8,64,384]{2,1,0:T(8,128)(2,1)}, u32[]{:S(2)}, u32[]{:S(2)}) %collective-permute-start.1) | collective-permute-done | bytes 393248 | tf_op jit(solution)/shard_map/ppermute | solution.py:52
  182.8 4.3 all-reduce.1.length_ref
  195.0 4.6 all-to-all-start.4
  203.8 5.2 fusion.4
  209.7 4.1 fusion.11
  222.5 3.3 collective-permute-start.3
  231.9 3.1 copy.240
  240.3 3.3 add_convert_fusion.q_ref
  246.2 46.8 %collective-permute-done.3 = bf16[2,4,512,64]{2,3,1,0:T(8,128)(2,1)} collective-permute-done((bf16[2,4,512,64]{2,3,1,0:T(8,128)(2,1)}, bf16[2,4,512,64]{2,3,1,0:T(8,128)(2,1)}, u32[]{:S(2)}, u32[]{:S(2)}) %collective-permute-start.3) | collective-permute-done | bytes 524320 | tf_op jit(solution)/shard_map/ppermute | solution.py:540
  293.0 3.4 collective-permute-start.11
  301.5 17.0 %shard_map.212 = bf16[4,512,256]{2,1,0:T(8,128)(2,1)S(1)} custom-call(s32[1]{0:T(128)} %bitcast.2.late_ref, s32[4]{0:T(128)S(1)} %all-reduce.1.length_ref, bf16[4,512,256]{2,1,0:T(8,128)(2,1)S(1)} %add_convert_fusion.q_ref, bf16[4,512,64]{2,1,0:T(8,128)(2,1)S(1)} %bitcast.328, bf16[4,512,64]{2,1,0:T(8,128)(2,1)S(1)} %bitcast.330, ...), custom_call_target="tpu_custom_call" | custom-call | flops 3000000000 | bytes 8388608 | tf_op jit(solution)/shard_map/pallas_call | solution.py:201
  319.8 39.9 %all-to-all-start.1 = ((bf16[8,256,256]{1,2,0:T(8,128)(2,1)}), bf16[8,256,256]{1,2,0:T(8,128)(2,1)S(1)}, u32[]{:S(2)}, u32[]{:S(2)}) async-start(bf16[8,256,256]{1,2,0:T(8,128)(2,1)} %copy.248), calls=%async_computation.1 | async-start | bytes 2097152 | tf_op jit(solution)/shard_map/all_to_all | solution.py:546
  390.8 17.7 %collective-permute-done.6 = bf16[8,64,1024]{2,1,0:T(8,128)(2,1)S(1)} collective-permute-done((bf16[8,64,1024]{2,1,0:T(8,128)(2,1)}, bf16[8,64,1024]{2,1,0:T(8,128)(2,1)S(1)}, u32[]{:S(2)}, u32[]{:S(2)}) %collective-permute-start.6) | collective-permute-done | bytes 1048608 | tf_op jit(solution)/shard_map/ppermute | solution.py:52
  409.5 21.4 %collective-permute-done.9 = bf16[8,64,1024]{2,1,0:T(8,128)(2,1)S(1)} collective-permute-done((bf16[8,64,1024]{2,1,0:T(8,128)(2,1)}, bf16[8,64,1024]{2,1,0:T(8,128)(2,1)S(1)}, u32[]{:S(2)}, u32[]{:S(2)}) %collective-permute-start.9) | collective-permute-done | bytes 1048608 | tf_op jit(solution)/shard_map/ppermute | solution.py:52
  432.0 21.0 %collective-permute-done.12 = bf16[8,64,1024]{2,1,0:T(8,128)(2,1)S(1)} collective-permute-done((bf16[8,64,1024]{2,1,0:T(8,128)(2,1)}, bf16[8,64,1024]{2,1,0:T(8,128)(2,1)S(1)}, u32[]{:S(2)}, u32[]{:S(2)}) %collective-permute-start.12) | collective-permute-done | bytes 1048608 | tf_op jit(solution)/shard_map/ppermute | solution.py:52
  455.1 6.4 multiply_reduce_fusion.2
  462.8 107.9 %shard_map.213 = (f32[256,2048]{1,0:T(8,128)}, bf16[8,256,2048]{2,1,0:T(8,128)(2,1)}, bf16[2048,1024]{1,0:T(8,128)(2,1)}, bf16[2048,1024]{1,0:T(8,128)(2,1)}, bf16[2048,1024]{1,0:T(8,128)(2,1)}) custom-call(bf16[256,2048]{1,0:T(8,128)(2,1)} %multiply_convert_fusion.own_ref, bf16[8,256,2048]{2,1,0:T(8,128)(2,1)} %bitcast.390, ...), custom_call_target="tpu_custom_call" | custom-call | flops 77309411328 | bytes 62914560 | tf_op jit(solution)/shard_map/pallas_call | solution.py:458
  570.7 4.9 slice_bitcast_fusion
  586.2 41.7 %collective-permute-done.35 = bf16[4,2,128,1024]{3,2,1,0:T(8,128)(2,1)} collective-permute-done((bf16[4,2,128,1024]{3,2,1,0:T(8,128)(2,1)}, bf16[4,2,128,1024]{3,2,1,0:T(8,128)(2,1)}, u32[]{:S(2)}, u32[]{:S(2)}) %collective-permute-start.35) | collective-permute-done | bytes 2097184 | tf_op jit(solution)/shard_map/ppermute | solution.py:52
  630.4 5.4 convert_add_fusion
  636.0 3.2 collective-permute-start.14
  639.6 33.2 %collective-permute-done.33 = bf16[4,2,128,1024]{3,2,1,0:T(8,128)(2,1)} collective-permute-done((bf16[4,2,128,1024]{3,2,1,0:T(8,128)(2,1)S(1)}, bf16[4,2,128,1024]{3,2,1,0:T(8,128)(2,1)}, u32[]{:S(2)}, u32[]{:S(2)}) %collective-permute-start.33) | collective-permute-done | bytes 2097184 | tf_op jit(solution)/shard_map/ppermute | solution.py:52
  677.8 39.0 %collective-permute-done.31 = bf16[4,2,128,1024]{3,2,1,0:T(8,128)(2,1)} collective-permute-done((bf16[4,2,128,1024]{3,2,1,0:T(8,128)(2,1)}, bf16[4,2,128,1024]{3,2,1,0:T(8,128)(2,1)}, u32[]{:S(2)}, u32[]{:S(2)}) %collective-permute-start.31) | collective-permute-done | bytes 2097184 | tf_op jit(solution)/shard_map/ppermute | solution.py:52
  721.8 3.2 collective-permute-start.15
  726.5 9.7 collective-permute-done.15
  736.4 17.7 %collective-permute-done.17 = bf16[256,1024]{1,0:T(8,128)(2,1)S(1)} collective-permute-done((bf16[256,1024]{1,0:T(8,128)(2,1)S(1)}, bf16[256,1024]{1,0:T(8,128)(2,1)S(1)}, u32[]{:S(2)}, u32[]{:S(2)}) %collective-permute-start.17) | collective-permute-done | bytes 524320 | tf_op jit(solution)/shard_map/ppermute | solution.py:52
  760.5 6.3 all-to-all-start.5
  766.8 3.4 fusion.25
  772.6 5.7 copy-done.9
  781.4 6.8 all-to-all-done.5
  788.2 4.2 all-to-all-start.9
  794.6 35.0 %shard_map.214 = (f32[4,512,256]{2,1,0:T(8,128)}, f32[4,512,64]{2,1,0:T(8,128)S(1)}, f32[4,512,64]{2,1,0:T(8,128)S(1)}, bf16[4,512,64]{2,1,0:T(8,128)(2,1)S(1)}, bf16[4,512,64]{2,1,0:T(8,128)(2,1)S(1)}) custom-call(s32[1]{0:T(128)} %bitcast.2.late_ref, s32[4]{0:T(128)S(1)} %all-reduce.1.length_ref, bf16[4,512,256]{2,1,0:T(8,128)(2,1)} %copy-done, ...), custom_call_target="tpu_custom_call" | custom-call | flops 8000000000 | bytes 8388608 | tf_op jit(solution)/shard_map/pallas_call | solution.py:201
  831.2 3.0 copy.269
  834.2 3.7 reshape.381
  837.9 3.2 broadcast_multiply_fusion
  846.5 3.1 copy.268
  853.0 18.1 %collective-permute-done.18 = bf16[2,4,512,64]{2,3,1,0:T(8,128)(2,1)} collective-permute-done((bf16[2,4,512,64]{2,3,1,0:T(8,128)(2,1)}, bf16[2,4,512,64]{2,3,1,0:T(8,128)(2,1)}, u32[]{:S(2)}, u32[]{:S(2)}) %collective-permute-start.18) | collective-permute-done | bytes 524320 | tf_op jit(solution)/shard_map/ppermute | solution.py:584
  881.0 11.4 %fusion.3 = (f32[2048]{0:T(1024)S(1)}, f32[2048,2048]{1,0:T(8,128)}) fusion(bf16[1,2048,2048]{2,1,0:T(8,128)(2,1)} %all-gather.11.cloned.1.call-done, f32[2048]{0:T(1024)S(1)} %copy-done.62, bf16[2048,384]{1,0:T(8,128)(2,1)S(1)} %bitcast.364, bf16[2048,64]{0,1:T(8,128)(2,1)S(1)} %copy-done.52, bf16[2048,64]{0,1:T(8,128)(2,1)S(1)} %fusion.55, ...), kind=kOutput, calls=%fused_computation.5 | convolution fusion | flops 3242719232 | bytes 28327936 | tf_op jit(solution)/shard_map/dot_general | solution.py:131
  892.5 4.1 all-to-all-start.8
  896.6 7.0 fusion.9
  906.1 6.6 reshape.385
  918.6 3.2 fusion.26
  921.8 6.0 fusion.6
  927.8 4.3 all-to-all-start.7
  932.1 3.6 constant_dynamic-slice_fusion.1
  938.9 4.4 collective-permute-done.24
  945.2 5.9 bitcast_add_fusion
  951.1 3.3 copy-done.11
  957.8 12.9 %collective-permute-done.25 = bf16[4,128,512]{2,1,0:T(8,128)(2,1)S(1)} collective-permute-done((bf16[4,128,512]{2,1,0:T(8,128)(2,1)S(1)}, bf16[4,128,512]{2,1,0:T(8,128)(2,1)S(1)}, u32[]{:S(2)}, u32[]{:S(2)}) %collective-permute-start.25) | collective-permute-done | bytes 524320 | tf_op jit(solution)/shard_map/ppermute | solution.py:52
  971.7 3.7 all-to-all-start.6
  983.2 26.0 %all-to-all-done.6 = bf16[8,64,512]{2,1,0:T(8,128)(2,1)S(1)} async-done(((bf16[8,64,512]{2,1,0:T(8,128)(2,1)}), bf16[8,64,512]{2,1,0:T(8,128)(2,1)S(1)}, u32[]{:S(2)}, u32[]{:S(2)}) %all-to-all-start.6) | async-done | bytes 524320 | tf_op jit(solution)/shard_map/all_to_all | solution.py:103
  1010.2 3.4 bitcast_add_fusion.2
  1015.7 6.0 bitcast_add_fusion.1
  1035.9 4.2 collective-permute-done.28
  1043.1 17.5 %collective-permute-done.20 = bf16[2,256,1024]{2,1,0:T(8,128)(2,1)} collective-permute-done((bf16[2,256,1024]{2,1,0:T(8,128)(2,1)S(1)}, bf16[2,256,1024]{2,1,0:T(8,128)(2,1)}, u32[]{:S(2)}, u32[]{:S(2)}) %collective-permute-start.20) | collective-permute-done | bytes 1048608 | tf_op jit(solution)/shard_map/ppermute | solution.py:52
  1068.6 5.7 collective-permute-done.21
  1074.6 7.1 collective-permute-done.23
  (359 shorter events, 209.1 us)
Async XLA Ops:
  7.2 196.6 %all-gather.11.cloned.1.call-start = ((), (), s32[]{:S(2)}) async-start(), calls=%async_computation.12 | async-start | bytes 9437184 | tf_op jit(solution)/shard_map/all_gather | solution.py:521
  7.9 446.2 %all-gather.7.cloned.1.call-start = ((), (), s32[]{:S(2)}) async-start(), calls=%async_computation.10 | async-start | bytes 8650752 | tf_op jit(solution)/shard_map/all_gather | solution.py:549
  8.7 454.1 %all-gather.9.cloned.1.call-start = ((), (), s32[]{:S(2)}) async-start(), calls=%async_computation.11 | async-start | bytes 9437184 | tf_op jit(solution)/shard_map/all_gather | solution.py:553
  13.6 15.3 %all-to-all-start = ((bf16[8,64,384]{2,1,0:T(8,128)(2,1)}), bf16[8,64,384]{2,1,0:T(8,128)(2,1)S(1)}, u32[]{:S(2)}, u32[]{:S(2)}) async-start(bf16[8,64,384]{2,1,0:T(8,128)(2,1)} %copy.234), calls=%async_computation | async-start | bytes 786432 | tf_op jit(solution)/shard_map/all_to_all | solution.py:84
  28.9 25.0 %all-to-all-start.2 = ((bf16[8,64,1024]{2,1,0:T(8,128)(2,1)}), bf16[8,64,1024]{2,1,0:T(8,128)(2,1)}, u32[]{:S(2)}, u32[]{:S(2)}) async-start(bf16[8,64,1024]{2,1,0:T(8,128)(2,1)} %copy.249), calls=%async_computation.2 | async-start | bytes 2097152 | tf_op jit(solution)/shard_map/all_to_all | solution.py:84
  33.8 24.3 %copy-start.66 = (bf16[64]{0:T(256)(128)(2,1)S(1)}, bf16[64]{0:T(256)(128)(2,1)}, u32[]{:S(2)}) copy-start(bf16[64]{0:T(256)(128)(2,1)} %param.21) | copy-start | bytes 388
  33.8 24.3 %copy-start.67 = (bf16[64]{0:T(256)(128)(2,1)S(1)}, bf16[64]{0:T(256)(128)(2,1)}, u32[]{:S(2)}) copy-start(bf16[64]{0:T(256)(128)(2,1)} %param.16) | copy-start | bytes 388
  33.8 104.3 %copy-start.65 = (s32[1,256]{1,0:T(1,128)S(1)}, s32[1,256]{1,0:T(1,128)}, u32[]{:S(2)}) copy-start(s32[1,256]{1,0:T(1,128)} %param.15) | copy-start | bytes 3076
  33.8 117.6 %copy-start.68 = (u32[32]{0:T(128)S(1)}, u32[32]{0:T(128)}, u32[]{:S(2)}) copy-start(u32[32]{0:T(128)} %constant.189) | copy-start | bytes 388
  33.8 153.3 %copy-start.48 = (bf16[64,8192]{1,0:T(8,128)(2,1)S(1)}, bf16[64,8192]{1,0:T(8,128)(2,1)}, u32[]{:S(2)}) copy-start(bf16[64,8192]{1,0:T(8,128)(2,1)} %param.24) | copy-start | bytes 3145732
  53.8 141.2 %all-to-all-start.3 = ((bf16[8,64,1024]{2,1,0:T(8,128)(2,1)}), bf16[8,64,1024]{2,1,0:T(8,128)(2,1)}, u32[]{:S(2)}, u32[]{:S(2)}) async-start(bf16[8,64,1024]{2,1,0:T(8,128)(2,1)} %copy.254), calls=%async_computation.3 | async-start | bytes 2097152 | tf_op jit(solution)/shard_map/all_to_all | solution.py:84
  152.8 28.9 %collective-permute-start.1 = (bf16[8,64,384]{2,1,0:T(8,128)(2,1)S(1)}, bf16[8,64,384]{2,1,0:T(8,128)(2,1)}, u32[]{:S(2)}, u32[]{:S(2)}) collective-permute-start(bf16[8,64,384]{2,1,0:T(8,128)(2,1)S(1)} %all-to-all-done), channel_id=1, source_target_pairs={{0,2},{2,0},{1,3},{3,1},{4,6},{6,4},{5,7},{7,5},{8,10},{10,8},{9,1... | collective-permute-start | bytes 1179656 | tf_op jit(solution)/shard_map/ppermute | solution.py:52
  153.0 61.8 %copy-start.34 = (f32[2048,32]{0,1:T(8,128)}, f32[2048,32]{0,1:T(8,128)S(1)}, u32[]{:S(2)}) copy-start(f32[2048,32]{0,1:T(8,128)S(1)} %broadcast_multiply_fusion.1) | copy-start | bytes 786436
  153.0 36.6 %collective-permute-start = (bf16[8,64,384]{2,1,0:T(8,128)(2,1)S(1)}, bf16[8,64,384]{2,1,0:T(8,128)(2,1)}, u32[]{:S(2)}, u32[]{:S(2)}) collective-permute-start(bf16[8,64,384]{2,1,0:T(8,128)(2,1)S(1)} %all-to-all-done), channel_id=1, source_target_pairs={{0,16},{16,0},{1,17},{17,1},{2,18},{18,2},{3,19},{19,3},{4,20},{20... | collective-permute-start | bytes 1179656 | tf_op jit(solution)/shard_map/ppermute | solution.py:52
  181.7 11.4 %collective-permute-start.2 = (bf16[8,64,384]{2,1,0:T(8,128)(2,1)}, bf16[8,64,384]{2,1,0:T(8,128)(2,1)}, u32[]{:S(2)}, u32[]{:S(2)}) collective-permute-start(bf16[8,64,384]{2,1,0:T(8,128)(2,1)} %collective-permute-done.1), channel_id=1, source_target_pairs={{0,16},{16,0},{1,17},{17,1},{2,18},{18,2},{3,19},{19,3},{4,20},{20... | collective-permute-start | bytes 1179656 | tf_op jit(solution)/shard_map/ppermute | solution.py:52
  182.8 26.3 %copy-start.57 = (f32[1,2048]{1,0:T(1,128)}, f32[1,2048]{1,0:T(1,128)S(1)}, u32[]{:S(2)}) copy-start(f32[1,2048]{1,0:T(1,128)S(1)} %get-tuple-element.59) | copy-start | bytes 24580
  194.2 165.6 %collective-permute-start.4 = (bf16[8,64,1024]{2,1,0:T(8,128)(2,1)}, bf16[8,64,1024]{2,1,0:T(8,128)(2,1)}, u32[]{:S(2)}, u32[]{:S(2)}) collective-permute-start(bf16[8,64,1024]{2,1,0:T(8,128)(2,1)} %all-to-all-done.2), channel_id=1, source_target_pairs={{0,16},{16,0},{1,17},{17,1},{2,18},{18,2},{3,19},{19,3},{4,20},{20... | collective-permute-start | bytes 3145736 | tf_op jit(solution)/shard_map/ppermute | solution.py:52
  195.0 170.4 %collective-permute-start.5 = (bf16[8,64,1024]{2,1,0:T(8,128)(2,1)}, bf16[8,64,1024]{2,1,0:T(8,128)(2,1)}, u32[]{:S(2)}, u32[]{:S(2)}) collective-permute-start(bf16[8,64,1024]{2,1,0:T(8,128)(2,1)} %all-to-all-done.2), channel_id=1, source_target_pairs={{0,2},{2,0},{1,3},{3,1},{4,6},{6,4},{5,7},{7,5},{8,10},{10,8},{9,1... | collective-permute-start | bytes 3145736 | tf_op jit(solution)/shard_map/ppermute | solution.py:52
  195.0 51.2 %all-to-all-start.4 = ((bf16[8,64,1024]{2,1,0:T(8,128)(2,1)}), bf16[8,64,1024]{2,1,0:T(8,128)(2,1)}, u32[]{:S(2)}, u32[]{:S(2)}) async-start(bf16[8,64,1024]{2,1,0:T(8,128)(2,1)} %copy.259), calls=%async_computation.4 | async-start | bytes 2097152 | tf_op jit(solution)/shard_map/all_to_all | solution.py:84
  199.6 183.2 %collective-permute-start.7 = (bf16[8,64,1024]{2,1,0:T(8,128)(2,1)}, bf16[8,64,1024]{2,1,0:T(8,128)(2,1)}, u32[]{:S(2)}, u32[]{:S(2)}) collective-permute-start(bf16[8,64,1024]{2,1,0:T(8,128)(2,1)} %all-to-all-done.3), channel_id=1, source_target_pairs={{0,16},{16,0},{1,17},{17,1},{2,18},{18,2},{3,19},{19,3},{4,20},{20... | collective-permute-start | bytes 3145736 | tf_op jit(solution)/shard_map/ppermute | solution.py:52
  200.9 170.5 %collective-permute-start.8 = (bf16[8,64,1024]{2,1,0:T(8,128)(2,1)}, bf16[8,64,1024]{2,1,0:T(8,128)(2,1)}, u32[]{:S(2)}, u32[]{:S(2)}) collective-permute-start(bf16[8,64,1024]{2,1,0:T(8,128)(2,1)} %all-to-all-done.3), channel_id=1, source_target_pairs={{0,2},{2,0},{1,3},{3,1},{4,6},{6,4},{5,7},{7,5},{8,10},{10,8},{9,1... | collective-permute-start | bytes 3145736 | tf_op jit(solution)/shard_map/ppermute | solution.py:52
  222.5 70.5 %collective-permute-start.3 = (bf16[2,4,512,64]{2,3,1,0:T(8,128)(2,1)}, bf16[2,4,512,64]{2,3,1,0:T(8,128)(2,1)}, u32[]{:S(2)}, u32[]{:S(2)}) collective-permute-start(bf16[2,4,512,64]{2,3,1,0:T(8,128)(2,1)} %pad_maximum_fusion.7), channel_id=1, source_target_pairs={{0,2},{1,3},{4,6},{5,7},{8,10},{9,11},{12,14},{13,15},{16,18},{17,... | collective-permute-start | bytes 1572872 | tf_op jit(solution)/shard_map/ppermute | solution.py:540
  243.6 55.9 %copy-start = (bf16[4,512,256]{2,1,0:T(8,128)(2,1)}, bf16[4,512,256]{2,1,0:T(8,128)(2,1)S(1)}, u32[]{:S(2)}) copy-start(bf16[4,512,256]{2,1,0:T(8,128)(2,1)S(1)} %add_convert_fusion.q_ref) | copy-start | bytes 3145732
  293.0 84.0 %collective-permute-start.11 = (bf16[8,64,1024]{2,1,0:T(8,128)(2,1)}, bf16[8,64,1024]{2,1,0:T(8,128)(2,1)}, u32[]{:S(2)}, u32[]{:S(2)}) collective-permute-start(bf16[8,64,1024]{2,1,0:T(8,128)(2,1)} %all-to-all-done.4), channel_id=1, source_target_pairs={{0,2},{2,0},{1,3},{3,1},{4,6},{6,4},{5,7},{7,5},{8,10},{10,8},{9,1... | collective-permute-start | bytes 3145736 | tf_op jit(solution)/shard_map/ppermute | solution.py:52
  319.8 134.3 %all-to-all-start.1 = ((bf16[8,256,256]{1,2,0:T(8,128)(2,1)}), bf16[8,256,256]{1,2,0:T(8,128)(2,1)S(1)}, u32[]{:S(2)}, u32[]{:S(2)}) async-start(bf16[8,256,256]{1,2,0:T(8,128)(2,1)} %copy.248), calls=%async_computation.1 | async-start | bytes 2097152 | tf_op jit(solution)/shard_map/all_to_all | solution.py:546
  359.8 27.6 %collective-permute-start.10 = (bf16[8,64,1024]{2,1,0:T(8,128)(2,1)}, bf16[8,64,1024]{2,1,0:T(8,128)(2,1)S(1)}, u32[]{:S(2)}, u32[]{:S(2)}) collective-permute-start(bf16[8,64,1024]{2,1,0:T(8,128)(2,1)} %all-to-all-done.4), channel_id=1, source_target_pairs={{0,16},{16,0},{1,17},{17,1},{2,18},{18,2},{3,19},{19,3},{4,20},{20... | collective-permute-start | bytes 3145736 | tf_op jit(solution)/shard_map/ppermute | solution.py:52
  365.4 43.1 %collective-permute-start.6 = (bf16[8,64,1024]{2,1,0:T(8,128)(2,1)}, bf16[8,64,1024]{2,1,0:T(8,128)(2,1)S(1)}, u32[]{:S(2)}, u32[]{:S(2)}) collective-permute-start(bf16[8,64,1024]{2,1,0:T(8,128)(2,1)} %collective-permute-done.5), channel_id=1, source_target_pairs={{0,16},{16,0},{1,17},{17,1},{2,18},{18,2},{3,19},{19,3},{4,20},{20... | collective-permute-start | bytes 3145736 | tf_op jit(solution)/shard_map/ppermute | solution.py:52
  371.4 59.5 %collective-permute-start.9 = (bf16[8,64,1024]{2,1,0:T(8,128)(2,1)}, bf16[8,64,1024]{2,1,0:T(8,128)(2,1)S(1)}, u32[]{:S(2)}, u32[]{:S(2)}) collective-permute-start(bf16[8,64,1024]{2,1,0:T(8,128)(2,1)} %collective-permute-done.8), channel_id=1, source_target_pairs={{0,16},{16,0},{1,17},{17,1},{2,18},{18,2},{3,19},{19,3},{4,20},{20... | collective-permute-start | bytes 3145736 | tf_op jit(solution)/shard_map/ppermute | solution.py:52
  377.0 76.0 %collective-permute-start.12 = (bf16[8,64,1024]{2,1,0:T(8,128)(2,1)}, bf16[8,64,1024]{2,1,0:T(8,128)(2,1)S(1)}, u32[]{:S(2)}, u32[]{:S(2)}) collective-permute-start(bf16[8,64,1024]{2,1,0:T(8,128)(2,1)} %collective-permute-done.11), channel_id=1, source_target_pairs={{0,16},{16,0},{1,17},{17,1},{2,18},{18,2},{3,19},{19,3},{4,20},{20... | collective-permute-start | bytes 3145736 | tf_op jit(solution)/shard_map/ppermute | solution.py:52
  575.6 54.8 %collective-permute-start.13 = (bf16[2,2,256,2048]{3,2,1,0:T(8,128)(2,1)}, bf16[2,2,256,2048]{3,2,1,0:T(8,128)(2,1)}, u32[]{:S(2)}, u32[]{:S(2)}) collective-permute-start(bf16[2,2,256,2048]{3,2,1,0:T(8,128)(2,1)} %slice_bitcast_fusion), channel_id=1, source_target_pairs={{0,4},{4,0},{1,5},{5,1},{2,6},{6,2},{3,7},{7,3},{8,12},{12,8},{9,1... | collective-permute-start | bytes 12582920 | tf_op jit(solution)/shard_map/ppermute | solution.py:52
  579.1 48.8 %collective-permute-start.35 = (bf16[4,2,128,1024]{3,2,1,0:T(8,128)(2,1)}, bf16[4,2,128,1024]{3,2,1,0:T(8,128)(2,1)}, u32[]{:S(2)}, u32[]{:S(2)}) collective-permute-start(bf16[4,2,128,1024]{3,2,1,0:T(8,128)(2,1)} %dynamic-slice_bitcast_fusion), channel_id=1, source_target_pairs={{0,16},{16,0},{1,17},{17,1},{2,18},{18,2},{3,19},{19,3},{4,20},{20... | collective-permute-start | bytes 6291464 | tf_op jit(solution)/shard_map/ppermute | solution.py:52
  581.8 91.0 %collective-permute-start.33 = (bf16[4,2,128,1024]{3,2,1,0:T(8,128)(2,1)S(1)}, bf16[4,2,128,1024]{3,2,1,0:T(8,128)(2,1)}, u32[]{:S(2)}, u32[]{:S(2)}) collective-permute-start(bf16[4,2,128,1024]{3,2,1,0:T(8,128)(2,1)S(1)} %dynamic-slice_bitcast_fusion.1), channel_id=1, source_target_pairs={{0,16},{16,0},{1,17},{17,1},{2,18},{18,2},{3,19},{19,3},{4,20},{20... | collective-permute-start | bytes 6291464 | tf_op jit(solution)/shard_map/ppermute | solution.py:52
  584.6 132.2 %collective-permute-start.31 = (bf16[4,2,128,1024]{3,2,1,0:T(8,128)(2,1)}, bf16[4,2,128,1024]{3,2,1,0:T(8,128)(2,1)}, u32[]{:S(2)}, u32[]{:S(2)}) collective-permute-start(bf16[4,2,128,1024]{3,2,1,0:T(8,128)(2,1)} %dynamic-slice_bitcast_fusion.2), channel_id=1, source_target_pairs={{0,16},{16,0},{1,17},{17,1},{2,18},{18,2},{3,19},{19,3},{4,20},{20... | collective-permute-start | bytes 6291464 | tf_op jit(solution)/shard_map/ppermute | solution.py:52
  585.5 42.4 %copy-start.40 = (bf16[2048,1024]{1,0:T(8,128)(2,1)S(1)}, bf16[2048,1024]{1,0:T(8,128)(2,1)}, u32[]{:S(2)}) copy-start(bf16[2048,1024]{1,0:T(8,128)(2,1)} %get-tuple-element.30) | copy-start | bytes 12582916
  635.9 36.9 %copy-start.38 = (bf16[2048,1024]{1,0:T(8,128)(2,1)S(1)}, bf16[2048,1024]{1,0:T(8,128)(2,1)}, u32[]{:S(2)}) copy-start(bf16[2048,1024]{1,0:T(8,128)(2,1)} %get-tuple-element.29) | copy-start | bytes 12582916
  636.0 84.7 %collective-permute-start.14 = (bf16[2,256,1024]{2,1,0:T(8,128)(2,1)S(1)}, bf16[2,256,1024]{2,1,0:T(8,128)(2,1)S(1)}, u32[]{:S(2)}, u32[]{:S(2)}) collective-permute-start(bf16[2,256,1024]{2,1,0:T(8,128)(2,1)S(1)} %slice_bitcast_fusion.9), channel_id=1, source_target_pairs={{0,1},{1,0},{2,3},{3,2},{4,5},{5,4},{6,7},{7,6},{8,9},{9,8},{10,11... | collective-permute-start | bytes 3145736 | tf_op jit(solution)/shard_map/ppermute | solution.py:52
  639.3 81.3 %collective-permute-start.16 = (bf16[2,256,1024]{2,1,0:T(8,128)(2,1)S(1)}, bf16[2,256,1024]{2,1,0:T(8,128)(2,1)S(1)}, u32[]{:S(2)}, u32[]{:S(2)}) collective-permute-start(bf16[2,256,1024]{2,1,0:T(8,128)(2,1)S(1)} %slice_bitcast_fusion.7), channel_id=1, source_target_pairs={{0,8},{8,0},{1,9},{9,1},{2,10},{10,2},{3,11},{11,3},{4,12},{12,4},... | collective-permute-start | bytes 3145736 | tf_op jit(solution)/shard_map/ppermute | solution.py:52
  639.6 85.6 %collective-permute-start.36 = (bf16[4,128,1024]{2,1,0:T(8,128)(2,1)S(1)}, bf16[4,128,1024]{2,1,0:T(8,128)(2,1)S(1)}, u32[]{:S(2)}, u32[]{:S(2)}) collective-permute-start(bf16[4,128,1024]{2,1,0:T(8,128)(2,1)S(1)} %fusion.33), channel_id=1, source_target_pairs={{0,2},{2,0},{1,3},{3,1},{4,6},{6,4},{5,7},{7,5},{8,10},{10,8},{9,1... | collective-permute-start | bytes 3145736 | tf_op jit(solution)/shard_map/ppermute | solution.py:52
  672.8 44.0 %copy-start.37 = (bf16[2048,1024]{1,0:T(8,128)(2,1)S(1)}, bf16[2048,1024]{1,0:T(8,128)(2,1)}, u32[]{:S(2)}) copy-start(bf16[2048,1024]{1,0:T(8,128)(2,1)} %get-tuple-element.28) | copy-start | bytes 12582916
  676.8 90.0 %collective-permute-start.34 = (bf16[4,128,1024]{2,1,0:T(8,128)(2,1)}, bf16[4,128,1024]{2,1,0:T(8,128)(2,1)}, u32[]{:S(2)}, u32[]{:S(2)}) collective-permute-start(bf16[4,128,1024]{2,1,0:T(8,128)(2,1)} %fusion.32), channel_id=1, source_target_pairs={{0,2},{2,0},{1,3},{3,1},{4,6},{6,4},{5,7},{7,5},{8,10},{10,8},{9,1... | collective-permute-start | bytes 3145736 | tf_op jit(solution)/shard_map/ppermute | solution.py:52
  720.6 198.0 %collective-permute-start.32 = (bf16[4,128,1024]{2,1,0:T(8,128)(2,1)}, bf16[4,128,1024]{2,1,0:T(8,128)(2,1)}, u32[]{:S(2)}, u32[]{:S(2)}) collective-permute-start(bf16[4,128,1024]{2,1,0:T(8,128)(2,1)} %fusion.31), channel_id=1, source_target_pairs={{0,2},{2,0},{1,3},{3,1},{4,6},{6,4},{5,7},{7,5},{8,10},{10,8},{9,1... | collective-permute-start | bytes 3145736 | tf_op jit(solution)/shard_map/ppermute | solution.py:52
  721.8 14.4 %collective-permute-start.15 = (bf16[256,1024]{1,0:T(8,128)(2,1)S(1)}, bf16[256,1024]{1,0:T(8,128)(2,1)S(1)}, u32[]{:S(2)}, u32[]{:S(2)}) collective-permute-start(bf16[256,1024]{1,0:T(8,128)(2,1)S(1)} %fusion.49), channel_id=1, source_target_pairs={{0,8},{8,0},{1,9},{9,1},{2,10},{10,2},{3,11},{11,3},{4,12},{12,4},... | collective-permute-start | bytes 1572872 | tf_op jit(solution)/shard_map/ppermute | solution.py:52
  725.1 29.0 %collective-permute-start.17 = (bf16[256,1024]{1,0:T(8,128)(2,1)S(1)}, bf16[256,1024]{1,0:T(8,128)(2,1)S(1)}, u32[]{:S(2)}, u32[]{:S(2)}) collective-permute-start(bf16[256,1024]{1,0:T(8,128)(2,1)S(1)} %fusion.50), channel_id=1, source_target_pairs={{0,1},{1,0},{2,3},{3,2},{4,5},{5,4},{6,7},{7,6},{8,9},{9,8},{10,11... | collective-permute-start | bytes 1572872 | tf_op jit(solution)/shard_map/ppermute | solution.py:52
  726.5 27.8 %copy-start.31 = (bf16[1,256,2048]{2,1,0:T(8,128)(2,1)S(1)}, bf16[1,256,2048]{2,1,0:T(8,128)(2,1)}, u32[]{:S(2)}) copy-start(bf16[1,256,2048]{2,1,0:T(8,128)(2,1)} %param.25) | copy-start | bytes 3145732
  726.5 27.8 %copy-start.64 = (pred[256]{0:T(512)(128)(4,1)S(1)}, pred[256]{0:T(512)(128)(4,1)}, u32[]{:S(2)}) copy-start(pred[256]{0:T(512)(128)(4,1)} %copy-done.63) | copy-start | bytes 772
  760.5 27.8 %all-to-all-start.5 = ((bf16[8,256,256]{2,1,0:T(8,128)(2,1)}), bf16[8,256,256]{2,1,0:T(8,128)(2,1)S(1)}, u32[]{:S(2)}, u32[]{:S(2)}) async-start(bf16[8,256,256]{2,1,0:T(8,128)(2,1)} %bitcast.325), calls=%async_computation.5 | async-start | bytes 2097152 | tf_op jit(solution)/shard_map/all_to_all | solution.py:573
  780.9 164.2 %collective-permute-start.26 = (bf16[2,2,2,2,64,2048]{5,4,3,2,1,0:T(8,128)(2,1)}, bf16[2,2,2,2,64,2048]{5,4,3,2,1,0:T(8,128)(2,1)}, u32[]{:S(2)}, u32[]{:S(2)}) collective-permute-start(bf16[2,2,2,2,64,2048]{5,4,3,2,1,0:T(8,128)(2,1)} %fusion.5), channel_id=1, source_target_pairs={{0,4},{4,0},{1,5},{5,1},{2,6},{6,2},{3,7},{7,3},{8,12},{12,8},{9,1... | collective-permute-start | bytes 12582920 | tf_op jit(solution)/shard_map/ppermute | solution.py:52
  788.2 104.2 %all-to-all-start.9 = ((bf16[8,64,1024]{2,1,0:T(8,128)(2,1)}), bf16[8,64,1024]{2,1,0:T(8,128)(2,1)}, u32[]{:S(2)}, u32[]{:S(2)}) async-start(bf16[8,64,1024]{2,1,0:T(8,128)(2,1)} %bitcast.143), calls=%async_computation.9 | async-start | bytes 2097152 | tf_op jit(solution)/shard_map/all_to_all | solution.py:103
  842.5 28.5 %collective-permute-start.18 = (bf16[2,4,512,64]{2,3,1,0:T(8,128)(2,1)}, bf16[2,4,512,64]{2,3,1,0:T(8,128)(2,1)}, u32[]{:S(2)}, u32[]{:S(2)}) collective-permute-start(bf16[2,4,512,64]{2,3,1,0:T(8,128)(2,1)} %copy.270), channel_id=1, source_target_pairs={{2,0},{3,1},{6,4},{7,5},{10,8},{11,9},{14,12},{15,13},{18,16},{19,... | collective-permute-start | bytes 1572872 | tf_op jit(solution)/shard_map/ppermute | solution.py:584
  892.5 35.4 %all-to-all-start.8 = ((bf16[8,64,1024]{2,1,0:T(8,128)(2,1)}), bf16[8,64,1024]{2,1,0:T(8,128)(2,1)S(1)}, u32[]{:S(2)}, u32[]{:S(2)}) async-start(bf16[8,64,1024]{2,1,0:T(8,128)(2,1)} %bitcast.136), calls=%async_computation.8 | async-start | bytes 2097152 | tf_op jit(solution)/shard_map/all_to_all | solution.py:103
  917.5 25.8 %collective-permute-start.24 = (bf16[4,2,128,512]{3,2,0,1:T(8,128)(2,1)}, bf16[4,2,128,512]{3,2,0,1:T(8,128)(2,1)}, u32[]{:S(2)}, u32[]{:S(2)}) collective-permute-start(bf16[4,2,128,512]{3,2,0,1:T(8,128)(2,1)} %bitcast.370), channel_id=1, source_target_pairs={{0,16},{16,0},{1,17},{17,1},{2,18},{18,2},{3,19},{19,3},{4,20},{20... | collective-permute-start | bytes 3145736 | tf_op jit(solution)/shard_map/ppermute | solution.py:52
  927.8 43.9 %all-to-all-start.7 = ((bf16[8,64,1024]{2,1,0:T(8,128)(2,1)}), bf16[8,64,1024]{2,1,0:T(8,128)(2,1)}, u32[]{:S(2)}, u32[]{:S(2)}) async-start(bf16[8,64,1024]{2,1,0:T(8,128)(2,1)} %bitcast.129), calls=%async_computation.7 | async-start | bytes 2097152 | tf_op jit(solution)/shard_map/all_to_all | solution.py:103
  938.5 77.2 %collective-permute-start.19 = (bf16[2,2,256,2048]{3,2,1,0:T(8,128)(2,1)}, bf16[2,2,256,2048]{3,2,1,0:T(8,128)(2,1)}, u32[]{:S(2)}, u32[]{:S(2)}) collective-permute-start(bf16[2,2,256,2048]{3,2,1,0:T(8,128)(2,1)} %fusion.6), channel_id=1, source_target_pairs={{0,4},{4,0},{1,5},{5,1},{2,6},{6,2},{3,7},{7,3},{8,12},{12,8},{9,1... | collective-permute-start | bytes 12582920 | tf_op jit(solution)/shard_map/ppermute | solution.py:52
  945.1 25.7 %collective-permute-start.25 = (bf16[4,128,512]{2,1,0:T(8,128)(2,1)S(1)}, bf16[4,128,512]{2,1,0:T(8,128)(2,1)S(1)}, u32[]{:S(2)}, u32[]{:S(2)}) collective-permute-start(bf16[4,128,512]{2,1,0:T(8,128)(2,1)S(1)} %fusion.47), channel_id=1, source_target_pairs={{0,2},{2,0},{1,3},{3,1},{4,6},{6,4},{5,7},{7,5},{8,10},{10,8},{9,1... | collective-permute-start | bytes 1572872 | tf_op jit(solution)/shard_map/ppermute | solution.py:52
  956.2 54.1 %collective-permute-start.27 = (bf16[2,2,2,64,2048]{4,3,2,1,0:T(8,128)(2,1)}, bf16[2,2,2,64,2048]{4,3,2,1,0:T(8,128)(2,1)}, u32[]{:S(2)}, u32[]{:S(2)}) collective-permute-start(bf16[2,2,2,64,2048]{4,3,2,1,0:T(8,128)(2,1)} %fusion.19), channel_id=1, source_target_pairs={{0,8},{8,0},{1,9},{9,1},{2,10},{10,2},{3,11},{11,3},{4,12},{12,4},... | collective-permute-start | bytes 6291464 | tf_op jit(solution)/shard_map/ppermute | solution.py:52
  971.7 37.4 %all-to-all-start.6 = ((bf16[8,64,512]{2,1,0:T(8,128)(2,1)}), bf16[8,64,512]{2,1,0:T(8,128)(2,1)S(1)}, u32[]{:S(2)}, u32[]{:S(2)}) async-start(bf16[8,64,512]{2,1,0:T(8,128)(2,1)} %bitcast.107), calls=%async_computation.6 | async-start | bytes 1048576 | tf_op jit(solution)/shard_map/all_to_all | solution.py:103
  1013.8 26.3 %collective-permute-start.28 = (bf16[2,2,64,2048]{3,2,1,0:T(8,128)(2,1)S(1)}, bf16[2,2,64,2048]{3,2,1,0:T(8,128)(2,1)}, u32[]{:S(2)}, u32[]{:S(2)}) collective-permute-start(bf16[2,2,64,2048]{3,2,1,0:T(8,128)(2,1)S(1)} %fusion.30), channel_id=1, source_target_pairs={{0,1},{1,0},{2,3},{3,2},{4,5},{5,4},{6,7},{7,6},{8,9},{9,8},{10,11... | collective-permute-start | bytes 3145736 | tf_op jit(solution)/shard_map/ppermute | solution.py:52
  1026.8 33.8 %collective-permute-start.20 = (bf16[2,256,1024]{2,1,0:T(8,128)(2,1)S(1)}, bf16[2,256,1024]{2,1,0:T(8,128)(2,1)}, u32[]{:S(2)}, u32[]{:S(2)}) collective-permute-start(bf16[2,256,1024]{2,1,0:T(8,128)(2,1)S(1)} %fusion.28), channel_id=1, source_target_pairs={{0,1},{1,0},{2,3},{3,2},{4,5},{5,4},{6,7},{7,6},{8,9},{9,8},{10,11... | collective-permute-start | bytes 3145736 | tf_op jit(solution)/shard_map/ppermute | solution.py:52
  1034.3 26.3 %copy-start.20 = (f32[2,2,256,1024]{3,2,1,0:T(8,128)S(1)}, f32[2,2,256,1024]{3,2,1,0:T(8,128)}, u32[]{:S(2)}) copy-start(f32[2,2,256,1024]{3,2,1,0:T(8,128)} %copy-done.19) | copy-start | bytes 12582916
  1034.4 29.3 %collective-permute-start.22 = (bf16[2,256,1024]{2,1,0:T(8,128)(2,1)S(1)}, bf16[2,256,1024]{2,1,0:T(8,128)(2,1)S(1)}, u32[]{:S(2)}, u32[]{:S(2)}) collective-permute-start(bf16[2,256,1024]{2,1,0:T(8,128)(2,1)S(1)} %fusion.29), channel_id=1, source_target_pairs={{0,8},{8,0},{1,9},{9,1},{2,10},{10,2},{3,11},{11,3},{4,12},{12,4},... | collective-permute-start | bytes 3145736 | tf_op jit(solution)/shard_map/ppermute | solution.py:52
  1042.3 23.5 %collective-permute-start.29 = (bf16[2,64,2048]{2,1,0:T(8,128)(2,1)S(1)}, bf16[2,64,2048]{2,1,0:T(8,128)(2,1)S(1)}, u32[]{:S(2)}, u32[]{:S(2)}) collective-permute-start(bf16[2,64,2048]{2,1,0:T(8,128)(2,1)S(1)} %fusion.48), channel_id=1, source_target_pairs={{0,16},{16,0},{1,17},{17,1},{2,18},{18,2},{3,19},{19,3},{4,20},{20... | collective-permute-start | bytes 1572872 | tf_op jit(solution)/shard_map/ppermute | solution.py:52
  1062.3 12.1 %collective-permute-start.21 = (bf16[256,1024]{1,0:T(8,128)(2,1)S(1)}, bf16[256,1024]{1,0:T(8,128)(2,1)S(1)}, u32[]{:S(2)}, u32[]{:S(2)}) collective-permute-start(bf16[256,1024]{1,0:T(8,128)(2,1)S(1)} %fusion.45), channel_id=1, source_target_pairs={{0,8},{8,0},{1,9},{9,1},{2,10},{10,2},{3,11},{11,3},{4,12},{12,4},... | collective-permute-start | bytes 1572872 | tf_op jit(solution)/shard_map/ppermute | solution.py:52
  1064.3 17.4 %collective-permute-start.23 = (bf16[256,1024]{1,0:T(8,128)(2,1)S(1)}, bf16[256,1024]{1,0:T(8,128)(2,1)S(1)}, u32[]{:S(2)}, u32[]{:S(2)}) collective-permute-start(bf16[256,1024]{1,0:T(8,128)(2,1)S(1)} %fusion.46), channel_id=1, source_target_pairs={{0,1},{1,0},{2,3},{3,2},{4,5},{5,4},{6,7},{7,6},{8,9},{9,8},{10,11... | collective-permute-start | bytes 1572872 | tf_op jit(solution)/shard_map/ppermute | solution.py:52
  1066.0 19.0 %collective-permute-start.30 = (bf16[64,2048]{1,0:T(8,128)(2,1)S(1)}, bf16[64,2048]{1,0:T(8,128)(2,1)S(1)}, u32[]{:S(2)}, u32[]{:S(2)}) collective-permute-start(bf16[64,2048]{1,0:T(8,128)(2,1)S(1)} %fusion.58), channel_id=1, source_target_pairs={{0,2},{2,0},{1,3},{3,1},{4,6},{6,4},{5,7},{7,5},{8,10},{10,8},{9,1... | collective-permute-start | bytes 786440 | tf_op jit(solution)/shard_map/ppermute | solution.py:52
  (57 other events, 252.5 us)
Sparse Core Ops, SparseCore 0:
  9.6 77.8 all-gather.10
  90.4 89.4 all-gather.6
  181.4 110.7 all-gather.8

commit v3 on v2

--- a/solution.py
+++ b/solution.py
@@ -36,15 +36,28 @@
     return jnp.cos(angles), jnp.sin(angles)
 
 
-def rotate(v, cosine, sine):
-    first, second = jnp.split(v, 2, axis=-1)
-    return v * cosine + jnp.concatenate([-second, first], axis=-1) * sine
-
-
-def rotate_back(v, cosine, sine):
-    turned = v * sine
-    first, second = jnp.split(turned, 2, axis=-1)
-    return v * cosine + jnp.concatenate([second, -first], axis=-1)
+def rope_lanes(cosine, sine):
+    signed = jnp.where(jnp.arange(SIZE) < SIZE // 2, -sine, sine)
+    ones, zeros = jnp.ones_like(cosine), jnp.zeros_like(sine)
+    return (
+        jnp.concatenate([cosine, cosine, cosine, ones], axis=-1),
+        jnp.concatenate([signed, signed, signed, zeros], axis=-1),
+    )
+
+
+def swap_halves(v):
+    lane = lax.broadcasted_iota(jnp.int32, v.shape, 1)
+    low = lax.rem(lane, SIZE) < SIZE // 2
+    return jnp.where(low, pltpu.roll(v, 128 - SIZE // 2, 1), pltpu.roll(v, SIZE // 2, 1))
+
+
+def rope_blocks(v, cosine, sine, sign):
+    outs = []
+    for n in range(3):
+        block = v[:, n * 128 : (n + 1) * 128]
+        cols = slice(128, 256) if n == 2 else slice(0, 128)
+        outs.append(block * cosine[:, cols] + sign * swap_halves(block) * sine[:, cols])
+    return jnp.concatenate(outs, axis=-1)
 
 
 def shift(value, axis, step):
@@ -73,34 +86,19 @@
     return jnp.concatenate([left, right], axis=-1)
 
 
-def slices_of(weight, rows):
-    return weight.reshape(rows, 8, -1)
-
-
-def gather_slices(local):
-    rows, _, width = local.shape
-    n_a, n_h = lax.axis_size("a"), lax.axis_size("h")
-    a, h = lax.axis_index("a"), lax.axis_index("h")
-    piece = lax.all_to_all(local.transpose(1, 0, 2), TEAM, 0, 0, tiled=True)
-    whole = jnp.zeros((n_a, 4, n_h, 2 * rows, width), local.dtype)
-    for dh in range(n_h):
-        from_h = shift(piece, "h", -dh) if dh else piece
-        for da in range(n_a):
-            block = shift(from_h, "a", -da) if da else from_h
-            whole = lax.dynamic_update_slice(
-                whole,
-                block.reshape(1, 4, 1, 2 * rows, width),
-                (lax.rem(a + da, n_a), 0, lax.rem(h + dh, n_h), 0, 0),
-            )
-    return whole.reshape(-1, width)
-
-
-def scatter_slices(partial, rows):
-    width = partial.shape[-1]
-    view = partial.reshape(lax.axis_size("a"), 4, lax.axis_size("h"), 2 * rows, width)
-    view = scatter_step(view, "a", 0)
-    view = scatter_step(view, "h", 1)
-    owned = lax.all_to_all(view.reshape(8, rows, width).astype(BF), TEAM, 0, 0, tiled=True)
+def together(*values):
+    return lax.optimization_barrier(values)
+
+
+def fold_a(partial, rows):
+    view = partial.reshape(lax.axis_size("a"), 4, lax.axis_size("h"), 2 * rows, partial.shape[-1])
+    return scatter_step(view, "a", 0)
+
+
+def fold_team(view, rows):
+    owned = lax.all_to_all(
+        view.reshape(8, rows, view.shape[-1]).astype(BF), TEAM, 0, 0, tiled=True
+    )
     return owned.transpose(1, 0, 2).astype(F32)
 
 
@@ -155,41 +153,105 @@
     return own * part, early * part
 
 
-def forward_kernel(late_ref, length_ref, q_ref, k_ref, v_ref, ek_ref, ev_ref, o_ref):
+Q_END, K_END, V_END = SHARE * SIZE, SHARE * SIZE + SIZE, SHARE * SIZE + 2 * SIZE
+
+
+def project_kernel(x_ref, gain_ref, w_ref, cos_ref, sin_ref, normed_ref, out_ref):
+    x = x_ref[0].astype(F32)
+    normed = (x * norm_parts(x) * gain_ref[...]).astype(BF)
+    normed_ref[...] = normed
+    qkv = dot(normed, w_ref[...], NN)
+    out_ref[...] = rope_blocks(qkv, cos_ref[...], sin_ref[...], 1.0).astype(BF)
+
+
+def project_call(team_packed, gain, w_qkv, cosine, sine):
+    _, rows, _ = team_packed.shape
+    width = gain.shape[-1]
+    return pl.pallas_call(
+        project_kernel,
+        grid=(8,),
+        in_specs=[
+            pl.BlockSpec((1, rows, width), lambda i: (i, 0, 0)),
+            pl.BlockSpec((1, width), lambda i: (0, 0)),
+            pl.BlockSpec((width, V_END), lambda i: (0, 0)),
+            pl.BlockSpec((rows, 256), lambda i: (i, 0)),
+            pl.BlockSpec((rows, 256), lambda i: (i, 0)),
+        ],
+        out_specs=[
+            pl.BlockSpec((rows, width), lambda i: (i, 0)),
+            pl.BlockSpec((rows, V_END), lambda i: (i, 0)),
+        ],
+        out_shape=[
+            jax.ShapeDtypeStruct((8 * rows, width), BF),
+            jax.ShapeDtypeStruct((8 * rows, V_END), BF),
+        ],
+        compiler_params=pltpu.CompilerParams(vmem_limit_bytes=40 * 2**20),
+        cost_estimate=pl.CostEstimate(
+            flops=16 * rows * width * V_END, bytes_accessed=24 * 2**20, transcendentals=0
+        ),
+    )(team_packed, gain, w_qkv, cosine, sine)
+
+
+def unrotate_kernel(own_ref, back_ref, cos_ref, sin_ref, out_ref):
+    own = own_ref[...]
+    tail = own[:, Q_END:] + back_ref[...].astype(F32)
+    total = jnp.concatenate([own[:, :Q_END], tail], axis=-1)
+    out_ref[...] = rope_blocks(total, cos_ref[...], sin_ref[...], -1.0).astype(BF)
+
+
+def unrotate_call(own, back, cosine, sine):
+    tokens = own.shape[0]
+    rows = tokens // 4
+
+    def spec(x):
+        return pl.BlockSpec((rows, x.shape[1]), lambda i: (i, 0))
+
+    return pl.pallas_call(
+        unrotate_kernel,
+        grid=(4,),
+        in_specs=[spec(x) for x in (own, back, cosine, sine)],
+        out_specs=spec(own),
+        out_shape=jax.ShapeDtypeStruct(own.shape, BF),
+        cost_estimate=pl.CostEstimate(flops=10**7, bytes_accessed=9 * 2**20, transcendentals=0),
+    )(own, back, cosine, sine)
+
+
+def forward_kernel(late_ref, length_ref, qkv_ref, early_ref, o_ref):
     late, length = late_ref[0], length_ref[pl.program_id(0)]
+    keys, values = qkv_ref[0, :, Q_END:K_END], qkv_ref[0, :, K_END:V_END]
+    early_keys, early_values = early_ref[0, :, :SIZE], early_ref[0, :, SIZE:]
     outs = []
     for head in range(SHARE):
-        q = q_ref[0, :, head * SIZE : (head + 1) * SIZE]
-        own, early = softmax_parts(late, length, q, k_ref[0], ek_ref[0])
-        outs.append(dot(own.astype(BF), v_ref[0], NN) + dot(early.astype(BF), ev_ref[0], NN))
+        q = qkv_ref[0, :, head * SIZE : (head + 1) * SIZE]
+        own, early = softmax_parts(late, length, q, keys, early_keys)
+        outs.append(dot(own.astype(BF), values, NN) + dot(early.astype(BF), early_values, NN))
     o_ref[0] = jnp.concatenate(outs, axis=-1).astype(BF)
 
 
-def backward_kernel(
-    late_ref, length_ref, q_ref, k_ref, v_ref, ek_ref, ev_ref, g_ref, dq_ref, dk_ref, dv_ref, edk_ref, edv_ref
-):
+def backward_kernel(late_ref, length_ref, qkv_ref, early_ref, g_ref, d_ref, ed_ref):
     late, length = late_ref[0], length_ref[pl.program_id(0)]
+    keys, values = qkv_ref[0, :, Q_END:K_END], qkv_ref[0, :, K_END:V_END]
+    early_keys, early_values = early_ref[0, :, :SIZE], early_ref[0, :, SIZE:]
     scale = SIZE**-0.5
     dqs = []
     dk = dv = edk = edv = 0.0
     for head in range(SHARE):
-        q = q_ref[0, :, head * SIZE : (head + 1) * SIZE]
+        q = qkv_ref[0, :, head * SIZE : (head + 1) * SIZE]
         g = g_ref[0, :, head * SIZE : (head + 1) * SIZE]
-        own, early = softmax_parts(late, length, q, k_ref[0], ek_ref[0])
-        dp, edp = dot(g, v_ref[0], NT), dot(g, ev_ref[0], NT)
+        own, early = softmax_parts(late, length, q, keys, early_keys)
+        dp, edp = dot(g, values, NT), dot(g, early_values, NT)
         inner = jnp.sum(own * dp, axis=-1, keepdims=True) + jnp.sum(
             early * edp, axis=-1, keepdims=True
         )
         ds = (own * (dp - inner)).astype(BF)
         eds = (early * (edp - inner)).astype(BF)
-        dqs.append((dot(ds, k_ref[0], NN) + dot(eds, ek_ref[0], NN)) * scale)
+        dqs.append((dot(ds, keys, NN) + dot(eds, early_keys, NN)) * scale)
         dv = dv + dot(own.astype(BF), g, TN)
         edv = edv + dot(early.astype(BF), g, TN)
         dk = dk + dot(ds, q, TN)
         edk = edk + dot(eds, q, TN)
-    dq_ref[0] = jnp.concatenate(dqs, axis=-1)
-    dk_ref[0], dv_ref[0] = dk * scale, dv
-    edk_ref[0], edv_ref[0] = (edk * scale).astype(BF), edv.astype(BF)
+    d_ref[0] = jnp.concatenate(dqs + [dk * scale, dv], axis=-1)
+    ed_ref[0] = jnp.concatenate([edk * scale, edv], axis=-1).astype(BF)
 
 
 def attention_call(kernel, late, lengths, arrays, outs, flops):
@@ -218,9 +280,16 @@
 def ffn_kernel(
     own_ref,
     grad_ref,
-    wg_ref,
-    wu_ref,
-    wd_ref,
+    *refs,
+):
+    n_pieces = len(refs) - 28
+    ffn_body(own_ref, grad_ref, refs[:n_pieces], *refs[n_pieces:])
+
+
+def ffn_body(
+    own_ref,
+    grad_ref,
+    piece_refs,
     gn_ref,
     dn_ref,
     dwg_ref,
@@ -315,16 +384,24 @@
         gather_copy(own_ref, 2 * k, chip(k)).start()
     own_copy = pltpu.make_async_copy(own_ref, xs.at[part(0)], local_sem.at[0])
     own_copy.start()
-    loads = [
-        pltpu.make_async_copy(source, target, local_sem.at[1 + j])
-        for j, (source, target) in enumerate(((wg_ref, wg), (wu_ref, wu), (wd_ref, wd)))
-    ]
-    for load in loads:
-        load.start()
+    a, h = lax.axis_index("a"), lax.axis_index("h")
+    n_a, n_h = lax.axis_size("a"), lax.axis_size("h")
+    chunk = piece_refs[0].shape[1]
+    for j, target in enumerate((wg, wu, wd)):
+        near, near_a, far, far_a = piece_refs[4 * j : 4 * j + 4]
+        for dh, first, rest in ((0, near, near_a), (1, far, far_a)):
+            for da in range(n_a):
+                source = rest.at[da - 1] if da else first
+                ra, rh = lax.rem(a + n_a - da, n_a), lax.rem(h + dh, n_h)
+                for pair in range(4):
+                    start = pl.multiple_of(((ra * 4 + pair) * n_h + rh) * chunk, chunk)
+                    pltpu.make_async_copy(
+                        source.at[pair], target.at[pl.ds(start, chunk)], local_sem.at[1 + j]
+                    ).start()
     for slot in range(8):
         grad_copy(slot).start()
-    for load in loads:
-        load.wait()
+    for j, target in enumerate((wg, wu, wd)):
+        pltpu.make_async_copy(target, target, local_sem.at[1 + j]).wait()
     own_copy.wait()
 
     def block(i, carry):
@@ -449,15 +526,15 @@
         owner_copy(k).wait_send()
 
 
-def ffn_call(own, team_grad, gate_w, up_w, down_w):
+def ffn_call(own, team_grad, pieces):
     rows, width = own.shape
-    hidden = gate_w.shape[1]
+    hidden = pieces[0].shape[-1]
     team = 8 * rows
     anywhere = pl.BlockSpec(memory_space=pl.ANY)
     stages = max(3, width // hidden)
     return pl.pallas_call(
         ffn_kernel,
-        in_specs=[anywhere] * 5,
+        in_specs=[anywhere] * (2 + len(pieces)),
         out_specs=[pl.BlockSpec(memory_space=pltpu.VMEM)] + [anywhere] * 4,
         out_shape=[
             jax.ShapeDtypeStruct((rows, width), F32),
@@ -478,7 +555,272 @@
         cost_estimate=pl.CostEstimate(
             flops=18 * team * width * hidden, bytes_accessed=60 * 2**20, transcendentals=team * hidden
         ),
-    )(own, team_grad, gate_w, up_w, down_w)
+    )(own, team_grad, *pieces)
+
+
+def opening_kernel(
+    tok_ref,
+    grad_ref,
+    qkv_ref,
+    gain_ref,
+    gate_ref,
+    up_ref,
+    down_ref,
+    toks,
+    grads,
+    slab,
+    gains,
+    gate0,
+    gate_h,
+    gate_a,
+    gate_far,
+    up0,
+    up_h,
+    up_a,
+    down0,
+    down_a,
+    team_send,
+    team_recv,
+    tok_send,
+    tok_recv,
+    local_sem,
+    h_send,
+    h_recv,
+    a_send,
+    a_recv,
+):
+    a, b, c, h, l = (lax.axis_index(axis) for axis in EVERY)
+    n_a = lax.axis_size("a")
+    n_rows = qkv_ref.shape[0]
+    q_wide, f_wide, g_rows = slab.shape[-1], gate0.shape[-1], gain_ref.shape[0]
+
+    def flip(off):
+        return lax.rem(b + off // 4, 2), lax.rem(c + off // 2 % 2, 2), lax.rem(l + off % 2, 2)
+
+    def peer(off):
+        pb, pc, p_l = flip(off)
+        return {"b": pb, "c": pc, "l": p_l}
+
+    def number(off):
+        pb, pc, p_l = flip(off)
+        return (pb * 2 + pc) * 2 + p_l
+
+    def a_peer(step):
+        return {"a": lax.rem(a + step, n_a)}
+
+    h_peer = {"h": 1 - h}
+    barrier = pltpu.get_barrier_semaphore()
+    others = [peer(off) for off in range(1, 8)] + [h_peer] + [a_peer(s) for s in range(1, n_a)]
+    for other in others:
+        pl.semaphore_signal(barrier, inc=1, device_id=other, device_id_type=MESH)
+    pl.semaphore_wait(barrier, len(others))
+
+    def source(which, off):
+        t = number(off)
+        if which == 0:
+            return qkv_ref.at[:, pl.ds(pl.multiple_of(t * q_wide, 128), q_wide)]
+        if which == 1:
+            return gain_ref
+        ref = (gate_ref, up_ref, down_ref)[which - 2]
+        return ref.at[:, pl.ds(pl.multiple_of(t * f_wide, 128), f_wide)]
+
+    def place(which, off):
+        pb, pc, p_l = flip(off)
+        pair = pb * 2 + pc
+        rows = pl.ds(pl.multiple_of(p_l * n_rows, n_rows), n_rows)
+        if which == 0:
+            return slab.at[a, pair, h, rows]
+        if which == 1:
+            return gains.at[a, pair, h, pl.ds(pl.multiple_of(p_l * g_rows, g_rows), g_rows)]
+        return (gate0, up0, down0)[which - 2].at[pair, rows]
+
+    def team_copy(which, off, arriving=False):
+        return pltpu.make_async_remote_copy(
+            src_ref=source(which, off),
+            dst_ref=place(which, off if arriving else 0),
+            send_sem=team_send.at[which, off],
+            recv_sem=team_recv.at[which, off],
+            device_id=peer(off),
+            device_id_type=MESH,
+        )
+
+    def own_copy(which):
+        return pltpu.make_async_copy(source(which, 0), place(which, 0), local_sem.at[which])
+
+    def tok_copy(which, from_off, to_off, sem):
+        whole = (toks, grads)[which]
+        held = (tok_ref, grad_ref)[which] if sem < 6 and sem != 3 else whole.at[number(from_off)]
+        return pltpu.make_async_remote_copy(
+            src_ref=held,
+            dst_ref=whole.at[number(from_off)],
+            send_sem=tok_send.at[which, sem],
+            recv_sem=tok_recv.at[which, sem],
+            device_id=peer(to_off),
+            device_id_type=MESH,
+        )
+
+    def forward(which, off):
+        return tok_copy(which, off, 2, off + 2)
+
+    def region(which, ra, rh):
+        if which == 0:
+            return slab.at[ra, :, rh]
+        return gains.at[ra, :, rh]
+
+    def h_copy(which, arriving=False):
+        if which >= 2:
+            src, dst = ((gate0, gate_h), (up0, up_h))[which - 2]
+        else:
+            src = region(which, a, h)
+            dst = region(which, a, 1 - h if arriving else h)
+        return pltpu.make_async_remote_copy(
+            src_ref=src,
+            dst_ref=dst,
+            send_sem=h_send.at[which],
+            recv_sem=h_recv.at[which],
+            device_id=h_peer,
+            device_id_type=MESH,
+        )
+
+    def a_copy(which, step, arriving=False):
+        if which >= 4:
+            src = (gate0, up0, down0, gate_h)[which - 4]
+            dst = (gate_a, up_a, down_a, gate_far)[which - 4].at[step - 1]
+        else:
+            rh = h if which < 2 else 1 - h
+            src = region(which % 2, a, rh)
+            dst = region(which % 2, lax.rem(a + n_a - step, n_a) if arriving else a, rh)
+        return pltpu.make_async_remote_copy(
+            src_ref=src,
+            dst_ref=dst,
+            send_sem=a_send.at[which, step - 1],
+            recv_sem=a_recv.at[which, step - 1],
+            device_id=a_peer(step),
+            device_id_type=MESH,
+        )
+
+    def team_arrived(which):
+        own_copy(which).wait()
+        for off in range(1, 8):
+            team_copy(which, off, arriving=True).wait_recv()
+
+    away = (4, 1, 5)
+    steps = range(1, n_a)
+
+    def team_start(*which):
+        for w in which:
+            for off in range(1, 8):
+                team_copy(w, off).start()
+            own_copy(w).start()
+
+    def a_start(*which):
+        for w in which:
+            for step in steps:
+                a_copy(w, step).start()
+
+    team_start(0, 1)
+    own_toks = [
+        pltpu.make_async_copy(src, dst.at[number(0)], local_sem.at[5 + n])
+        for n, (src, dst) in enumerate(((tok_ref, toks), (grad_ref, grads)))
+    ]
+    for which in (0, 1):
+        own_toks[which].start()
+        tok_copy(which, 0, 2, 2).start()
+    team_arrived(0)
+    team_arrived(1)
+    h_copy(0).start()
+    h_copy(1).start()
+    a_start(0, 1)
+    team_start(2, 3)
+    team_arrived(2)
+    a_start(4)
+    for off in away:
+        tok_copy(0, 0, off, off).start()
+    team_arrived(3)
+    a_start(5)
+    team_start(4)
+    for which in (0, 1):
+        h_copy(which, arriving=True).wait_recv()
+    h_copy(2).start()
+    a_start(2, 3)
+    for off in away:
+        tok_copy(0, off, off, off).wait_recv()
+        forward(0, off).start()
+    for off in away:
+        tok_copy(1, 0, off, off).start()
+    team_arrived(4)
+    a_start(6)
+    h_copy(2).wait_recv()
+    h_copy(3).start()
+    a_start(7)
+    for off in away:
+        tok_copy(1, off, off, off).wait_recv()
+        forward(1, off).start()
+    for which in (0, 1):
+        own_toks[which].wait()
+        tok_copy(which, 2, 2, 2).wait_recv()
+        for off in away:
+            tok_copy(which, off + 2, 2, off + 2).wait_recv()
+    for which in range(8):
+        for step in steps:
+            a_copy(which, step, arriving=True).wait_recv()
+            a_copy(which, step).wait_send()
+    h_copy(3).wait_recv()
+    for which in range(4):
+        h_copy(which).wait_send()
+    for which in range(5):
+        for off in range(1, 8):
+            team_copy(which, off).wait_send()
+    for which in (0, 1):
+        for off in (2,) + away:
+            tok_copy(which, 0, off, off).wait_send()
+        for off in away:
+            forward(which, off).wait_send()
+
+
+def opening_call(packed, grad_out, qkv_local, gain_tile, gate, up, down):
+    n_a, n_h = lax.axis_size("a"), lax.axis_size("h")
+    rows = gate.shape[0]
+    q_wide, f_wide = qkv_local.shape[1] // 8, gate.shape[1] // 8
+    anywhere = pl.BlockSpec(memory_space=pl.ANY)
+    piece = (4, 2 * rows, f_wide)
+    shapes = [
+        (8,) + packed.shape,
+        (8,) + grad_out.shape,
+        (n_a, 4, n_h, 2 * rows, q_wide),
+        (n_a, 4, n_h, 2 * gain_tile.shape[0], 128),
+        piece,
+        piece,
+        (n_a - 1,) + piece,
+        (n_a - 1,) + piece,
+        piece,
+        piece,
+        (n_a - 1,) + piece,
+        piece,
+        (n_a - 1,) + piece,
+    ]
+    dma = pltpu.SemaphoreType.DMA
+    return pl.pallas_call(
+        opening_kernel,
+        in_specs=[anywhere] * 7,
+        out_specs=[anywhere] * 13,
+        out_shape=[jax.ShapeDtypeStruct(shape, BF) for shape in shapes],
+        scratch_shapes=[
+            dma((5, 8)),
+            dma((5, 8)),
+            dma((2, 8)),
+            dma((2, 8)),
+            dma((7,)),
+            dma((4,)),
+            dma((4,)),
+            dma((8, n_a - 1)),
+            dma((8, n_a - 1)),
+        ],
+        compiler_params=pltpu.CompilerParams(
+            collective_id=1, has_side_effects=True, vmem_limit_bytes=8 * 2**20
+        ),
+        cost_estimate=pl.CostEstimate(flops=0, bytes_accessed=300 * 2**20, transcendentals=0),
+    )(packed, grad_out, qkv_local, gain_tile, gate, up, down)
 
 
 def norm_parts(value):
@@ -511,101 +853,121 @@
     rows = w_gate.shape[0]
     h, l = lax.axis_index("h"), lax.axis_index("l")
     half = 2 * slots
+    q_width = SHARE * SIZE
     own_slot = (h * 2 + l) * slots + jnp.arange(slots, dtype=jnp.int32)
     valid = (own_slot < lengths[0])[:, None]
     own = inputs[0]
     grad_out = jnp.where(valid, out_grad[0], jnp.zeros((), BF))
 
-    gains = lax.all_gather(jnp.stack([attn_gain, ffn_gain]), EVERY, axis=1, tiled=True).astype(F32)
-    attn_gain_full, ffn_gain_full = gains[0], gains[1]
-    team_inputs = lax.all_gather(own, TEAM, axis=0, tiled=True)
-    team_positions = lax.all_gather(positions[0], TEAM, axis=0, tiled=True)
-    team_lengths = lax.all_gather(lengths, ("b", "c"), axis=0, tiled=True)
-    w_qkv = gather_slices(
-        jnp.concatenate([slices_of(w, rows) for w in (w_query, w_key, w_value)], axis=-1)
-    )
-    cosine, sine = rope_tables(team_positions)
-
-    team_f = team_inputs.astype(F32)
-    normed_attn = (team_f * norm_parts(team_f) * attn_gain_full).astype(BF)
-    qkv = dot(normed_attn, w_qkv, NN)
-    q_width = SHARE * SIZE
-    tokens = qkv.shape[0]
-    query = rotate(
-        qkv[:, :q_width].reshape(tokens, SHARE, SIZE), cosine[:, None], sine[:, None]
-    ).astype(BF)
-    query = query.reshape(4, half, q_width)
-    keys = rotate(qkv[:, q_width : q_width + SIZE], cosine, sine).astype(BF).reshape(4, half, SIZE)
-    values = qkv[:, q_width + SIZE :].astype(BF).reshape(4, half, SIZE)
-    early = lax.ppermute(jnp.stack([keys, values]), "h", [(0, 1)])
-    attention_in = (query, keys, values, early[0], early[1])
+    numbers = jnp.stack([positions[0], jnp.broadcast_to(lengths, (slots,))], axis=-1)
+    digits = jnp.concatenate([numbers // 128, numbers % 128], axis=-1).astype(BF)
+    packed = jnp.concatenate([own, jnp.pad(digits, ((0, 0), (0, 124)))], axis=-1)
+    gain_tile = jnp.pad(jnp.stack([attn_gain, ffn_gain]), ((0, 0), (0, 64 - rows)))
+    gain_tile = jnp.broadcast_to(gain_tile.reshape(1, 128), (16, 128))
+    qkv_local = jnp.concatenate(
+        [w.reshape(rows, 8, -1) for w in (w_query, w_key, w_value)], axis=-1
+    ).reshape(rows, -1)
+    (
+        team_packed,
+        team_grad,
+        slab,
+        gains,
+        gate0,
+        gate_h,
+        gate_a,
+        gate_far,
+        up0,
+        up_h,
+        up_a,
+        down0,
+        down_a,
+    ) = opening_call(packed, grad_out, qkv_local, gain_tile, w_gate, w_up, w_down)
+    slab, w_output = together(slab, w_output)
+    w_out = lax.all_gather(w_output, EVERY, axis=0, tiled=True)
+    steps = range(1, lax.axis_size("a"))
+    w_qkv = slab.reshape(width, V_END)
+    gains = gains.reshape(-1, 16, 128)[:, 0].astype(F32)
+    attn_gain_full = gains[:, :rows].reshape(1, width)
+    ffn_gain_full = gains[:, 64 : 64 + rows].reshape(1, width)
+    down_h = shift(down0, "h", 1)
+    up_far = [shift(up_h, "a", s) for s in steps]
+
+    tokens = 8 * slots
+    digits = team_packed[:, :, width : width + 4].reshape(tokens, 4).astype(jnp.int32)
+    cosine, sine = rope_lanes(*rope_tables(digits[:, 0] * 128 + digits[:, 2]))
+    team_lengths = (digits[:, 1] * 128 + digits[:, 3])[::half]
+    normed_attn, qkv = project_call(team_packed, attn_gain_full, w_qkv, cosine, sine)
+    qkv = qkv.reshape(4, half, V_END)
+    early = lax.ppermute(qkv[:, :, Q_END:], "h", [(0, 1)])
     late = h.astype(jnp.int32).reshape(1)
     attended = attention_call(
-        forward_kernel, late, team_lengths, attention_in, [(q_width, BF)], 3 * 10**9
+        forward_kernel, late, team_lengths, (qkv, early), [(q_width, BF)], 3 * 10**9
     )[0]
+    attended, down_h = together(attended, down_h)
+    down_far = [shift(down_h, "a", s) for s in steps]
     attended = lax.all_to_all(attended.reshape(8, slots, q_width), TEAM, 0, 0, tiled=True)
     attended = attended.transpose(1, 0, 2).reshape(slots, HEADS * SIZE)
 
-    w_out = lax.all_gather(w_output, EVERY, axis=0, tiled=True)
     hidden = own.astype(F32) + dot(attended, w_out, NN)
     normed_ffn = (hidden * norm_parts(hidden) * ffn_gain_full).astype(BF)
 
-    team_grad = lax.all_gather(grad_out, TEAM, axis=0, tiled=True)
-    gate_w = gather_slices(slices_of(w_gate, rows))
-    up_w = gather_slices(slices_of(w_up, rows))
-    down_w = gather_slices(slices_of(w_down, rows))
-    grad_nffn, down_part, gate_dw, up_dw, down_dw = ffn_call(
-        normed_ffn, team_grad.reshape(8, slots, width), gate_w, up_w, down_w
-    )
-    down_out = relative_scatter(down_part.reshape(2, 2, 2, slots, width))
-    output = jnp.where(valid, hidden + down_out, 0.0).astype(BF)
-    gate_grad = scatter_slices(gate_dw, rows).reshape(rows, -1)
-    up_grad = scatter_slices(up_dw, rows).reshape(rows, -1)
-    down_grad = scatter_slices(down_dw, rows).reshape(rows, -1)
+    pieces = [gate0, gate_a, gate_h, gate_far]
+    pieces += [up0, up_a, up_h, jnp.stack(up_far)]
+    pieces += [down0, down_a, down_h, jnp.stack(down_far)]
+    grad_nffn, down_part, gate_dw, up_dw, down_dw = ffn_call(normed_ffn, team_grad, pieces)
+    gate_sum = fold_a(gate_dw, rows)
 
     grad_hidden, hat = norm_back(hidden, ffn_gain_full, grad_nffn)
     grad_hidden = grad_hidden + grad_out.astype(F32)
     ffn_gain_term = jnp.sum(grad_nffn * hat, axis=0)
 
     grad_branch = grad_hidden.astype(BF)
-    output_grad = rows_scatter(dot(attended, grad_branch, TN), rows)
     grad_attended = dot(grad_branch, w_out, NT).astype(BF)
     grad_heads = lax.all_to_all(
         grad_attended.reshape(slots, 8, q_width).transpose(1, 0, 2), TEAM, 0, 0, tiled=True
     ).reshape(4, half, q_width)
-    grad_query, grad_keys, grad_values, grad_ek, grad_ev = attention_call(
+    grad_heads, gate_sum, up_dw, down_part = together(grad_heads, gate_sum, up_dw, down_part)
+    up_sum = fold_a(up_dw, rows)
+    gate_sum = scatter_step(gate_sum, "h", 1)
+    output_grad = rows_scatter(dot(attended, grad_branch, TN), rows)
+    grad_own, grad_early = attention_call(
         backward_kernel,
         late,
         team_lengths,
-        attention_in + (grad_heads,),
-        [(q_width, F32), (SIZE, F32), (SIZE, F32), (SIZE, BF), (SIZE, BF)],
+        (qkv, early, grad_heads),
+        [(V_END, F32), (2 * SIZE, BF)],
         8 * 10**9,
     )
-    back = lax.ppermute(jnp.stack([grad_ek, grad_ev]), "h", [(1, 0)]).astype(F32)
-    grad_q = rotate_back(
-        grad_query.reshape(tokens, SHARE, SIZE), cosine[:, None], sine[:, None]
-    ).reshape(tokens, q_width)
-    grad_k = rotate_back((grad_keys + back[0]).reshape(tokens, SIZE), cosine, sine)
-    grad_v = (grad_values + back[1]).reshape(tokens, SIZE)
-    grad_qkv = jnp.concatenate([grad_q, grad_k, grad_v], axis=-1).astype(BF)
+    back = lax.ppermute(grad_early, "h", [(1, 0)])
+    back, up_sum, down_dw, gate_sum = together(back, up_sum, down_dw, gate_sum)
+    down_sum = fold_a(down_dw, rows)
+    up_sum = scatter_step(up_sum, "h", 1)
+    grad_qkv = unrotate_call(
+        grad_own.reshape(tokens, V_END), back.reshape(tokens, 2 * SIZE), cosine, sine
+    )
     partial = dot(grad_qkv, w_qkv, NT)
-    attn_gain_term = jnp.sum(partial * (team_f * norm_parts(team_f)), axis=0)
+    grad_nattn = team_scatter(partial)
+    grad_input, _ = norm_back(own.astype(F32), attn_gain_full, grad_nattn)
+    input_grad = (grad_hidden + grad_input).astype(BF)
+    attn_gain_term = jnp.sum(partial * normed_attn.astype(F32), axis=0) / attn_gain_full[0]
     extra = jnp.stack([attn_gain_term, ffn_gain_term], axis=-1)
     extra = jnp.pad(extra, ((0, 0), (0, 126)))
     slab = jnp.concatenate([dot(normed_attn, grad_qkv, TN), extra], axis=-1)
-    qkv_grad = scatter_slices(slab, rows)
-    grad_nattn = team_scatter(partial)
-    grad_input, _ = norm_back(own.astype(F32), attn_gain_full, grad_nattn)
-    input_grad = (grad_hidden + grad_input).astype(BF)
-    q_end, k_end, v_end = q_width, q_width + SIZE, q_width + 2 * SIZE
-    gain_grads = jnp.sum(qkv_grad[:, :, v_end : v_end + 2], axis=1)
+    qkv_grad = fold_team(scatter_step(fold_a(slab, rows), "h", 1), rows)
+    gain_grads = jnp.sum(qkv_grad[:, :, V_END : V_END + 2], axis=1)
+    down_out = relative_scatter(down_part.reshape(2, 2, 2, slots, width))
+    output = jnp.where(valid, hidden + down_out, 0.0).astype(BF)
+    down_sum = scatter_step(down_sum, "h", 1)
+    gate_grad, up_grad, down_grad = (
+        fold_team(x, rows).reshape(rows, -1) for x in (gate_sum, up_sum, down_sum)
+    )
     return (
         output[None],
         input_grad[None],
         gain_grads[:, 0],
-        qkv_grad[:, :, :q_end].reshape(rows, -1),
-        qkv_grad[:, :, q_end:k_end].reshape(rows, -1),
-        qkv_grad[:, :, k_end:v_end].reshape(rows, -1),
+        qkv_grad[:, :, :Q_END].reshape(rows, -1),
+        qkv_grad[:, :, Q_END:K_END].reshape(rows, -1),
+        qkv_grad[:, :, K_END:V_END].reshape(rows, -1),
         output_grad,
         gain_grads[:, 1],
         gate_grad,

time: 1100 us -> 926 us (0.84)
  Pallas kernels: 160 us -> 377 us
  waiting for transfers between devices: 410 us -> 212 us
  blocking collectives: 97.5 us -> 0 us
  local copies, waits for them, and re-layouts: 161 us -> 109 us
  starting transfers between devices: 126 us -> 102 us
  other arithmetic: 88.9 us -> 66.3 us
    pallas_call x1 -> x4, Pallas kernels: 108 us -> 325 us  [the longest x1 198 us: opening_call(): pl.pallas_call(opening_kernel, in_specs=[anywhere] * 7, out_specs=[anywhe...]
    ppermute x35 -> x26, waiting for transfers between devices: 283 us -> 144 us  [shift(): return lax.ppermute(value, axis, [(i, (i + step) % n) for i in range(n)])]
    all_gather x2 -> x0, blocking collectives: 93.2 us -> none  [the longest x1 79.8 us: local(): lax.all_gather(jnp.stack([attn_gain, ffn_gain]), EVERY, axis=1, tiled=True)]
    ppermute x2, waiting for transfers between devices: 64.8 us -> 16 us  [the longest x1 9.63 us: local(): early = lax.ppermute(qkv[:, :, Q_END:], 'h', [(0, 1)])]
    dynamic_update_slice x16 -> x0, local copies, waits for them, and re-layouts: 25.8 us -> none  [gather_slices(): lax.dynamic_update_slice(whole, block.reshape(1, 4, 1, 2 * rows, width),...]
    all_to_all x8 -> x4, waiting for transfers between devices: 54.4 us -> 33.7 us  [fold_team(): lax.all_to_all(view.reshape(8, rows, view.shape[-1]).astype(BF), TEAM, 0,...]
    all_to_all x1, waiting for transfers between devices: 0.01 us -> 18.6 us  [local(): lax.all_to_all(attended.reshape(8, slots, q_width), TEAM, 0, 0, tiled=True)]
    all_to_all x8 -> x4, starting transfers between devices: 34.5 us -> 17.9 us  [fold_team(): lax.all_to_all(view.reshape(8, rows, view.shape[-1]).astype(BF), TEAM, 0,...]
  transfers between devices with their start and end apart: 50 -> 35, of which waited for: 23 -> 17; matrix products, arithmetic and copies ran while one was open for 23% -> 18% of each run, Pallas kernels for 5% -> 8%
where the time goes in v3:
time: 926 us; the launch traced here: 918 us
  Pallas kernels  377 us (41%)
  waiting for transfers between devices  212 us (23%)
  local copies, waits for them, and re-layouts  109 us (12%)
  starting transfers between devices  102 us (11%)
  other arithmetic  66.3 us (7%)
  matrix products  35.8 us (4%)
  between operations  16.3 us (2%)
    pallas_call x1, Pallas kernels, opening_call(): pl.pallas_call(opening_kernel, in_specs=[anywhere] * 7, out_specs=[anywhe...  198 us
    ppermute x26, waiting for transfers between devices, shift(): return lax.ppermute(value, axis, [(i, (i + step) % n) for i in range(n)])  144 us
    pallas_call x1, Pallas kernels, ffn_call(): pl.pallas_call(ffn_kernel, in_specs=[anywhere] * (2 + len(pieces)), out_s...  108 us
    pallas_call x2, Pallas kernels, attention_call(): pl.pallas_call(kernel, grid_spec=pltpu.PrefetchScalarGridSpec(num_scalar_...  51.5 us
    all_to_all x1, starting transfers between devices, local(): lax.all_to_all(attended.reshape(8, slots, q_width), TEAM, 0, 0, tiled=True)  43.7 us
    unnamed x118, local copies, waits for them, and re-layouts  38.7 us
    dot_general x5, matrix products, dot(): lax.dot_general(a, b, ((over[0], over[1]), ((), ())), preferred_element_t...  35.8 us
    all_to_all x4, waiting for transfers between devices, fold_team(): lax.all_to_all(view.reshape(8, rows, view.shape[-1]).astype(BF), TEAM, 0,...  33.7 us
  transfers between devices with their start and end apart: 35, of which 17 were waited for; matrix products, arithmetic and copies ran while one was open for 18% of the time, Pallas kernels for 8%

profile of v3, /device:TPU:0, one launch (start us, length us, event | category | flops | bytes accessed | tf_op | source)
XLA Modules:
  0.0 918.2 jit_solution(6319603224309709438)
XLA Ops:
  14.1 197.5 %shard_map.212 = (bf16[8,256,2176]{2,1,0:T(8,128)(2,1)S(1)}, bf16[8,256,2048]{2,1,0:T(8,128)(2,1)S(1)}, bf16[2,4,2,128,384]{4,3,2,1,0:T(8,128)(2,1)S(1)}, bf16[2...) custom-call(bf16[256,2176]{1,0:T(8,128)(2,1)S(1)} %fusion.18.tok_ref, ...), custom_call_target="tpu_custom_call" | custom-call | bytes 314572800 | tf_op jit(solution)/shard_map/pallas_call | solution.py:803
  211.6 3.5 copy-done.2
  215.1 3.3 copy-done.9
  227.6 2.5 fusion.47
  234.0 4.1 negate_select_fusion
  239.3 13.7 %shard_map.213 = (bf16[2048,2048]{1,0:T(8,128)(2,1)}, bf16[2048,384]{1,0:T(8,128)(2,1)S(1)}) custom-call(bf16[8,256,2176]{2,1,0:T(8,128)(2,1)} %copy-done.2, f32[1,2048]{1,0:T(1,128)S(1)} %reshape.236.gain_ref, bf16[2048,384]{1,0:T(8,128)(2,1)S(1)} %bitcast.221, f32[2048,256]{1,0:T(8,128)S(1)} %get-tuple-element.103.cos_ref, ...), custom_call_target="tpu_custom_call" | custom-call | flops 3221225472 | bytes 25165824 | tf_op jit(solution)/shard_map/pallas_call | solution.py:170
  255.1 5.1 collective-permute-start
  262.1 9.6 %collective-permute-done.early_ref = bf16[4,512,128]{2,1,0:T(8,128)(2,1)S(1)} collective-permute-done((bf16[4,512,128]{2,1,0:T(8,128)(2,1)}, bf16[4,512,128]{2,1,0:T(8,128)(2,1)S(1)}, u32[]{:S(2)}, u32[]{:S(2)}) %collective-permute-start) | collective-permute-done | bytes 524320 | tf_op jit(solution)/shard_map/ppermute | solution.py:901
  273.2 17.0 %shard_map.214 = bf16[4,512,256]{2,1,0:T(8,128)(2,1)S(1)} custom-call(s32[1]{0:T(128)} %bitcast.2.late_ref, s32[4]{0:T(128)S(1)} %slice.97.length_ref, bf16[4,512,384]{2,1,0:T(8,128)(2,1)S(1)} %bitcast.227, bf16[4,512,128]{2,1,0:T(8,128)(2,1)S(1)} %collective-permute-done.early_ref), custom_call_target="tpu_custom_call" | custom-call | flops 3000000000 | bytes 8388608 | tf_op jit(solution)/shard_map/pallas_call | solution.py:263
  291.5 43.7 %all-to-all-start = ((bf16[8,256,256]{1,2,0:T(8,128)(2,1)}), bf16[8,256,256]{1,2,0:T(8,128)(2,1)}, u32[]{:S(2)}, u32[]{:S(2)}) async-start(bf16[8,256,256]{1,2,0:T(8,128)(2,1)} %copy.91), calls=%async_computation | async-start | bytes 2097152 | tf_op jit(solution)/shard_map/all_to_all | solution.py:908
  339.1 18.6 %all-to-all-done = bf16[8,256,256]{1,2,0:T(8,128)(2,1)} async-done(((bf16[8,256,256]{1,2,0:T(8,128)(2,1)}), bf16[8,256,256]{1,2,0:T(8,128)(2,1)}, u32[]{:S(2)}, u32[]{:S(2)}) %all-to-all-start) | async-done | bytes 1048608 | tf_op jit(solution)/shard_map/all_to_all | solution.py:908
  357.7 6.4 multiply_reduce_fusion.3
  365.7 17.7 %collective-permute-done.3 = bf16[4,128,1024]{2,1,0:T(8,128)(2,1)} collective-permute-done((bf16[4,128,1024]{2,1,0:T(8,128)(2,1)}, bf16[4,128,1024]{2,1,0:T(8,128)(2,1)}, u32[]{:S(2)}, u32[]{:S(2)}) %collective-permute-start.3) | collective-permute-done | bytes 1048608 | tf_op jit(solution)/shard_map/ppermute | solution.py:65
  383.5 108.2 %shard_map.215 = (f32[256,2048]{1,0:T(8,128)}, bf16[8,256,2048]{2,1,0:T(8,128)(2,1)}, bf16[2048,1024]{1,0:T(8,128)(2,1)}, bf16[2048,1024]{1,0:T(8,128)(2,1)}, bf16[2048,1024]{1,0:T(8,128)(2,1)}) custom-call(bf16[256,2048]{1,0:T(8,128)(2,1)} %multiply_convert_fusion.own_ref, bf16[8,256,2048]{2,1,0:T(8,128)(2,1)} %copy-done.9, ...), custom_call_target="tpu_custom_call" | custom-call | flops 77309411328 | bytes 62914560 | tf_op jit(solution)/shard_map/pallas_call | solution.py:535
  491.7 3.3 dynamic-slice_bitcast_fusion.2
  497.8 2.0 copy-done.28
  499.9 2.4 convolution_convert_fusion
  503.3 5.7 all-to-all-start.1
  509.2 10.2 %fusion.28 = f32[2,2,2,2,2,64,2048]{6,5,4,3,2,1,0:T(8,128)} fusion(bf16[2,2,2,2,2,64,256]{6,5,4,3,2,1,0:T(8,128)(2,1)} %bitcast.67, f32[256,2048]{1,0:T(8,128)} %copy-done.26), kind=kOutput, calls=%fused_computation.89 | convolution fusion | flops 2148007936 | bytes 19922944 | tf_op jit(solution)/shard_map/dot_general | solution.py:129
  519.4 23.0 %collective-permute-done.4 = bf16[4,2,128,1024]{3,2,1,0:T(8,128)(2,1)} collective-permute-done((bf16[4,2,128,1024]{3,2,1,0:T(8,128)(2,1)}, bf16[4,2,128,1024]{3,2,1,0:T(8,128)(2,1)}, u32[]{:S(2)}, u32[]{:S(2)}) %collective-permute-start.4) | collective-permute-done | bytes 2097184 | tf_op jit(solution)/shard_map/ppermute | solution.py:65
  542.4 4.5 convert_add_fusion.3
  550.3 6.1 fusion
  557.5 3.3 collective-permute-start.12
  560.8 34.5 %shard_map.216 = (f32[4,512,384]{2,1,0:T(8,128)}, bf16[4,512,128]{2,1,0:T(8,128)(2,1)S(1)}) custom-call(s32[1]{0:T(128)} %bitcast.2.late_ref, s32[4]{0:T(128)S(1)} %slice.97.length_ref, bf16[4,512,384]{2,1,0:T(8,128)(2,1)S(1)} %bitcast.228, bf16[4,512,128]{2,1,0:T(8,128)(2,1)S(1)} %collective-permute-done.early_ref, bf16[4,512,256]{2,1,0:T(8,128)(2,1)S(1)} %bitcast.224), custom_call_target="tpu_custom_call" | custom-call | flops 8000000000 | bytes 8388608 | tf_op jit(solution)/shard_map/pallas_call | solution.py:263
  596.6 4.9 slice_bitcast_fusion
  601.4 17.0 %collective-permute-done.12 = bf16[4,128,1024]{2,1,0:T(8,128)(2,1)S(1)} collective-permute-done((bf16[4,128,1024]{2,1,0:T(8,128)(2,1)S(1)}, bf16[4,128,1024]{2,1,0:T(8,128)(2,1)S(1)}, u32[]{:S(2)}, u32[]{:S(2)}) %collective-permute-start.12) | collective-permute-done | bytes 1048608 | tf_op jit(solution)/shard_map/ppermute | solution.py:65
  619.8 2.9 convert_add_fusion.2
  622.7 6.3 collective-permute-done.10
  631.4 6.0 shard_map.217
  637.4 10.9 %multiply_reduce_fusion = (f32[2048]{0:T(1024)S(1)}, f32[2048,2048]{1,0:T(8,128)}) fusion(bf16[2048,2048]{1,0:T(8,128)(2,1)} %get-tuple-element.75, bf16[2048,384]{1,0:T(8,128)(2,1)} %shard_map.217, bf16[2048,384]{1,0:T(8,128)(2,1)S(1)} %bitcast.222), kind=kOutput, calls=%fused_computation | convolution fusion | flops 3233806336 | bytes 28319744 | tf_op jit(solution)/shard_map/dot_general | solution.py:129
  648.4 5.9 fusion.49
  654.4 2.3 pad_maximum_fusion
  656.6 6.6 reshape.249
  663.2 2.3 constant_dynamic-slice_fusion
  665.5 2.5 copy.114
  669.3 3.6 constant_dynamic-slice_fusion.1
  673.0 2.7 fusion.23
  675.7 4.1 copy.97
  679.8 3.6 all-to-all-start.3
  683.4 5.9 bitcast_add_fusion
  693.0 7.4 collective-permute-done.18
  702.2 6.3 fusion.1
  708.6 10.8 %collective-permute-done.25 = bf16[4,128,1024]{2,1,0:T(8,128)(2,1)S(1)} collective-permute-done((bf16[4,128,1024]{2,1,0:T(8,128)(2,1)}, bf16[4,128,1024]{2,1,0:T(8,128)(2,1)S(1)}, u32[]{:S(2)}, u32[]{:S(2)}) %collective-permute-start.25) | collective-permute-done | bytes 1048608 | tf_op jit(solution)/shard_map/ppermute | solution.py:65
  720.7 9.8 %collective-permute-done.19 = bf16[4,128,512]{2,1,0:T(8,128)(2,1)S(1)} collective-permute-done((bf16[4,128,512]{2,1,0:T(8,128)(2,1)S(1)}, bf16[4,128,512]{2,1,0:T(8,128)(2,1)S(1)}, u32[]{:S(2)}, u32[]{:S(2)}) %collective-permute-start.19) | collective-permute-done | bytes 524320 | tf_op jit(solution)/shard_map/ppermute | solution.py:65
  731.5 3.7 all-to-all-start.2
  737.0 3.4 convert_add_fusion.1
  740.4 2.1 copy-done.30
  743.7 4.5 collective-permute-done.21
  748.2 2.5 bitcast_add_fusion.2
  755.7 3.6 all-to-all-start.4
  759.3 5.4 convert_add_fusion
  775.2 33.6 %all-to-all-done.4 = bf16[8,64,1024]{2,1,0:T(8,128)(2,1)S(1)} async-done(((bf16[8,64,1024]{2,1,0:T(8,128)(2,1)}), bf16[8,64,1024]{2,1,0:T(8,128)(2,1)S(1)}, u32[]{:S(2)}, u32[]{:S(2)}) %all-to-all-start.4) | async-done | bytes 1048608 | tf_op jit(solution)/shard_map/all_to_all | solution.py:99
  812.0 2.6 fusion.16
  814.6 7.1 all-to-all-start.5
  821.7 2.2 bitcast_add_fusion.5
  824.7 10.5 %collective-permute-done.6 = bf16[2,256,1024]{2,1,0:T(8,128)(2,1)} collective-permute-done((bf16[2,256,1024]{2,1,0:T(8,128)(2,1)}, bf16[2,256,1024]{2,1,0:T(8,128)(2,1)}, u32[]{:S(2)}, u32[]{:S(2)}) %collective-permute-start.6) | collective-permute-done | bytes 1048608 | tf_op jit(solution)/shard_map/ppermute | solution.py:65
  835.2 3.5 fusion.13
  838.8 2.3 collective-permute-start.7
  843.6 9.6 %collective-permute-done.7 = bf16[256,1024]{1,0:T(8,128)(2,1)S(1)} collective-permute-done((bf16[256,1024]{1,0:T(8,128)(2,1)S(1)}, bf16[256,1024]{1,0:T(8,128)(2,1)S(1)}, u32[]{:S(2)}, u32[]{:S(2)}) %collective-permute-start.7) | collective-permute-done | bytes 524320 | tf_op jit(solution)/shard_map/ppermute | solution.py:65
  854.4 7.0 collective-permute-done.9
  862.5 5.9 bitcast_add_fusion.1
  874.1 19.2 %collective-permute-done.14 = bf16[2,256,1024]{2,1,0:T(8,128)(2,1)S(1)} collective-permute-done((bf16[2,256,1024]{2,1,0:T(8,128)(2,1)S(1)}, bf16[2,256,1024]{2,1,0:T(8,128)(2,1)S(1)}, u32[]{:S(2)}, u32[]{:S(2)}) %collective-permute-start.14) | collective-permute-done | bytes 1048608 | tf_op jit(solution)/shard_map/ppermute | solution.py:65
  899.6 5.4 collective-permute-done.15
  905.2 2.4 collective-permute-done.17
  (252 shorter events, 97.7 us)
Async XLA Ops:
  7.2 4.9 copy-start.52
  7.2 4.9 copy-start.51
  7.2 5.0 copy-start.41
  7.2 350.5 %all-gather.2.cloned.1.call-start = ((), (), s32[]{:S(2)}) async-start(), calls=%async_computation.6 | async-start | bytes 8650752 | tf_op jit(solution)/shard_map/all_gather | solution.py:886
  211.6 3.5 copy-start.2
  215.1 3.3 copy-start.9
  226.3 63.9 %collective-permute-start.1 = (bf16[4,128,1024]{2,1,0:T(8,128)(2,1)}, bf16[4,128,1024]{2,1,0:T(8,128)(2,1)}, u32[]{:S(2)}, u32[]{:S(2)}) collective-permute-start(bf16[4,128,1024]{2,1,0:T(8,128)(2,1)} %get-tuple-element.50.refs_8_), channel_id=1, source_target_pairs={{0,2},{2,0},{1,3},{3,1},{4,6},{6,4},{5,7},{7,5},{8,10},{10,8},{9,1... | collective-permute-start | bytes 3145736 | tf_op jit(solution)/shard_map/ppermute | solution.py:65
  239.3 13.7 %copy-start = (f32[2048,256]{1,0:T(8,128)}, f32[2048,256]{1,0:T(8,128)S(1)}, u32[]{:S(2)}) copy-start(f32[2048,256]{1,0:T(8,128)S(1)} %get-tuple-element.103.cos_ref) | copy-start | bytes 6291460
  239.3 13.7 %copy-start.1 = (f32[2048,256]{1,0:T(8,128)}, f32[2048,256]{1,0:T(8,128)S(1)}, u32[]{:S(2)}) copy-start(f32[2048,256]{1,0:T(8,128)S(1)} %get-tuple-element.104.sin_ref) | copy-start | bytes 6291460
  255.1 16.7 %collective-permute-start = (bf16[4,512,128]{2,1,0:T(8,128)(2,1)}, bf16[4,512,128]{2,1,0:T(8,128)(2,1)S(1)}, u32[]{:S(2)}, u32[]{:S(2)}) collective-permute-start(bf16[4,512,128]{2,1,0:T(8,128)(2,1)} %slice.128), channel_id=1, source_target_pairs={{0,2},{1,3},{4,6},{5,7},{8,10},{9,11},{12,14},{13,15},{16,18},{17,... | collective-permute-start | bytes 1572872 | tf_op jit(solution)/shard_map/ppermute | solution.py:901
  291.5 43.7 %copy-start.16 = (bf16[4,128,1024]{2,1,0:T(8,128)(2,1)S(1)}, bf16[4,128,1024]{2,1,0:T(8,128)(2,1)}, u32[]{:S(2)}) copy-start(bf16[4,128,1024]{2,1,0:T(8,128)(2,1)} %copy-done.15) | copy-start | bytes 3145732
  291.5 66.2 %all-to-all-start = ((bf16[8,256,256]{1,2,0:T(8,128)(2,1)}), bf16[8,256,256]{1,2,0:T(8,128)(2,1)}, u32[]{:S(2)}, u32[]{:S(2)}) async-start(bf16[8,256,256]{1,2,0:T(8,128)(2,1)} %copy.91), calls=%async_computation | async-start | bytes 2097152 | tf_op jit(solution)/shard_map/all_to_all | solution.py:908
  335.3 30.3 %collective-permute-start.2 = (bf16[4,128,1024]{2,1,0:T(8,128)(2,1)S(1)}, bf16[4,128,1024]{2,1,0:T(8,128)(2,1)}, u32[]{:S(2)}, u32[]{:S(2)}) collective-permute-start(bf16[4,128,1024]{2,1,0:T(8,128)(2,1)S(1)} %copy-done.16), channel_id=1, source_target_pairs={{0,16},{16,0},{1,17},{17,1},{2,18},{18,2},{3,19},{19,3},{4,20},{20... | collective-permute-start | bytes 3145736 | tf_op jit(solution)/shard_map/ppermute | solution.py:65
  338.4 45.0 %collective-permute-start.3 = (bf16[4,128,1024]{2,1,0:T(8,128)(2,1)}, bf16[4,128,1024]{2,1,0:T(8,128)(2,1)}, u32[]{:S(2)}, u32[]{:S(2)}) collective-permute-start(bf16[4,128,1024]{2,1,0:T(8,128)(2,1)} %collective-permute-done.1.refs_10_), channel_id=1, source_target_pairs={{0,16},{16,0},{1,17},{17,1},{2,18},{18,2},{3,19},{19,3},{4,20},{20... | collective-permute-start | bytes 3145736 | tf_op jit(solution)/shard_map/ppermute | solution.py:65
  491.6 4.9 copy-start.20
  491.6 4.9 copy-start.35
  491.6 5.5 copy-start.42
  495.0 47.4 %collective-permute-start.4 = (bf16[4,2,128,1024]{3,2,1,0:T(8,128)(2,1)}, bf16[4,2,128,1024]{3,2,1,0:T(8,128)(2,1)}, u32[]{:S(2)}, u32[]{:S(2)}) collective-permute-start(bf16[4,2,128,1024]{3,2,1,0:T(8,128)(2,1)} %dynamic-slice_bitcast_fusion.2), channel_id=1, source_target_pairs={{0,16},{16,0},{1,17},{17,1},{2,18},{18,2},{3,19},{19,3},{4,20},{20... | collective-permute-start | bytes 6291464 | tf_op jit(solution)/shard_map/ppermute | solution.py:65
  496.5 3.4 copy-start.28
  503.3 43.6 %all-to-all-start.1 = ((bf16[8,256,256]{2,1,0:T(8,128)(2,1)}), bf16[8,256,256]{2,1,0:T(8,128)(2,1)S(1)}, u32[]{:S(2)}, u32[]{:S(2)}) async-start(bf16[8,256,256]{2,1,0:T(8,128)(2,1)} %bitcast.237), calls=%async_computation.1 | async-start | bytes 2097152 | tf_op jit(solution)/shard_map/all_to_all | solution.py:926
  509.2 33.2 %copy-start.45 = (bf16[2048,1024]{1,0:T(8,128)(2,1)S(1)}, bf16[2048,1024]{1,0:T(8,128)(2,1)}, u32[]{:S(2)}) copy-start(bf16[2048,1024]{1,0:T(8,128)(2,1)} %get-tuple-element.64) | copy-start | bytes 12582916
  548.7 8.6 copy-start.33
  548.7 71.1 %collective-permute-start.11 = (bf16[4,2,128,1024]{3,2,1,0:T(8,128)(2,1)S(1)}, bf16[4,2,128,1024]{3,2,1,0:T(8,128)(2,1)S(1)}, u32[]{:S(2)}, u32[]{:S(2)}) collective-permute-start(bf16[4,2,128,1024]{3,2,1,0:T(8,128)(2,1)S(1)} %dynamic-slice_bitcast_fusion.1), channel_id=1, source_target_pairs={{0,16},{16,0},{1,17},{17,1},{2,18},{18,2},{3,19},{19,3},{4,20},{20... | collective-permute-start | bytes 6291464 | tf_op jit(solution)/shard_map/ppermute | solution.py:65
  556.3 4.5 copy-start.8
  556.3 127.1 %collective-permute-start.20 = (bf16[2,2,2,2,64,2048]{5,4,3,2,1,0:T(8,128)(2,1)}, bf16[2,2,2,2,64,2048]{5,4,3,2,1,0:T(8,128)(2,1)}, u32[]{:S(2)}, u32[]{:S(2)}) collective-permute-start(bf16[2,2,2,2,64,2048]{5,4,3,2,1,0:T(8,128)(2,1)} %fusion), channel_id=1, source_target_pairs={{0,4},{4,0},{1,5},{5,1},{2,6},{6,2},{3,7},{7,3},{8,12},{12,8},{9,1... | collective-permute-start | bytes 12582920 | tf_op jit(solution)/shard_map/ppermute | solution.py:65
  557.5 61.0 %collective-permute-start.12 = (bf16[4,128,1024]{2,1,0:T(8,128)(2,1)S(1)}, bf16[4,128,1024]{2,1,0:T(8,128)(2,1)S(1)}, u32[]{:S(2)}, u32[]{:S(2)}) collective-permute-start(bf16[4,128,1024]{2,1,0:T(8,128)(2,1)S(1)} %fusion.19), channel_id=1, source_target_pairs={{0,2},{2,0},{1,3},{3,1},{4,6},{6,4},{5,7},{7,5},{8,10},{10,8},{9,1... | collective-permute-start | bytes 3145736 | tf_op jit(solution)/shard_map/ppermute | solution.py:65
  595.3 33.8 %collective-permute-start.10 = (bf16[4,512,128]{2,1,0:T(8,128)(2,1)S(1)}, bf16[4,512,128]{2,1,0:T(8,128)(2,1)S(1)}, u32[]{:S(2)}, u32[]{:S(2)}) collective-permute-start(bf16[4,512,128]{2,1,0:T(8,128)(2,1)S(1)} %get-tuple-element.70), channel_id=1, source_target_pairs={{2,0},{3,1},{6,4},{7,5},{10,8},{11,9},{14,12},{15,13},{18,16},{19,... | collective-permute-start | bytes 1572872 | tf_op jit(solution)/shard_map/ppermute | solution.py:941
  601.4 18.4 %copy-start.44 = (bf16[2048,1024]{1,0:T(8,128)(2,1)S(1)}, bf16[2048,1024]{1,0:T(8,128)(2,1)}, u32[]{:S(2)}) copy-start(bf16[2048,1024]{1,0:T(8,128)(2,1)} %get-tuple-element.71) | copy-start | bytes 12582916
  601.4 157.9 %collective-permute-start.5 = (bf16[2,2,256,2048]{3,2,1,0:T(8,128)(2,1)}, bf16[2,2,256,2048]{3,2,1,0:T(8,128)(2,1)}, u32[]{:S(2)}, u32[]{:S(2)}) collective-permute-start(bf16[2,2,256,2048]{3,2,1,0:T(8,128)(2,1)} %slice_bitcast_fusion), channel_id=1, source_target_pairs={{0,4},{4,0},{1,5},{5,1},{2,6},{6,2},{3,7},{7,3},{8,12},{12,8},{9,1... | collective-permute-start | bytes 12582920 | tf_op jit(solution)/shard_map/ppermute | solution.py:65
  619.8 9.3 %copy-start.43 = (bf16[2048,1024]{1,0:T(8,128)(2,1)S(1)}, bf16[2048,1024]{1,0:T(8,128)(2,1)}, u32[]{:S(2)}) copy-start(bf16[2048,1024]{1,0:T(8,128)(2,1)} %get-tuple-element.78) | copy-start | bytes 12582916
  630.7 106.3 %collective-permute-start.26 = (bf16[4,2,128,1024]{3,2,1,0:T(8,128)(2,1)}, bf16[4,2,128,1024]{3,2,1,0:T(8,128)(2,1)}, u32[]{:S(2)}, u32[]{:S(2)}) collective-permute-start(bf16[4,2,128,1024]{3,2,1,0:T(8,128)(2,1)} %dynamic-slice_bitcast_fusion), channel_id=1, source_target_pairs={{0,16},{16,0},{1,17},{17,1},{2,18},{18,2},{3,19},{19,3},{4,20},{20... | collective-permute-start | bytes 6291464 | tf_op jit(solution)/shard_map/ppermute | solution.py:65
  637.4 11.1 %copy-start.34 = (bf16[2048,384]{1,0:T(8,128)(2,1)S(1)}, bf16[2048,384]{1,0:T(8,128)(2,1)}, u32[]{:S(2)}) copy-start(bf16[2048,384]{1,0:T(8,128)(2,1)} %shard_map.217) | copy-start | bytes 4718596
  668.0 32.5 %collective-permute-start.18 = (bf16[4,2,128,512]{3,2,0,1:T(8,128)(2,1)}, bf16[4,2,128,512]{3,2,0,1:T(8,128)(2,1)}, u32[]{:S(2)}, u32[]{:S(2)}) collective-permute-start(bf16[4,2,128,512]{3,2,0,1:T(8,128)(2,1)} %bitcast.206), channel_id=1, source_target_pairs={{0,16},{16,0},{1,17},{17,1},{2,18},{18,2},{3,19},{19,3},{4,20},{20... | collective-permute-start | bytes 3145736 | tf_op jit(solution)/shard_map/ppermute | solution.py:65
  675.7 43.6 %collective-permute-start.25 = (bf16[4,128,1024]{2,1,0:T(8,128)(2,1)}, bf16[4,128,1024]{2,1,0:T(8,128)(2,1)S(1)}, u32[]{:S(2)}, u32[]{:S(2)}) collective-permute-start(bf16[4,128,1024]{2,1,0:T(8,128)(2,1)} %fusion.23), channel_id=1, source_target_pairs={{0,2},{2,0},{1,3},{3,1},{4,6},{6,4},{5,7},{7,5},{8,10},{10,8},{9,1... | collective-permute-start | bytes 3145736 | tf_op jit(solution)/shard_map/ppermute | solution.py:65
  679.8 51.6 %all-to-all-start.3 = ((bf16[8,64,1024]{2,1,0:T(8,128)(2,1)}), bf16[8,64,1024]{2,1,0:T(8,128)(2,1)S(1)}, u32[]{:S(2)}, u32[]{:S(2)}) async-start(bf16[8,64,1024]{2,1,0:T(8,128)(2,1)} %bitcast.80), calls=%async_computation.3 | async-start | bytes 2097152 | tf_op jit(solution)/shard_map/all_to_all | solution.py:99
  689.4 19.2 %copy-start.25 = (f32[2,2,2,2,64,2048]{5,4,3,2,1,0:T(8,128)}, f32[2,2,2,2,64,2048]{5,4,3,2,1,0:T(8,128)S(1)}, u32[]{:S(2)}) copy-start(f32[2,2,2,2,64,2048]{5,4,3,2,1,0:T(8,128)S(1)} %bitcast_add_fusion) | copy-start | bytes 25165828
  689.4 11.1 %copy-start.36 = (f32[1,4,2,128,512]{4,3,1,2,0:T(8,128)S(1)}, f32[1,4,2,128,512]{4,3,1,2,0:T(8,128)}, u32[]{:S(2)}) copy-start(f32[1,4,2,128,512]{4,3,1,2,0:T(8,128)} %copy.97) | copy-start | bytes 6291460
  691.0 57.2 %collective-permute-start.21 = (bf16[2,2,2,64,2048]{4,3,2,1,0:T(8,128)(2,1)}, bf16[2,2,2,64,2048]{4,3,2,1,0:T(8,128)(2,1)}, u32[]{:S(2)}, u32[]{:S(2)}) collective-permute-start(bf16[2,2,2,64,2048]{4,3,2,1,0:T(8,128)(2,1)} %fusion.11), channel_id=1, source_target_pairs={{0,8},{8,0},{1,9},{9,1},{2,10},{10,2},{3,11},{11,3},{4,12},{12,4},... | collective-permute-start | bytes 6291464 | tf_op jit(solution)/shard_map/ppermute | solution.py:65
  702.2 28.3 %collective-permute-start.19 = (bf16[4,128,512]{2,1,0:T(8,128)(2,1)S(1)}, bf16[4,128,512]{2,1,0:T(8,128)(2,1)S(1)}, u32[]{:S(2)}, u32[]{:S(2)}) collective-permute-start(bf16[4,128,512]{2,1,0:T(8,128)(2,1)S(1)} %fusion.35), channel_id=1, source_target_pairs={{0,2},{2,0},{1,3},{3,1},{4,6},{6,4},{5,7},{7,5},{8,10},{10,8},{9,1... | collective-permute-start | bytes 1572872 | tf_op jit(solution)/shard_map/ppermute | solution.py:65
  702.2 17.1 %copy-start.29 = (f32[4,2,128,1024]{3,2,1,0:T(8,128)S(1)}, f32[4,2,128,1024]{3,2,1,0:T(8,128)}, u32[]{:S(2)}) copy-start(f32[4,2,128,1024]{3,2,1,0:T(8,128)} %convert_add_fusion.2) | copy-start | bytes 12582916
  719.3 143.2 %collective-permute-start.13 = (bf16[2,2,256,2048]{3,2,1,0:T(8,128)(2,1)}, bf16[2,2,256,2048]{3,2,1,0:T(8,128)(2,1)}, u32[]{:S(2)}, u32[]{:S(2)}) collective-permute-start(bf16[2,2,256,2048]{3,2,1,0:T(8,128)(2,1)} %fusion.1), channel_id=1, source_target_pairs={{0,4},{4,0},{1,5},{5,1},{2,6},{6,2},{3,7},{7,3},{8,12},{12,8},{9,1... | collective-permute-start | bytes 12582920 | tf_op jit(solution)/shard_map/ppermute | solution.py:65
  731.5 24.3 %all-to-all-start.2 = ((bf16[8,64,512]{2,1,0:T(8,128)(2,1)}), bf16[8,64,512]{2,1,0:T(8,128)(2,1)S(1)}, u32[]{:S(2)}, u32[]{:S(2)}) async-start(bf16[8,64,512]{2,1,0:T(8,128)(2,1)} %bitcast.63), calls=%async_computation.2 | async-start | bytes 1048576 | tf_op jit(solution)/shard_map/all_to_all | solution.py:99
  735.2 13.0 %slice-start = ((s8[8388608]{0:T(1024)(128)(4,1)}), s8[4194304]{0:T(1024)(128)(4,1)S(1)}, s32[]{:S(2)}) async-start(s8[8388608]{0:T(1024)(128)(4,1)} %bitcast.233), calls=%async_computation.7 | async-start | bytes 8388608
  737.0 11.3 %slice-start.1 = ((s8[8388608]{0:T(1024)(128)(4,1)}), s8[4194304]{0:T(1024)(128)(4,1)S(1)}, s32[]{:S(2)}) async-start(s8[8388608]{0:T(1024)(128)(4,1)} %bitcast.233), calls=%async_computation.8 | async-start | bytes 8388608
  743.7 66.9 %collective-permute-start.27 = (bf16[4,128,1024]{2,1,0:T(8,128)(2,1)}, bf16[4,128,1024]{2,1,0:T(8,128)(2,1)}, u32[]{:S(2)}, u32[]{:S(2)}) collective-permute-start(bf16[4,128,1024]{2,1,0:T(8,128)(2,1)} %fusion.24), channel_id=1, source_target_pairs={{0,2},{2,0},{1,3},{3,1},{4,6},{6,4},{5,7},{7,5},{8,10},{10,8},{9,1... | collective-permute-start | bytes 3145736 | tf_op jit(solution)/shard_map/ppermute | solution.py:65
  753.8 67.9 %collective-permute-start.22 = (bf16[2,2,64,2048]{3,2,1,0:T(8,128)(2,1)}, bf16[2,2,64,2048]{3,2,1,0:T(8,128)(2,1)}, u32[]{:S(2)}, u32[]{:S(2)}) collective-permute-start(bf16[2,2,64,2048]{3,2,1,0:T(8,128)(2,1)} %fusion.22), channel_id=1, source_target_pairs={{0,1},{1,0},{2,3},{3,2},{4,5},{5,4},{6,7},{7,6},{8,9},{9,8},{10,11... | collective-permute-start | bytes 3145736 | tf_op jit(solution)/shard_map/ppermute | solution.py:65
  755.7 53.1 %all-to-all-start.4 = ((bf16[8,64,1024]{2,1,0:T(8,128)(2,1)}), bf16[8,64,1024]{2,1,0:T(8,128)(2,1)S(1)}, u32[]{:S(2)}, u32[]{:S(2)}) async-start(bf16[8,64,1024]{2,1,0:T(8,128)(2,1)} %bitcast.84), calls=%async_computation.4 | async-start | bytes 2097152 | tf_op jit(solution)/shard_map/all_to_all | solution.py:99
  764.7 3.7 copy-start.24
  766.0 69.2 %collective-permute-start.6 = (bf16[2,256,1024]{2,1,0:T(8,128)(2,1)}, bf16[2,256,1024]{2,1,0:T(8,128)(2,1)}, u32[]{:S(2)}, u32[]{:S(2)}) collective-permute-start(bf16[2,256,1024]{2,1,0:T(8,128)(2,1)} %slice_bitcast_fusion.7), channel_id=1, source_target_pairs={{0,1},{1,0},{2,3},{3,2},{4,5},{5,4},{6,7},{7,6},{8,9},{9,8},{10,11... | collective-permute-start | bytes 3145736 | tf_op jit(solution)/shard_map/ppermute | solution.py:65
  769.5 65.7 %collective-permute-start.8 = (bf16[2,256,1024]{2,1,0:T(8,128)(2,1)}, bf16[2,256,1024]{2,1,0:T(8,128)(2,1)}, u32[]{:S(2)}, u32[]{:S(2)}) collective-permute-start(bf16[2,256,1024]{2,1,0:T(8,128)(2,1)} %slice_bitcast_fusion.5), channel_id=1, source_target_pairs={{0,8},{8,0},{1,9},{9,1},{2,10},{10,2},{3,11},{11,3},{4,12},{12,4},... | collective-permute-start | bytes 3145736 | tf_op jit(solution)/shard_map/ppermute | solution.py:65
  814.6 83.3 %all-to-all-start.5 = ((bf16[8,64,1024]{2,1,0:T(8,128)(2,1)}), bf16[8,64,1024]{2,1,0:T(8,128)(2,1)S(1)}, u32[]{:S(2)}, u32[]{:S(2)}) async-start(bf16[8,64,1024]{2,1,0:T(8,128)(2,1)} %bitcast.91), calls=%async_computation.5 | async-start | bytes 2097152 | tf_op jit(solution)/shard_map/all_to_all | solution.py:99
  824.0 17.3 %collective-permute-start.23 = (bf16[2,64,2048]{2,1,0:T(8,128)(2,1)S(1)}, bf16[2,64,2048]{2,1,0:T(8,128)(2,1)S(1)}, u32[]{:S(2)}, u32[]{:S(2)}) collective-permute-start(bf16[2,64,2048]{2,1,0:T(8,128)(2,1)S(1)} %fusion.36), channel_id=1, source_target_pairs={{0,16},{16,0},{1,17},{17,1},{2,18},{18,2},{3,19},{19,3},{4,20},{20... | collective-permute-start | bytes 1572872 | tf_op jit(solution)/shard_map/ppermute | solution.py:65
  838.8 14.5 %collective-permute-start.7 = (bf16[256,1024]{1,0:T(8,128)(2,1)S(1)}, bf16[256,1024]{1,0:T(8,128)(2,1)S(1)}, u32[]{:S(2)}, u32[]{:S(2)}) collective-permute-start(bf16[256,1024]{1,0:T(8,128)(2,1)S(1)} %fusion.37), channel_id=1, source_target_pairs={{0,8},{8,0},{1,9},{9,1},{2,10},{10,2},{3,11},{11,3},{4,12},{12,4},... | collective-permute-start | bytes 1572872 | tf_op jit(solution)/shard_map/ppermute | solution.py:65
  841.2 20.2 %collective-permute-start.9 = (bf16[256,1024]{1,0:T(8,128)(2,1)S(1)}, bf16[256,1024]{1,0:T(8,128)(2,1)S(1)}, u32[]{:S(2)}, u32[]{:S(2)}) collective-permute-start(bf16[256,1024]{1,0:T(8,128)(2,1)S(1)} %fusion.38), channel_id=1, source_target_pairs={{0,1},{1,0},{2,3},{3,2},{4,5},{5,4},{6,7},{7,6},{8,9},{9,8},{10,11... | collective-permute-start | bytes 1572872 | tf_op jit(solution)/shard_map/ppermute | solution.py:65
  841.4 21.1 %copy-start.48 = (f32[2,64,2048]{2,1,0:T(8,128)}, f32[2,64,2048]{2,1,0:T(8,128)S(1)}, u32[]{:S(2)}) copy-start(f32[2,64,2048]{2,1,0:T(8,128)S(1)} %bitcast_add_fusion.10) | copy-start | bytes 3145732
  842.2 31.1 %collective-permute-start.24 = (bf16[64,2048]{1,0:T(8,128)(2,1)}, bf16[64,2048]{1,0:T(8,128)(2,1)S(1)}, u32[]{:S(2)}, u32[]{:S(2)}) collective-permute-start(bf16[64,2048]{1,0:T(8,128)(2,1)} %fusion.41), channel_id=1, source_target_pairs={{0,2},{2,0},{1,3},{3,1},{4,6},{6,4},{5,7},{7,5},{8,10},{10,8},{9,1... | collective-permute-start | bytes 786440 | tf_op jit(solution)/shard_map/ppermute | solution.py:65
  870.0 23.4 %collective-permute-start.14 = (bf16[2,256,1024]{2,1,0:T(8,128)(2,1)S(1)}, bf16[2,256,1024]{2,1,0:T(8,128)(2,1)S(1)}, u32[]{:S(2)}, u32[]{:S(2)}) collective-permute-start(bf16[2,256,1024]{2,1,0:T(8,128)(2,1)S(1)} %fusion.20), channel_id=1, source_target_pairs={{0,1},{1,0},{2,3},{3,2},{4,5},{5,4},{6,7},{7,6},{8,9},{9,8},{10,11... | collective-permute-start | bytes 3145736 | tf_op jit(solution)/shard_map/ppermute | solution.py:65
  870.2 3.1 copy-start.49
  870.2 24.1 %collective-permute-start.16 = (bf16[2,256,1024]{2,1,0:T(8,128)(2,1)S(1)}, bf16[2,256,1024]{2,1,0:T(8,128)(2,1)S(1)}, u32[]{:S(2)}, u32[]{:S(2)}) collective-permute-start(bf16[2,256,1024]{2,1,0:T(8,128)(2,1)S(1)} %fusion.21), channel_id=1, source_target_pairs={{0,8},{8,0},{1,9},{9,1},{2,10},{10,2},{3,11},{11,3},{4,12},{12,4},... | collective-permute-start | bytes 3145736 | tf_op jit(solution)/shard_map/ppermute | solution.py:65
  893.8 11.2 %collective-permute-start.15 = (bf16[256,1024]{1,0:T(8,128)(2,1)S(1)}, bf16[256,1024]{1,0:T(8,128)(2,1)S(1)}, u32[]{:S(2)}, u32[]{:S(2)}) collective-permute-start(bf16[256,1024]{1,0:T(8,128)(2,1)S(1)} %fusion.33), channel_id=1, source_target_pairs={{0,8},{8,0},{1,9},{9,1},{2,10},{10,2},{3,11},{11,3},{4,12},{12,4},... | collective-permute-start | bytes 1572872 | tf_op jit(solution)/shard_map/ppermute | solution.py:65
  896.4 11.2 %collective-permute-start.17 = (bf16[256,1024]{1,0:T(8,128)(2,1)S(1)}, bf16[256,1024]{1,0:T(8,128)(2,1)S(1)}, u32[]{:S(2)}, u32[]{:S(2)}) collective-permute-start(bf16[256,1024]{1,0:T(8,128)(2,1)S(1)} %fusion.34), channel_id=1, source_target_pairs={{0,1},{1,0},{2,3},{3,2},{4,5},{5,4},{6,7},{7,6},{8,9},{9,8},{10,11... | collective-permute-start | bytes 1572872 | tf_op jit(solution)/shard_map/ppermute | solution.py:65
  898.2 6.8 copy-start.38
  898.2 9.4 %copy-start.40 = (f32[2,256,1024]{2,1,0:T(8,128)S(1)}, f32[2,256,1024]{2,1,0:T(8,128)}, u32[]{:S(2)}) copy-start(f32[2,256,1024]{2,1,0:T(8,128)} %copy-done.39) | copy-start | bytes 6291460
  899.6 8.1 copy-start.23
  (26 other events, 40.5 us)
Sparse Core Ops, SparseCore 0:
  226.4 125.2 all-gather.1

commit v4 on v3

--- a/solution.py
+++ b/solution.py
@@ -65,13 +65,20 @@
     return lax.ppermute(value, axis, [(i, (i + step) % n) for i in range(n)])
 
 
-def scatter_step(value, axis, dim):
+def after(value, earlier):
+    return lax.optimization_barrier((value, earlier))[0]
+
+
+def scatter_step(value, axis, dim, pin=None):
     n = lax.axis_size(axis)
     me = lax.axis_index(axis)
     kept = lax.dynamic_index_in_dim(value, me, dim, keepdims=False).astype(F32)
     for s in range(1, n):
         sent = lax.dynamic_index_in_dim(value, lax.rem(me + s, n), dim, keepdims=False)
-        kept = kept + shift(sent.astype(BF), axis, s).astype(F32)
+        arrived = shift(sent.astype(BF), axis, s)
+        if pin is not None:
+            arrived = after(arrived, pin)
+        kept = kept + arrived.astype(F32)
     return kept
 
 
@@ -90,9 +97,9 @@
     return lax.optimization_barrier(values)
 
 
-def fold_a(partial, rows):
+def fold_a(partial, rows, pin=None):
     view = partial.reshape(lax.axis_size("a"), 4, lax.axis_size("h"), 2 * rows, partial.shape[-1])
-    return scatter_step(view, "a", 0)
+    return scatter_step(view, "a", 0, pin)
 
 
 def fold_team(view, rows):
@@ -102,27 +109,13 @@
     return owned.transpose(1, 0, 2).astype(F32)
 
 
-def relative_scatter(partial):
-    half = partial.shape[-1] // 2
-
-    def fold(value, axis, dim):
-        kept = lax.index_in_dim(value, 0, dim, keepdims=False).astype(F32)
-        sent = lax.index_in_dim(value, 1, dim, keepdims=False).astype(BF)
-        return kept + shift(sent, axis, 1).astype(F32)
-
-    view = fold(partial, "c", 2)
-    left = fold(fold(view[..., :half], "l", 0), "b", 0)
-    right = fold(fold(view[..., half:], "b", 1), "l", 0)
-    return jnp.concatenate([left, right], axis=-1)
-
-
-def rows_scatter(partial, rows):
-    view = partial.reshape(lax.axis_size("a"), 2, 2, lax.axis_size("h"), 2, rows, -1)
-    view = scatter_step(view, "c", 2)
-    view = scatter_step(view, "b", 1)
-    view = scatter_step(view, "l", 2)
-    view = scatter_step(view, "a", 0)
-    return scatter_step(view, "h", 0)
+def fold(value, axis, dim, pin=None):
+    kept = lax.index_in_dim(value, 0, dim, keepdims=False).astype(F32)
+    sent = lax.index_in_dim(value, 1, dim, keepdims=False).astype(BF)
+    arrived = shift(sent, axis, 1)
+    if pin is not None:
+        arrived = after(arrived, pin)
+    return kept + arrived.astype(F32)
 
 
 def dot(a, b, over):
@@ -662,6 +655,31 @@
     def forward(which, off):
         return tok_copy(which, off, 2, off + 2)
 
+    def diagonal(which, half, arriving=False):
+        whole = (toks, grads)[which]
+        rows = whole.shape[1] // 2
+        owner, to, sem = ((4, 1, 5), (1, 4, 0))[half]
+        spot = pl.ds(half * rows, rows)
+        return pltpu.make_async_remote_copy(
+            src_ref=whole.at[number(owner), spot],
+            dst_ref=whole.at[number(5 if arriving else owner), spot],
+            send_sem=tok_send.at[which, sem],
+            recv_sem=tok_recv.at[which, sem],
+            device_id=peer(to),
+            device_id_type=MESH,
+        )
+
+    def hand_on(which):
+        for half, off in enumerate((4, 1)):
+            tok_copy(which, off, off, off).wait_recv()
+            diagonal(which, half).start()
+            forward(which, off).start()
+
+    def diagonal_arrived(which):
+        for half in (0, 1):
+            diagonal(which, half, arriving=True).wait_recv()
+        forward(which, 5).start()
+
     def region(which, ra, rh):
         if which == 0:
             return slab.at[ra, :, rh]
@@ -734,7 +752,7 @@
     team_start(2, 3)
     team_arrived(2)
     a_start(4)
-    for off in away:
+    for off in (4, 1):
         tok_copy(0, 0, off, off).start()
     team_arrived(3)
     a_start(5)
@@ -743,19 +761,17 @@
         h_copy(which, arriving=True).wait_recv()
     h_copy(2).start()
     a_start(2, 3)
-    for off in away:
-        tok_copy(0, off, off, off).wait_recv()
-        forward(0, off).start()
-    for off in away:
+    hand_on(0)
+    for off in (4, 1):
         tok_copy(1, 0, off, off).start()
+    diagonal_arrived(0)
     team_arrived(4)
     a_start(6)
     h_copy(2).wait_recv()
     h_copy(3).start()
     a_start(7)
-    for off in away:
-        tok_copy(1, off, off, off).wait_recv()
-        forward(1, off).start()
+    hand_on(1)
+    diagonal_arrived(1)
     for which in (0, 1):
         own_toks[which].wait()
         tok_copy(which, 2, 2, 2).wait_recv()
@@ -772,8 +788,10 @@
         for off in range(1, 8):
             team_copy(which, off).wait_send()
     for which in (0, 1):
-        for off in (2,) + away:
+        for off in (2, 4, 1):
             tok_copy(which, 0, off, off).wait_send()
+        for half in (0, 1):
+            diagonal(which, half).wait_send()
         for off in away:
             forward(which, off).wait_send()
 
@@ -915,7 +933,7 @@
     pieces += [up0, up_a, up_h, jnp.stack(up_far)]
     pieces += [down0, down_a, down_h, jnp.stack(down_far)]
     grad_nffn, down_part, gate_dw, up_dw, down_dw = ffn_call(normed_ffn, team_grad, pieces)
-    gate_sum = fold_a(gate_dw, rows)
+    down_view = down_part.reshape(2, 2, 2, slots, width)
 
     grad_hidden, hat = norm_back(hidden, ffn_gain_full, grad_nffn)
     grad_hidden = grad_hidden + grad_out.astype(F32)
@@ -926,10 +944,9 @@
     grad_heads = lax.all_to_all(
         grad_attended.reshape(slots, 8, q_width).transpose(1, 0, 2), TEAM, 0, 0, tiled=True
     ).reshape(4, half, q_width)
-    grad_heads, gate_sum, up_dw, down_part = together(grad_heads, gate_sum, up_dw, down_part)
-    up_sum = fold_a(up_dw, rows)
-    gate_sum = scatter_step(gate_sum, "h", 1)
-    output_grad = rows_scatter(dot(attended, grad_branch, TN), rows)
+    down_view = fold(down_view, "c", 2)
+    output_part = dot(attended, grad_branch, TN).astype(BF)
+    grad_heads, down_view, output_part = together(grad_heads, down_view, output_part)
     grad_own, grad_early = attention_call(
         backward_kernel,
         late,
@@ -938,26 +955,48 @@
         [(V_END, F32), (2 * SIZE, BF)],
         8 * 10**9,
     )
+    down_left = fold(down_view[..., : width // 2], "l", 0, grad_own)
+    down_right = fold(down_view[..., width // 2 :], "b", 1, grad_own)
+    gate_sum = fold_a(gate_dw, rows, grad_own)
     back = lax.ppermute(grad_early, "h", [(1, 0)])
-    back, up_sum, down_dw, gate_sum = together(back, up_sum, down_dw, gate_sum)
-    down_sum = fold_a(down_dw, rows)
-    up_sum = scatter_step(up_sum, "h", 1)
     grad_qkv = unrotate_call(
         grad_own.reshape(tokens, V_END), back.reshape(tokens, 2 * SIZE), cosine, sine
     )
+    n_a, n_h = lax.axis_size("a"), lax.axis_size("h")
+    output_view = output_part.reshape(n_a, 2, 2, n_h, 2, rows, -1)
+    output_view = scatter_step(output_view, "c", 2, grad_own)
+    gate_sum = scatter_step(after(gate_sum, back), "h", 1, grad_qkv)
+    up_sum = fold_a(up_dw, rows, grad_qkv)
     partial = dot(grad_qkv, w_qkv, NT)
-    grad_nattn = team_scatter(partial)
+    partial_view = scatter_step(partial.reshape(2, 2, 2, slots, width), "c", 1)
+    attn_gain_term = jnp.sum(partial * normed_attn.astype(F32), axis=0) / attn_gain_full[0]
+    terms = jnp.pad(jnp.stack([attn_gain_term, ffn_gain_term]), ((0, 6), (0, 0)))
+    extra = lax.dot_general(
+        terms, jnp.eye(8, 128, dtype=F32), ((TN[0], TN[1]), ((), ())), precision=lax.Precision.HIGHEST
+    )
+    slab = jnp.concatenate([dot(normed_attn, grad_qkv, TN), extra], axis=-1).astype(BF)
+    slab, partial_view, up_sum = together(slab, partial_view, up_sum)
+    left = scatter_step(partial_view[..., : width // 2], "l", 1, slab)
+    right = scatter_step(partial_view[..., width // 2 :], "b", 0, slab)
+    down_left = fold(down_left, "b", 0, left)
+    down_right = fold(down_right, "l", 0, left)
+    up_sum = scatter_step(up_sum, "h", 1, left)
+    down_sum = fold_a(down_dw, rows, left)
+    output_view = scatter_step(output_view, "b", 1, left)
+    left = scatter_step(left, "b", 0)
+    right = scatter_step(right, "l", 0)
+    grad_nattn = jnp.concatenate([left, right], axis=-1)
     grad_input, _ = norm_back(own.astype(F32), attn_gain_full, grad_nattn)
     input_grad = (grad_hidden + grad_input).astype(BF)
-    attn_gain_term = jnp.sum(partial * normed_attn.astype(F32), axis=0) / attn_gain_full[0]
-    extra = jnp.stack([attn_gain_term, ffn_gain_term], axis=-1)
-    extra = jnp.pad(extra, ((0, 0), (0, 126)))
-    slab = jnp.concatenate([dot(normed_attn, grad_qkv, TN), extra], axis=-1)
-    qkv_grad = fold_team(scatter_step(fold_a(slab, rows), "h", 1), rows)
+    down_sum = scatter_step(down_sum, "h", 1)
+    qkv_sum = scatter_step(fold_a(slab, rows, left), "h", 1)
+    output_view = scatter_step(output_view, "l", 2)
+    output_view = scatter_step(output_view, "a", 0)
+    output_grad = scatter_step(output_view, "h", 0)
+    down_out = jnp.concatenate([down_left, down_right], axis=-1)
+    output = jnp.where(valid, hidden + down_out, 0.0).astype(BF)
+    qkv_grad = fold_team(qkv_sum, rows)
     gain_grads = jnp.sum(qkv_grad[:, :, V_END : V_END + 2], axis=1)
-    down_out = relative_scatter(down_part.reshape(2, 2, 2, slots, width))
-    output = jnp.where(valid, hidden + down_out, 0.0).astype(BF)
-    down_sum = scatter_step(down_sum, "h", 1)
     gate_grad, up_grad, down_grad = (
         fold_team(x, rows).reshape(rows, -1) for x in (gate_sum, up_sum, down_sum)
     )

time: 926 us -> 897 us (0.969)
  waiting for transfers between devices: 212 us -> 183 us
  Pallas kernels: 377 us -> 353 us
  local copies, waits for them, and re-layouts: 109 us -> 119 us
    all_to_all x4, waiting for transfers between devices: 33.7 us -> 2.57 us  [fold_team(): lax.all_to_all(view.reshape(8, rows, view.shape[-1]).astype(BF), TEAM, 0,...]
    ppermute x26, waiting for transfers between devices: 144 us -> 114 us  [shift(): return lax.ppermute(value, axis, [(i, (i + step) % n) for i in range(n)])]
    ppermute x1, waiting for transfers between devices: 6.32 us -> 36.2 us  [local(): back = lax.ppermute(grad_early, 'h', [(1, 0)])]
    pallas_call x1, Pallas kernels: 198 us -> 174 us  [opening_call(): pl.pallas_call(opening_kernel, in_specs=[anywhere] * 7, out_specs=[anywhe...]
    ppermute x26, starting transfers between devices: 27.8 us -> 41.3 us  [shift(): return lax.ppermute(value, axis, [(i, (i + step) % n) for i in range(n)])]
    unnamed x118 -> x130, local copies, waits for them, and re-layouts: 38.7 us -> 44.9 us
    convert_element_type x14 -> x13, local copies, waits for them, and re-layouts: 20.7 us -> 15.1 us  [scatter_step(): arrived = shift(sent.astype(BF), axis, s)]
    add x19 -> x18, other arithmetic: 43.4 us -> 45.7 us  [the longest x14 33.6 us: scatter_step(): kept = kept + arrived.astype(F32)]
  transfers between devices with their start and end apart: 35 -> 35, of which waited for: 17 -> 13; matrix products, arithmetic and copies ran while one was open for 18% -> 20% of each run, Pallas kernels for 8% -> 8%
where the time goes in v4:
time: 897 us; the launch traced here: 890 us
  Pallas kernels  353 us (39%)
  waiting for transfers between devices  183 us (20%)
  local copies, waits for them, and re-layouts  119 us (13%)
  starting transfers between devices  111 us (12%)
  other arithmetic  73.2 us (8%)
  matrix products  35.1 us (4%)
  between operations  16 us (2%)
    pallas_call x1, Pallas kernels, opening_call(): pl.pallas_call(opening_kernel, in_specs=[anywhere] * 7, out_specs=[anywhe...  174 us
    ppermute x26, waiting for transfers between devices, shift(): return lax.ppermute(value, axis, [(i, (i + step) % n) for i in range(n)])  114 us
    pallas_call x1, Pallas kernels, ffn_call(): pl.pallas_call(ffn_kernel, in_specs=[anywhere] * (2 + len(pieces)), out_s...  108 us
    pallas_call x2, Pallas kernels, attention_call(): pl.pallas_call(kernel, grid_spec=pltpu.PrefetchScalarGridSpec(num_scalar_...  51.5 us
    all_to_all x1, starting transfers between devices, local(): lax.all_to_all(attended.reshape(8, slots, q_width), TEAM, 0, 0, tiled=True)  44.9 us
    unnamed x130, local copies, waits for them, and re-layouts  44.9 us
    ppermute x26, starting transfers between devices, shift(): return lax.ppermute(value, axis, [(i, (i + step) % n) for i in range(n)])  41.3 us
    ppermute x1, waiting for transfers between devices, local(): back = lax.ppermute(grad_early, 'h', [(1, 0)])  36.2 us
  transfers between devices with their start and end apart: 35, of which 13 were waited for; matrix products, arithmetic and copies ran while one was open for 20% of the time, Pallas kernels for 8%

profile of v4, /device:TPU:0, one launch (start us, length us, event | category | flops | bytes accessed | tf_op | source)
XLA Modules:
  0.0 889.6 jit_solution(4716821423783705559)
XLA Ops:
  14.8 174.4 %shard_map.212 = (bf16[8,256,2176]{2,1,0:T(8,128)(2,1)S(1)}, bf16[8,256,2048]{2,1,0:T(8,128)(2,1)S(1)}, bf16[2,4,2,128,384]{4,3,2,1,0:T(8,128)(2,1)S(1)}, bf16[2...) custom-call(bf16[256,2176]{1,0:T(8,128)(2,1)S(1)} %fusion.16.tok_ref, ...), custom_call_target="tpu_custom_call" | custom-call | bytes 314572800 | tf_op jit(solution)/shard_map/pallas_call | solution.py:821
  189.2 3.5 copy-done.2
  192.7 3.3 copy-done.11
  207.2 2.5 fusion.51
  213.3 4.1 negate_select_fusion
  218.7 13.7 %shard_map.213 = (bf16[2048,2048]{1,0:T(8,128)(2,1)}, bf16[2048,384]{1,0:T(8,128)(2,1)S(1)}) custom-call(bf16[8,256,2176]{2,1,0:T(8,128)(2,1)} %copy-done.2, f32[1,2048]{1,0:T(1,128)S(1)} %reshape.239.gain_ref, bf16[2048,384]{1,0:T(8,128)(2,1)S(1)} %bitcast.214, f32[2048,256]{1,0:T(8,128)S(1)} %get-tuple-element.133.cos_ref, ...), custom_call_target="tpu_custom_call" | custom-call | flops 3221225472 | bytes 25165824 | tf_op jit(solution)/shard_map/pallas_call | solution.py:163
  234.5 3.6 collective-permute-start
  240.0 9.4 %collective-permute-done.early_ref = bf16[4,512,128]{2,1,0:T(8,128)(2,1)S(1)} collective-permute-done((bf16[4,512,128]{2,1,0:T(8,128)(2,1)}, bf16[4,512,128]{2,1,0:T(8,128)(2,1)S(1)}, u32[]{:S(2)}, u32[]{:S(2)}) %collective-permute-start) | collective-permute-done | bytes 524320 | tf_op jit(solution)/shard_map/ppermute | solution.py:919
  250.9 17.0 %shard_map.214 = bf16[4,512,256]{2,1,0:T(8,128)(2,1)S(1)} custom-call(s32[1]{0:T(128)} %bitcast.2.late_ref, s32[4]{0:T(128)S(1)} %slice.97.length_ref, bf16[4,512,384]{2,1,0:T(8,128)(2,1)S(1)} %bitcast.220, bf16[4,512,128]{2,1,0:T(8,128)(2,1)S(1)} %collective-permute-done.early_ref), custom_call_target="tpu_custom_call" | custom-call | flops 3000000000 | bytes 8388608 | tf_op jit(solution)/shard_map/pallas_call | solution.py:256
  269.2 44.9 %all-to-all-start = ((bf16[8,256,256]{1,2,0:T(8,128)(2,1)}), bf16[8,256,256]{1,2,0:T(8,128)(2,1)}, u32[]{:S(2)}, u32[]{:S(2)}) async-start(bf16[8,256,256]{1,2,0:T(8,128)(2,1)} %copy.99), calls=%async_computation | async-start | bytes 2097152 | tf_op jit(solution)/shard_map/all_to_all | solution.py:926
  316.3 20.7 %all-to-all-done = bf16[8,256,256]{1,2,0:T(8,128)(2,1)} async-done(((bf16[8,256,256]{1,2,0:T(8,128)(2,1)}), bf16[8,256,256]{1,2,0:T(8,128)(2,1)}, u32[]{:S(2)}, u32[]{:S(2)}) %all-to-all-start) | async-done | bytes 1048608 | tf_op jit(solution)/shard_map/all_to_all | solution.py:926
  337.0 6.4 multiply_reduce_fusion.3
  345.0 17.3 %collective-permute-done.3 = bf16[4,128,1024]{2,1,0:T(8,128)(2,1)} collective-permute-done((bf16[4,128,1024]{2,1,0:T(8,128)(2,1)}, bf16[4,128,1024]{2,1,0:T(8,128)(2,1)}, u32[]{:S(2)}, u32[]{:S(2)}) %collective-permute-start.3) | collective-permute-done | bytes 1048608 | tf_op jit(solution)/shard_map/ppermute | solution.py:65
  362.3 107.7 %shard_map.215 = (f32[256,2048]{1,0:T(8,128)}, bf16[8,256,2048]{2,1,0:T(8,128)(2,1)}, bf16[2048,1024]{1,0:T(8,128)(2,1)}, bf16[2048,1024]{1,0:T(8,128)(2,1)}, bf16[2048,1024]{1,0:T(8,128)(2,1)}) custom-call(bf16[256,2048]{1,0:T(8,128)(2,1)} %multiply_convert_fusion.own_ref, bf16[8,256,2048]{2,1,0:T(8,128)(2,1)} %copy-done.11, ...), custom_call_target="tpu_custom_call" | custom-call | flops 77309411328 | bytes 62914560 | tf_op jit(solution)/shard_map/pallas_call | solution.py:528
  470.0 4.8 slice_bitcast_fusion
  477.1 3.0 multiply_reduce_fusion.1
  481.2 6.5 convolution_convert_fusion.2
  488.8 4.4 all-to-all-start.1
  494.7 3.2 dynamic-slice_bitcast_fusion.1
  499.7 7.1 convolution_convert_fusion
  508.6 7.2 convert_add_fusion.1
  517.2 34.5 %shard_map.216 = (f32[4,512,384]{2,1,0:T(8,128)}, bf16[4,512,128]{2,1,0:T(8,128)(2,1)S(1)}) custom-call(s32[1]{0:T(128)} %bitcast.2.late_ref, s32[4]{0:T(128)S(1)} %slice.97.length_ref, bf16[4,512,384]{2,1,0:T(8,128)(2,1)S(1)} %bitcast.221, bf16[4,512,128]{2,1,0:T(8,128)(2,1)S(1)} %collective-permute-done.early_ref, bf16[4,512,256]{2,1,0:T(8,128)(2,1)S(1)} %bitcast.217), custom_call_target="tpu_custom_call" | custom-call | flops 8000000000 | bytes 8388608 | tf_op jit(solution)/shard_map/pallas_call | solution.py:256
  553.0 6.7 constant_dynamic-slice_fusion.1
  563.4 2.5 convert_add_fusion.3
  565.9 36.2 %collective-permute-done.7 = bf16[4,512,128]{2,1,0:T(8,128)(2,1)S(1)} collective-permute-done((bf16[4,512,128]{2,1,0:T(8,128)(2,1)S(1)}, bf16[4,512,128]{2,1,0:T(8,128)(2,1)S(1)}, u32[]{:S(2)}, u32[]{:S(2)}) %collective-permute-start.7) | collective-permute-done | bytes 524320 | tf_op jit(solution)/shard_map/ppermute | solution.py:961
  603.3 5.8 shard_map.217
  609.1 7.6 multiply_reduce_fusion
  616.7 2.8 fusion
  623.9 3.3 copy-done.21
  627.2 2.7 slice_bitcast_fusion.5
  630.0 2.7 slice_bitcast_fusion.3
  634.4 2.6 fusion.15
  637.0 4.2 all-to-all-start.3
  641.1 6.9 convolution_convert_fusion.1
  653.3 4.5 convert_add_fusion.4
  657.8 5.9 collective-permute-done.11
  663.8 3.5 bitcast_add_fusion.9
  668.2 3.0 collective-permute-start.12
  675.5 5.9 bitcast_add_fusion
  681.4 3.0 fusion.49
  684.4 4.3 fusion.21
  688.7 2.9 collective-permute-start.25
  693.3 4.0 convert_add_fusion
  697.2 3.3 copy-done.27
  702.2 4.6 reshape.251
  706.8 3.0 constant_dynamic-slice_fusion.3
  709.8 2.5 copy.123
  716.5 15.8 %collective-permute-done.10 = bf16[2,256,1024]{2,1,0:T(8,128)(2,1)} collective-permute-done((bf16[2,256,1024]{2,1,0:T(8,128)(2,1)}, bf16[2,256,1024]{2,1,0:T(8,128)(2,1)}, u32[]{:S(2)}, u32[]{:S(2)}) %collective-permute-start.10) | collective-permute-done | bytes 1048608 | tf_op jit(solution)/shard_map/ppermute | solution.py:65
  736.6 2.7 fusion.14
  741.1 3.6 all-to-all-start.4
  746.6 3.3 convert_add_fusion.2
  752.1 8.3 collective-permute-done.14
  762.2 4.3 collective-permute-start.15
  769.1 38.5 %collective-permute-done.19 = bf16[2,2,2,64,2048]{4,3,1,0,2:T(8,128)(2,1)} collective-permute-done((bf16[2,2,2,64,2048]{4,3,1,0,2:T(8,128)(2,1)}, bf16[2,2,2,64,2048]{4,3,1,0,2:T(8,128)(2,1)}, u32[]{:S(2)}, u32[]{:S(2)}) %collective-permute-start.19) | collective-permute-done | bytes 2097184 | tf_op jit(solution)/shard_map/ppermute | solution.py:65
  807.7 2.5 bitcast_add_fusion.1
  813.2 2.8 collective-permute-done.13
  817.9 4.1 collective-permute-start.17
  825.3 11.7 %collective-permute-done.17 = bf16[4,128,512]{2,1,0:T(8,128)(2,1)S(1)} collective-permute-done((bf16[4,128,512]{2,1,0:T(8,128)(2,1)S(1)}, bf16[4,128,512]{2,1,0:T(8,128)(2,1)S(1)}, u32[]{:S(2)}, u32[]{:S(2)}) %collective-permute-start.17) | collective-permute-done | bytes 524320 | tf_op jit(solution)/shard_map/ppermute | solution.py:65
  839.2 4.3 all-to-all-start.2
  850.2 2.6 all-to-all-done.2
  852.8 3.6 all-to-all-start.5
  856.5 4.9 collective-permute-done.21
  864.3 2.6 collective-permute-start.22
  870.5 8.5 collective-permute-done.22
  (264 shorter events, 116.2 us)
Async XLA Ops:
  7.2 5.6 copy-start.25
  7.2 329.8 %all-gather.2.cloned.1.call-start = ((), (), s32[]{:S(2)}) async-start(), calls=%async_computation.6 | async-start | bytes 8650752 | tf_op jit(solution)/shard_map/all_gather | solution.py:904
  203.9 64.0 %collective-permute-start.1 = (bf16[4,128,1024]{2,1,0:T(8,128)(2,1)}, bf16[4,128,1024]{2,1,0:T(8,128)(2,1)}, u32[]{:S(2)}, u32[]{:S(2)}) collective-permute-start(bf16[4,128,1024]{2,1,0:T(8,128)(2,1)} %get-tuple-element.63.refs_8_), channel_id=1, source_target_pairs={{0,2},{2,0},{1,3},{3,1},{4,6},{6,4},{5,7},{7,5},{8,10},{10,8},{9,1... | collective-permute-start | bytes 3145736 | tf_op jit(solution)/shard_map/ppermute | solution.py:65
  206.0 12.7 %copy-start.9 = (f32[1,2048]{1,0:T(1,128)}, f32[1,2048]{1,0:T(1,128)S(1)}, u32[]{:S(2)}) copy-start(f32[1,2048]{1,0:T(1,128)S(1)} %reshape.239.gain_ref) | copy-start | bytes 24580
  218.7 13.7 %copy-start = (f32[2048,256]{1,0:T(8,128)}, f32[2048,256]{1,0:T(8,128)S(1)}, u32[]{:S(2)}) copy-start(f32[2048,256]{1,0:T(8,128)S(1)} %get-tuple-element.133.cos_ref) | copy-start | bytes 6291460
  218.7 13.7 %copy-start.1 = (f32[2048,256]{1,0:T(8,128)}, f32[2048,256]{1,0:T(8,128)S(1)}, u32[]{:S(2)}) copy-start(f32[2048,256]{1,0:T(8,128)S(1)} %get-tuple-element.134.sin_ref) | copy-start | bytes 6291460
  234.5 15.0 %collective-permute-start = (bf16[4,512,128]{2,1,0:T(8,128)(2,1)}, bf16[4,512,128]{2,1,0:T(8,128)(2,1)S(1)}, u32[]{:S(2)}, u32[]{:S(2)}) collective-permute-start(bf16[4,512,128]{2,1,0:T(8,128)(2,1)} %slice.128), channel_id=1, source_target_pairs={{0,2},{1,3},{4,6},{5,7},{8,10},{9,11},{12,14},{13,15},{16,18},{17,... | collective-permute-start | bytes 1572872 | tf_op jit(solution)/shard_map/ppermute | solution.py:919
  269.2 44.9 %copy-start.18 = (bf16[4,128,1024]{2,1,0:T(8,128)(2,1)S(1)}, bf16[4,128,1024]{2,1,0:T(8,128)(2,1)}, u32[]{:S(2)}) copy-start(bf16[4,128,1024]{2,1,0:T(8,128)(2,1)} %copy-done.17) | copy-start | bytes 3145732
  269.2 67.8 %all-to-all-start = ((bf16[8,256,256]{1,2,0:T(8,128)(2,1)}), bf16[8,256,256]{1,2,0:T(8,128)(2,1)}, u32[]{:S(2)}, u32[]{:S(2)}) async-start(bf16[8,256,256]{1,2,0:T(8,128)(2,1)} %copy.99), calls=%async_computation | async-start | bytes 2097152 | tf_op jit(solution)/shard_map/all_to_all | solution.py:926
  314.2 30.6 %collective-permute-start.2 = (bf16[4,128,1024]{2,1,0:T(8,128)(2,1)S(1)}, bf16[4,128,1024]{2,1,0:T(8,128)(2,1)}, u32[]{:S(2)}, u32[]{:S(2)}) collective-permute-start(bf16[4,128,1024]{2,1,0:T(8,128)(2,1)S(1)} %copy-done.18), channel_id=1, source_target_pairs={{0,16},{16,0},{1,17},{17,1},{2,18},{18,2},{3,19},{19,3},{4,20},{20... | collective-permute-start | bytes 3145736 | tf_op jit(solution)/shard_map/ppermute | solution.py:65
  315.2 47.1 %collective-permute-start.3 = (bf16[4,128,1024]{2,1,0:T(8,128)(2,1)}, bf16[4,128,1024]{2,1,0:T(8,128)(2,1)}, u32[]{:S(2)}, u32[]{:S(2)}) collective-permute-start(bf16[4,128,1024]{2,1,0:T(8,128)(2,1)} %collective-permute-done.1.refs_10_), channel_id=1, source_target_pairs={{0,16},{16,0},{1,17},{17,1},{2,18},{18,2},{3,19},{19,3},{4,20},{20... | collective-permute-start | bytes 3145736 | tf_op jit(solution)/shard_map/ppermute | solution.py:65
  470.0 10.0 %copy-start.49 = (bf16[1,256,2048]{2,1,0:T(8,128)(2,1)S(1)}, bf16[1,256,2048]{2,1,0:T(8,128)(2,1)}, u32[]{:S(2)}) copy-start(bf16[1,256,2048]{2,1,0:T(8,128)(2,1)} %param.25) | copy-start | bytes 3145732
  474.9 33.7 %collective-permute-start.4 = (bf16[2,2,256,2048]{3,2,1,0:T(8,128)(2,1)}, bf16[2,2,256,2048]{3,2,1,0:T(8,128)(2,1)}, u32[]{:S(2)}, u32[]{:S(2)}) collective-permute-start(bf16[2,2,256,2048]{3,2,1,0:T(8,128)(2,1)} %slice_bitcast_fusion), channel_id=1, source_target_pairs={{0,4},{4,0},{1,5},{5,1},{2,6},{6,2},{3,7},{7,3},{8,12},{12,8},{9,1... | collective-permute-start | bytes 12582920 | tf_op jit(solution)/shard_map/ppermute | solution.py:65
  481.2 6.5 copy-start.28
  488.8 27.1 %all-to-all-start.1 = ((bf16[8,256,256]{2,1,0:T(8,128)(2,1)}), bf16[8,256,256]{2,1,0:T(8,128)(2,1)S(1)}, u32[]{:S(2)}, u32[]{:S(2)}) async-start(bf16[8,256,256]{2,1,0:T(8,128)(2,1)} %bitcast.234), calls=%async_computation.1 | async-start | bytes 2097152 | tf_op jit(solution)/shard_map/all_to_all | solution.py:944
  494.6 5.1 copy-start.29
  494.7 13.9 %slice-start.2 = ((s8[8388608]{0:T(1024)(128)(4,1)}), s8[4194304]{0:T(1024)(128)(4,1)S(1)}, s32[]{:S(2)}) async-start(s8[8388608]{0:T(1024)(128)(4,1)} %bitcast.230), calls=%async_computation.9 | async-start | bytes 8388608
  497.9 9.0 %copy-start.51 = (bf16[2048,1024]{1,0:T(8,128)(2,1)S(1)}, bf16[2048,1024]{1,0:T(8,128)(2,1)}, u32[]{:S(2)}) copy-start(bf16[2048,1024]{1,0:T(8,128)(2,1)} %get-tuple-element.84) | copy-start | bytes 12582916
  497.9 10.7 %slice-start.3 = ((s8[8388608]{0:T(1024)(128)(4,1)}), s8[4194304]{0:T(1024)(128)(4,1)S(1)}, s32[]{:S(2)}) async-start(s8[8388608]{0:T(1024)(128)(4,1)} %bitcast.230), calls=%async_computation.10 | async-start | bytes 8388608
  497.9 61.8 %collective-permute-start.23 = (bf16[4,2,128,1024]{3,2,1,0:T(8,128)(2,1)}, bf16[4,2,128,1024]{3,2,1,0:T(8,128)(2,1)}, u32[]{:S(2)}, u32[]{:S(2)}) collective-permute-start(bf16[4,2,128,1024]{3,2,1,0:T(8,128)(2,1)} %dynamic-slice_bitcast_fusion.1), channel_id=1, source_target_pairs={{0,16},{16,0},{1,17},{17,1},{2,18},{18,2},{3,19},{19,3},{4,20},{20... | collective-permute-start | bytes 6291464 | tf_op jit(solution)/shard_map/ppermute | solution.py:65
  508.5 139.5 %collective-permute-start.9 = (bf16[4,2,128,1024]{3,2,1,0:T(8,128)(2,1)}, bf16[4,2,128,1024]{3,2,1,0:T(8,128)(2,1)}, u32[]{:S(2)}, u32[]{:S(2)}) collective-permute-start(bf16[4,2,128,1024]{3,2,1,0:T(8,128)(2,1)} %dynamic-slice_bitcast_fusion.2), channel_id=1, source_target_pairs={{0,16},{16,0},{1,17},{17,1},{2,18},{18,2},{3,19},{19,3},{4,20},{20... | collective-permute-start | bytes 6291464 | tf_op jit(solution)/shard_map/ppermute | solution.py:65
  551.7 50.4 %collective-permute-start.7 = (bf16[4,512,128]{2,1,0:T(8,128)(2,1)S(1)}, bf16[4,512,128]{2,1,0:T(8,128)(2,1)S(1)}, u32[]{:S(2)}, u32[]{:S(2)}) collective-permute-start(bf16[4,512,128]{2,1,0:T(8,128)(2,1)S(1)} %get-tuple-element.83), channel_id=1, source_target_pairs={{2,0},{3,1},{6,4},{7,5},{10,8},{11,9},{14,12},{15,13},{18,16},{19,... | collective-permute-start | bytes 1572872 | tf_op jit(solution)/shard_map/ppermute | solution.py:961
  562.2 113.3 %collective-permute-start.18 = (bf16[2,2,2,2,64,2048]{5,4,2,0,3,1:T(8,128)(2,1)}, bf16[2,2,2,2,64,2048]{5,4,2,0,3,1:T(8,128)(2,1)}, u32[]{:S(2)}, u32[]{:S(2)}) collective-permute-start(bf16[2,2,2,2,64,2048]{5,4,2,0,3,1:T(8,128)(2,1)} %bitcast.209), channel_id=1, source_target_pairs={{0,4},{4,0},{1,5},{5,1},{2,6},{6,2},{3,7},{7,3},{8,12},{12,8},{9,1... | collective-permute-start | bytes 12582920 | tf_op jit(solution)/shard_map/ppermute | solution.py:65
  565.9 36.2 %copy-start.34 = (f32[4,2,128,1024]{3,2,1,0:T(8,128)}, f32[4,2,128,1024]{3,2,1,0:T(8,128)S(1)}, u32[]{:S(2)}) copy-start(f32[4,2,128,1024]{3,2,1,0:T(8,128)S(1)} %convert_add_fusion.3) | copy-start | bytes 12582916
  603.3 29.4 %collective-permute-start.24 = (bf16[4,128,1024]{2,1,0:T(8,128)(2,1)}, bf16[4,128,1024]{2,1,0:T(8,128)(2,1)}, u32[]{:S(2)}, u32[]{:S(2)}) collective-permute-start(bf16[4,128,1024]{2,1,0:T(8,128)(2,1)} %fusion.20), channel_id=1, source_target_pairs={{0,2},{2,0},{1,3},{3,1},{4,6},{6,4},{5,7},{7,5},{8,10},{10,8},{9,1... | collective-permute-start | bytes 3145736 | tf_op jit(solution)/shard_map/ppermute | solution.py:65
  616.7 10.5 %copy-start.21 = (f32[2048,2048]{1,0:T(8,128)}, f32[2048,2048]{1,0:T(8,128)S(1)}, u32[]{:S(2)}) copy-start(f32[2048,2048]{1,0:T(8,128)S(1)} %get-tuple-element.132) | copy-start | bytes 50331652
  616.7 5.2 copy-start.50
  619.5 56.0 %collective-permute-start.8 = (bf16[2,2,256,2048]{3,2,1,0:T(8,128)(2,1)}, bf16[2,2,256,2048]{3,2,1,0:T(8,128)(2,1)}, u32[]{:S(2)}, u32[]{:S(2)}) collective-permute-start(bf16[2,2,256,2048]{3,2,1,0:T(8,128)(2,1)} %fusion), channel_id=1, source_target_pairs={{0,4},{4,0},{1,5},{5,1},{2,6},{6,2},{3,7},{7,3},{8,12},{12,8},{9,1... | collective-permute-start | bytes 12582920 | tf_op jit(solution)/shard_map/ppermute | solution.py:65
  622.0 12.4 %copy-start.35 = (f32[4,2,128,1024]{3,2,1,0:T(8,128)S(1)}, f32[4,2,128,1024]{3,2,1,0:T(8,128)}, u32[]{:S(2)}) copy-start(f32[4,2,128,1024]{3,2,1,0:T(8,128)} %copy-done.34) | copy-start | bytes 12582916
  630.0 27.9 %collective-permute-start.5 = (bf16[2,256,1024]{2,1,0:T(8,128)(2,1)}, bf16[2,256,1024]{2,1,0:T(8,128)(2,1)}, u32[]{:S(2)}, u32[]{:S(2)}) collective-permute-start(bf16[2,256,1024]{2,1,0:T(8,128)(2,1)} %slice_bitcast_fusion.5), channel_id=1, source_target_pairs={{0,1},{1,0},{2,3},{3,2},{4,5},{5,4},{6,7},{7,6},{8,9},{9,8},{10,11... | collective-permute-start | bytes 3145736 | tf_op jit(solution)/shard_map/ppermute | solution.py:65
  632.7 31.1 %collective-permute-start.11 = (bf16[2,256,1024]{2,1,0:T(8,128)(2,1)}, bf16[2,256,1024]{2,1,0:T(8,128)(2,1)}, u32[]{:S(2)}, u32[]{:S(2)}) collective-permute-start(bf16[2,256,1024]{2,1,0:T(8,128)(2,1)} %slice_bitcast_fusion.3), channel_id=1, source_target_pairs={{0,8},{8,0},{1,9},{9,1},{2,10},{10,2},{3,11},{11,3},{4,12},{12,4},... | collective-permute-start | bytes 3145736 | tf_op jit(solution)/shard_map/ppermute | solution.py:65
  637.0 36.8 %all-to-all-start.3 = ((bf16[8,64,1024]{2,1,0:T(8,128)(2,1)}), bf16[8,64,1024]{2,1,0:T(8,128)(2,1)S(1)}, u32[]{:S(2)}, u32[]{:S(2)}) async-start(bf16[8,64,1024]{2,1,0:T(8,128)(2,1)} %bitcast.233), calls=%async_computation.3 | async-start | bytes 2097152 | tf_op jit(solution)/shard_map/all_to_all | solution.py:106
  641.1 8.6 copy-start.10
  648.1 91.4 %collective-permute-start.26 = (bf16[4,2,128,1024]{3,2,1,0:T(8,128)(2,1)}, bf16[4,2,128,1024]{3,2,1,0:T(8,128)(2,1)}, u32[]{:S(2)}, u32[]{:S(2)}) collective-permute-start(bf16[4,2,128,1024]{3,2,1,0:T(8,128)(2,1)} %dynamic-slice_bitcast_fusion), channel_id=1, source_target_pairs={{0,16},{16,0},{1,17},{17,1},{2,18},{18,2},{3,19},{19,3},{4,20},{20... | collective-permute-start | bytes 6291464 | tf_op jit(solution)/shard_map/ppermute | solution.py:65
  667.3 4.8 copy-start.42
  668.2 72.9 %collective-permute-start.12 = (bf16[256,1024]{1,0:T(8,128)(2,1)}, bf16[256,1024]{1,0:T(8,128)(2,1)S(1)}, u32[]{:S(2)}, u32[]{:S(2)}) collective-permute-start(bf16[256,1024]{1,0:T(8,128)(2,1)} %fusion.34), channel_id=1, source_target_pairs={{0,1},{1,0},{2,3},{3,2},{4,5},{5,4},{6,7},{7,6},{8,9},{9,8},{10,11... | collective-permute-start | bytes 1572872 | tf_op jit(solution)/shard_map/ppermute | solution.py:65
  672.1 69.0 %collective-permute-start.6 = (bf16[256,1024]{1,0:T(8,128)(2,1)}, bf16[256,1024]{1,0:T(8,128)(2,1)}, u32[]{:S(2)}, u32[]{:S(2)}) collective-permute-start(bf16[256,1024]{1,0:T(8,128)(2,1)} %fusion.33), channel_id=1, source_target_pairs={{0,8},{8,0},{1,9},{9,1},{2,10},{10,2},{3,11},{11,3},{4,12},{12,4},... | collective-permute-start | bytes 1572872 | tf_op jit(solution)/shard_map/ppermute | solution.py:65
  684.4 8.3 copy-start.37
  684.4 8.8 copy-start.31
  688.7 47.3 %collective-permute-start.25 = (bf16[4,128,1024]{2,1,0:T(8,128)(2,1)}, bf16[4,128,1024]{2,1,0:T(8,128)(2,1)}, u32[]{:S(2)}, u32[]{:S(2)}) collective-permute-start(bf16[4,128,1024]{2,1,0:T(8,128)(2,1)} %fusion.21), channel_id=1, source_target_pairs={{0,2},{2,0},{1,3},{3,1},{4,6},{6,4},{5,7},{7,5},{8,10},{10,8},{9,1... | collective-permute-start | bytes 3145736 | tf_op jit(solution)/shard_map/ppermute | solution.py:65
  692.8 39.5 %collective-permute-start.10 = (bf16[2,256,1024]{2,1,0:T(8,128)(2,1)}, bf16[2,256,1024]{2,1,0:T(8,128)(2,1)}, u32[]{:S(2)}, u32[]{:S(2)}) collective-permute-start(bf16[2,256,1024]{2,1,0:T(8,128)(2,1)} %fusion.17), channel_id=1, source_target_pairs={{0,1},{1,0},{2,3},{3,2},{4,5},{5,4},{6,7},{7,6},{8,9},{9,8},{10,11... | collective-permute-start | bytes 3145736 | tf_op jit(solution)/shard_map/ppermute | solution.py:65
  716.5 20.2 %copy-start.32 = (f32[4,2,128,1024]{3,2,1,0:T(8,128)S(1)}, f32[4,2,128,1024]{3,2,1,0:T(8,128)}, u32[]{:S(2)}) copy-start(f32[4,2,128,1024]{3,2,1,0:T(8,128)} %convert_add_fusion.4) | copy-start | bytes 12582916
  732.3 28.1 %collective-permute-start.14 = (bf16[2,256,1024]{2,1,0:T(8,128)(2,1)S(1)}, bf16[2,256,1024]{2,1,0:T(8,128)(2,1)}, u32[]{:S(2)}, u32[]{:S(2)}) collective-permute-start(bf16[2,256,1024]{2,1,0:T(8,128)(2,1)S(1)} %fusion.18), channel_id=1, source_target_pairs={{0,8},{8,0},{1,9},{9,1},{2,10},{10,2},{3,11},{11,3},{4,12},{12,4},... | collective-permute-start | bytes 3145736 | tf_op jit(solution)/shard_map/ppermute | solution.py:65
  736.0 71.6 %collective-permute-start.19 = (bf16[2,2,2,64,2048]{4,3,1,0,2:T(8,128)(2,1)}, bf16[2,2,2,64,2048]{4,3,1,0,2:T(8,128)(2,1)}, u32[]{:S(2)}, u32[]{:S(2)}) collective-permute-start(bf16[2,2,2,64,2048]{4,3,1,0,2:T(8,128)(2,1)} %fusion.10), channel_id=1, source_target_pairs={{0,8},{8,0},{1,9},{9,1},{2,10},{10,2},{3,11},{11,3},{4,12},{12,4},... | collective-permute-start | bytes 6291464 | tf_op jit(solution)/shard_map/ppermute | solution.py:65
  739.4 76.8 %collective-permute-start.16 = (bf16[4,2,128,512]{3,2,0,1:T(8,128)(2,1)}, bf16[4,2,128,512]{3,2,0,1:T(8,128)(2,1)}, u32[]{:S(2)}, u32[]{:S(2)}) collective-permute-start(bf16[4,2,128,512]{3,2,0,1:T(8,128)(2,1)} %bitcast.56), channel_id=1, source_target_pairs={{0,16},{16,0},{1,17},{17,1},{2,18},{18,2},{3,19},{19,3},{4,20},{20... | collective-permute-start | bytes 3145736 | tf_op jit(solution)/shard_map/ppermute | solution.py:65
  741.1 98.2 %all-to-all-start.4 = ((bf16[8,64,1024]{2,1,0:T(8,128)(2,1)}), bf16[8,64,1024]{2,1,0:T(8,128)(2,1)S(1)}, u32[]{:S(2)}, u32[]{:S(2)}) async-start(bf16[8,64,1024]{2,1,0:T(8,128)(2,1)} %bitcast.81), calls=%async_computation.4 | async-start | bytes 2097152 | tf_op jit(solution)/shard_map/all_to_all | solution.py:106
  744.7 71.3 %collective-permute-start.13 = (bf16[256,1024]{1,0:T(8,128)(2,1)S(1)}, bf16[256,1024]{1,0:T(8,128)(2,1)S(1)}, u32[]{:S(2)}, u32[]{:S(2)}) collective-permute-start(bf16[256,1024]{1,0:T(8,128)(2,1)S(1)} %fusion.29), channel_id=1, source_target_pairs={{0,8},{8,0},{1,9},{9,1},{2,10},{10,2},{3,11},{11,3},{4,12},{12,4},... | collective-permute-start | bytes 1572872 | tf_op jit(solution)/shard_map/ppermute | solution.py:65
  746.6 13.8 %copy-start.36 = (f32[2,2,256,1024]{3,2,1,0:T(8,128)S(1)}, f32[2,2,256,1024]{3,2,1,0:T(8,128)}, u32[]{:S(2)}) copy-start(f32[2,2,256,1024]{3,2,1,0:T(8,128)} %get-tuple-element.111) | copy-start | bytes 12582916
  749.9 57.8 %slice-start = ((s8[8388608]{0:T(1024)(128)(4,1)}), s8[4194304]{0:T(1024)(128)(4,1)S(1)}, s32[]{:S(2)}) async-start(s8[8388608]{0:T(1024)(128)(4,1)} %bitcast.227), calls=%async_computation.7 | async-start | bytes 8388608
  750.1 16.4 %copy-start.43 = (f32[2,256,1024]{2,1,0:T(8,128)S(1)}, f32[2,256,1024]{2,1,0:T(8,128)}, u32[]{:S(2)}) copy-start(f32[2,256,1024]{2,1,0:T(8,128)} %copy-done.42) | copy-start | bytes 6291460
  750.1 87.8 %collective-permute-start.27 = (bf16[4,128,1024]{2,1,0:T(8,128)(2,1)S(1)}, bf16[4,128,1024]{2,1,0:T(8,128)(2,1)S(1)}, u32[]{:S(2)}, u32[]{:S(2)}) collective-permute-start(bf16[4,128,1024]{2,1,0:T(8,128)(2,1)S(1)} %fusion.22), channel_id=1, source_target_pairs={{0,2},{2,0},{1,3},{3,1},{4,6},{6,4},{5,7},{7,5},{8,10},{10,8},{9,1... | collective-permute-start | bytes 3145736 | tf_op jit(solution)/shard_map/ppermute | solution.py:65
  762.1 5.7 copy-start.24
  762.2 45.5 %slice-start.1 = ((s8[8388608]{0:T(1024)(128)(4,1)}), s8[4194304]{0:T(1024)(128)(4,1)S(1)}, s32[]{:S(2)}) async-start(s8[8388608]{0:T(1024)(128)(4,1)} %bitcast.227), calls=%async_computation.8 | async-start | bytes 8388608
  762.2 59.8 %collective-permute-start.15 = (bf16[256,1024]{1,0:T(8,128)(2,1)S(1)}, bf16[256,1024]{1,0:T(8,128)(2,1)S(1)}, u32[]{:S(2)}, u32[]{:S(2)}) collective-permute-start(bf16[256,1024]{1,0:T(8,128)(2,1)S(1)} %fusion.30), channel_id=1, source_target_pairs={{0,1},{1,0},{2,3},{3,2},{4,5},{5,4},{6,7},{7,6},{8,9},{9,8},{10,11... | collective-permute-start | bytes 1572872 | tf_op jit(solution)/shard_map/ppermute | solution.py:65
  810.2 6.0 copy-start.33
  810.2 5.8 copy-start.45
  810.2 6.0 copy-start.54
  811.3 32.2 %collective-permute-start.20 = (bf16[2,2,64,2048]{3,2,1,0:T(8,128)(2,1)}, bf16[2,2,64,2048]{3,2,1,0:T(8,128)(2,1)}, u32[]{:S(2)}, u32[]{:S(2)}) collective-permute-start(bf16[2,2,64,2048]{3,2,1,0:T(8,128)(2,1)} %fusion.19), channel_id=1, source_target_pairs={{0,1},{1,0},{2,3},{3,2},{4,5},{5,4},{6,7},{7,6},{8,9},{9,8},{10,11... | collective-permute-start | bytes 3145736 | tf_op jit(solution)/shard_map/ppermute | solution.py:65
  817.9 19.1 %collective-permute-start.17 = (bf16[4,128,512]{2,1,0:T(8,128)(2,1)S(1)}, bf16[4,128,512]{2,1,0:T(8,128)(2,1)S(1)}, u32[]{:S(2)}, u32[]{:S(2)}) collective-permute-start(bf16[4,128,512]{2,1,0:T(8,128)(2,1)S(1)} %fusion.31), channel_id=1, source_target_pairs={{0,2},{2,0},{1,3},{3,1},{4,6},{6,4},{5,7},{7,5},{8,10},{10,8},{9,1... | collective-permute-start | bytes 1572872 | tf_op jit(solution)/shard_map/ppermute | solution.py:65
  839.2 13.5 %all-to-all-start.2 = ((bf16[8,64,512]{2,1,0:T(8,128)(2,1)}), bf16[8,64,512]{2,1,0:T(8,128)(2,1)S(1)}, u32[]{:S(2)}, u32[]{:S(2)}) async-start(bf16[8,64,512]{2,1,0:T(8,128)(2,1)} %bitcast.59), calls=%async_computation.2 | async-start | bytes 1048576 | tf_op jit(solution)/shard_map/all_to_all | solution.py:106
  847.0 14.4 %collective-permute-start.21 = (bf16[2,64,2048]{2,1,0:T(8,128)(2,1)S(1)}, bf16[2,64,2048]{2,1,0:T(8,128)(2,1)}, u32[]{:S(2)}, u32[]{:S(2)}) collective-permute-start(bf16[2,64,2048]{2,1,0:T(8,128)(2,1)S(1)} %fusion.32), channel_id=1, source_target_pairs={{0,16},{16,0},{1,17},{17,1},{2,18},{18,2},{3,19},{19,3},{4,20},{20... | collective-permute-start | bytes 1572872 | tf_op jit(solution)/shard_map/ppermute | solution.py:65
  852.8 28.1 %all-to-all-start.5 = ((bf16[8,64,1024]{2,1,0:T(8,128)(2,1)}), bf16[8,64,1024]{2,1,0:T(8,128)(2,1)S(1)}, u32[]{:S(2)}, u32[]{:S(2)}) async-start(bf16[8,64,1024]{2,1,0:T(8,128)(2,1)} %bitcast.88), calls=%async_computation.5 | async-start | bytes 2097152 | tf_op jit(solution)/shard_map/all_to_all | solution.py:106
  856.3 5.1 copy-start.47
  864.3 14.7 %collective-permute-start.22 = (bf16[64,2048]{1,0:T(8,128)(2,1)}, bf16[64,2048]{1,0:T(8,128)(2,1)S(1)}, u32[]{:S(2)}, u32[]{:S(2)}) collective-permute-start(bf16[64,2048]{1,0:T(8,128)(2,1)} %fusion.37), channel_id=1, source_target_pairs={{0,2},{2,0},{1,3},{3,1},{4,6},{6,4},{5,7},{7,5},{8,10},{10,8},{9,1... | collective-permute-start | bytes 786440 | tf_op jit(solution)/shard_map/ppermute | solution.py:65
  (32 other events, 68.5 us)
Sparse Core Ops, SparseCore 0:
  204.0 126.9 all-gather.1

commit v5 on v4

--- a/solution.py
+++ b/solution.py
@@ -341,6 +341,18 @@
     def forward_copy(k):
         return gather_copy(xs.at[part(2 * k)], 2 * k + 1, sibling)
 
+    def diagonal(half):
+        slot, peer, sem = ((2, chip(2), 6), (4, chip(1), 0))[half]
+        shift_rows = half * (rows // 2)
+        return pltpu.make_async_remote_copy(
+            src_ref=xs.at[pl.ds(slot * rows + shift_rows, rows // 2)],
+            dst_ref=xs.at[pl.ds(6 * rows + shift_rows, rows // 2)],
+            send_sem=ag_send.at[sem],
+            recv_sem=ag_recv.at[sem],
+            device_id=peer,
+            device_id_type=MESH,
+        )
+
     def sibling_copy(k):
         spot = lax.rem(k, 2)
         return pltpu.make_async_remote_copy(
@@ -373,7 +385,7 @@
         return pltpu.make_async_copy(stage.at[spot], dn_ref.at[slot, :, cols], stage_sem.at[spot])
 
     gather_copy(own_ref, 1, sibling).start()
-    for k in (1, 2, 3):
+    for k in (1, 2):
         gather_copy(own_ref, 2 * k, chip(k)).start()
     own_copy = pltpu.make_async_copy(own_ref, xs.at[part(0)], local_sem.at[0])
     own_copy.start()
@@ -405,7 +417,12 @@
 
             @pl.when(i == at)
             def _():
-                gather_copy(own_ref, 2 * ready, chip(ready)).wait_recv()
+                if ready < 3:
+                    gather_copy(own_ref, 2 * ready, chip(ready)).wait_recv()
+                    diagonal(ready - 1).start()
+                else:
+                    diagonal(0).wait_recv()
+                    diagonal(1).wait_recv()
                 forward_copy(ready).start()
 
         @pl.when(second == 0)
@@ -513,8 +530,10 @@
     for k in (0, 1):
         sibling_copy(k).wait_send()
     gather_copy(own_ref, 1, sibling).wait_send()
+    for k in (1, 2):
+        gather_copy(own_ref, 2 * k, chip(k)).wait_send()
+        diagonal(k - 1).wait_send()
     for k in (1, 2, 3):
-        gather_copy(own_ref, 2 * k, chip(k)).wait_send()
         forward_copy(k).wait_send()
         owner_copy(k).wait_send()
 

time: 897 us -> 896 us (level)
  no operation moved by 1% of the time
where the time goes in v5:
time: 896 us; the launch traced here: 889 us
  Pallas kernels  353 us (39%)
  waiting for transfers between devices  183 us (20%)
  local copies, waits for them, and re-layouts  119 us (13%)
  starting transfers between devices  110 us (12%)
  other arithmetic  73.3 us (8%)
  matrix products  35 us (4%)
  between operations  16 us (2%)
    pallas_call x1, Pallas kernels, opening_call(): pl.pallas_call(opening_kernel, in_specs=[anywhere] * 7, out_specs=[anywhe...  174 us
    ppermute x26, waiting for transfers between devices, shift(): return lax.ppermute(value, axis, [(i, (i + step) % n) for i in range(n)])  114 us
    pallas_call x1, Pallas kernels, ffn_call(): pl.pallas_call(ffn_kernel, in_specs=[anywhere] * (2 + len(pieces)), out_s...  108 us
    pallas_call x2, Pallas kernels, attention_call(): pl.pallas_call(kernel, grid_spec=pltpu.PrefetchScalarGridSpec(num_scalar_...  51.5 us
    all_to_all x1, starting transfers between devices, local(): lax.all_to_all(attended.reshape(8, slots, q_width), TEAM, 0, 0, tiled=True)  44.9 us
    unnamed x130, local copies, waits for them, and re-layouts  44.9 us
    ppermute x26, starting transfers between devices, shift(): return lax.ppermute(value, axis, [(i, (i + step) % n) for i in range(n)])  40.8 us
    ppermute x1, waiting for transfers between devices, local(): back = lax.ppermute(grad_early, 'h', [(1, 0)])  35.9 us
  transfers between devices with their start and end apart: 35, of which 13 were waited for; matrix products, arithmetic and copies ran while one was open for 20% of the time, Pallas kernels for 8%

profile of v5, /device:TPU:0, one launch (start us, length us, event | category | flops | bytes accessed | tf_op | source)
XLA Modules:
  0.0 888.6 jit_solution(7676628115571852463)
XLA Ops:
  14.8 174.4 %shard_map.212 = (bf16[8,256,2176]{2,1,0:T(8,128)(2,1)S(1)}, bf16[8,256,2048]{2,1,0:T(8,128)(2,1)S(1)}, bf16[2,4,2,128,384]{4,3,2,1,0:T(8,128)(2,1)S(1)}, bf16[2...) custom-call(bf16[256,2176]{1,0:T(8,128)(2,1)S(1)} %fusion.16.tok_ref, ...), custom_call_target="tpu_custom_call" | custom-call | bytes 314572800 | tf_op jit(solution)/shard_map/pallas_call | solution.py:840
  189.2 3.5 copy-done.2
  192.7 3.3 copy-done.11
  207.2 2.5 fusion.51
  213.3 4.1 negate_select_fusion
  218.7 13.7 %shard_map.213 = (bf16[2048,2048]{1,0:T(8,128)(2,1)}, bf16[2048,384]{1,0:T(8,128)(2,1)S(1)}) custom-call(bf16[8,256,2176]{2,1,0:T(8,128)(2,1)} %copy-done.2, f32[1,2048]{1,0:T(1,128)S(1)} %reshape.239.gain_ref, bf16[2048,384]{1,0:T(8,128)(2,1)S(1)} %bitcast.214, f32[2048,256]{1,0:T(8,128)S(1)} %get-tuple-element.133.cos_ref, ...), custom_call_target="tpu_custom_call" | custom-call | flops 3221225472 | bytes 25165824 | tf_op jit(solution)/shard_map/pallas_call | solution.py:163
  234.5 3.6 collective-permute-start
  240.0 9.4 %collective-permute-done.early_ref = bf16[4,512,128]{2,1,0:T(8,128)(2,1)S(1)} collective-permute-done((bf16[4,512,128]{2,1,0:T(8,128)(2,1)}, bf16[4,512,128]{2,1,0:T(8,128)(2,1)S(1)}, u32[]{:S(2)}, u32[]{:S(2)}) %collective-permute-start) | collective-permute-done | bytes 524320 | tf_op jit(solution)/shard_map/ppermute | solution.py:938
  250.9 17.0 %shard_map.214 = bf16[4,512,256]{2,1,0:T(8,128)(2,1)S(1)} custom-call(s32[1]{0:T(128)} %bitcast.2.late_ref, s32[4]{0:T(128)S(1)} %slice.97.length_ref, bf16[4,512,384]{2,1,0:T(8,128)(2,1)S(1)} %bitcast.220, bf16[4,512,128]{2,1,0:T(8,128)(2,1)S(1)} %collective-permute-done.early_ref), custom_call_target="tpu_custom_call" | custom-call | flops 3000000000 | bytes 8388608 | tf_op jit(solution)/shard_map/pallas_call | solution.py:256
  269.2 44.9 %all-to-all-start = ((bf16[8,256,256]{1,2,0:T(8,128)(2,1)}), bf16[8,256,256]{1,2,0:T(8,128)(2,1)}, u32[]{:S(2)}, u32[]{:S(2)}) async-start(bf16[8,256,256]{1,2,0:T(8,128)(2,1)} %copy.99), calls=%async_computation | async-start | bytes 2097152 | tf_op jit(solution)/shard_map/all_to_all | solution.py:945
  316.3 20.7 %all-to-all-done = bf16[8,256,256]{1,2,0:T(8,128)(2,1)} async-done(((bf16[8,256,256]{1,2,0:T(8,128)(2,1)}), bf16[8,256,256]{1,2,0:T(8,128)(2,1)}, u32[]{:S(2)}, u32[]{:S(2)}) %all-to-all-start) | async-done | bytes 1048608 | tf_op jit(solution)/shard_map/all_to_all | solution.py:945
  337.0 6.4 multiply_reduce_fusion.3
  345.0 17.3 %collective-permute-done.3 = bf16[4,128,1024]{2,1,0:T(8,128)(2,1)} collective-permute-done((bf16[4,128,1024]{2,1,0:T(8,128)(2,1)}, bf16[4,128,1024]{2,1,0:T(8,128)(2,1)}, u32[]{:S(2)}, u32[]{:S(2)}) %collective-permute-start.3) | collective-permute-done | bytes 1048608 | tf_op jit(solution)/shard_map/ppermute | solution.py:65
  362.3 107.8 %shard_map.215 = (f32[256,2048]{1,0:T(8,128)}, bf16[8,256,2048]{2,1,0:T(8,128)(2,1)}, bf16[2048,1024]{1,0:T(8,128)(2,1)}, bf16[2048,1024]{1,0:T(8,128)(2,1)}, bf16[2048,1024]{1,0:T(8,128)(2,1)}) custom-call(bf16[256,2048]{1,0:T(8,128)(2,1)} %multiply_convert_fusion.own_ref, bf16[8,256,2048]{2,1,0:T(8,128)(2,1)} %copy-done.11, ...), custom_call_target="tpu_custom_call" | custom-call | flops 77309411328 | bytes 62914560 | tf_op jit(solution)/shard_map/pallas_call | solution.py:547
  470.2 4.8 slice_bitcast_fusion
  477.2 3.0 multiply_reduce_fusion.1
  481.3 6.5 convolution_convert_fusion.2
  488.9 3.6 all-to-all-start.1
  494.0 3.2 dynamic-slice_bitcast_fusion.1
  498.7 7.0 convolution_convert_fusion
  508.1 7.2 convert_add_fusion.1
  516.7 34.5 %shard_map.216 = (f32[4,512,384]{2,1,0:T(8,128)}, bf16[4,512,128]{2,1,0:T(8,128)(2,1)S(1)}) custom-call(s32[1]{0:T(128)} %bitcast.2.late_ref, s32[4]{0:T(128)S(1)} %slice.97.length_ref, bf16[4,512,384]{2,1,0:T(8,128)(2,1)S(1)} %bitcast.221, bf16[4,512,128]{2,1,0:T(8,128)(2,1)S(1)} %collective-permute-done.early_ref, bf16[4,512,256]{2,1,0:T(8,128)(2,1)S(1)} %bitcast.217), custom_call_target="tpu_custom_call" | custom-call | flops 8000000000 | bytes 8388608 | tf_op jit(solution)/shard_map/pallas_call | solution.py:256
  552.4 6.7 constant_dynamic-slice_fusion.1
  562.8 2.5 convert_add_fusion.3
  565.3 35.9 %collective-permute-done.7 = bf16[4,512,128]{2,1,0:T(8,128)(2,1)S(1)} collective-permute-done((bf16[4,512,128]{2,1,0:T(8,128)(2,1)S(1)}, bf16[4,512,128]{2,1,0:T(8,128)(2,1)S(1)}, u32[]{:S(2)}, u32[]{:S(2)}) %collective-permute-start.7) | collective-permute-done | bytes 524320 | tf_op jit(solution)/shard_map/ppermute | solution.py:980
  602.5 5.8 shard_map.217
  608.2 7.6 multiply_reduce_fusion
  615.9 2.8 fusion
  623.0 3.3 copy-done.21
  626.4 2.7 slice_bitcast_fusion.5
  629.1 2.7 slice_bitcast_fusion.3
  633.5 2.6 fusion.15
  636.1 4.2 all-to-all-start.3
  640.3 6.9 convolution_convert_fusion.1
  652.3 4.5 convert_add_fusion.4
  656.8 6.1 collective-permute-done.11
  662.9 3.5 bitcast_add_fusion.9
  667.3 3.0 collective-permute-start.12
  674.6 5.9 bitcast_add_fusion
  680.5 3.0 fusion.49
  683.5 4.3 fusion.21
  687.8 2.9 collective-permute-start.25
  692.4 4.0 convert_add_fusion
  696.3 3.3 copy-done.27
  701.3 4.6 reshape.251
  705.9 3.0 constant_dynamic-slice_fusion.3
  708.9 2.5 copy.123
  715.6 15.7 %collective-permute-done.10 = bf16[2,256,1024]{2,1,0:T(8,128)(2,1)} collective-permute-done((bf16[2,256,1024]{2,1,0:T(8,128)(2,1)}, bf16[2,256,1024]{2,1,0:T(8,128)(2,1)}, u32[]{:S(2)}, u32[]{:S(2)}) %collective-permute-start.10) | collective-permute-done | bytes 1048608 | tf_op jit(solution)/shard_map/ppermute | solution.py:65
  735.7 2.8 fusion.14
  740.1 3.6 all-to-all-start.4
  745.6 3.3 convert_add_fusion.2
  751.1 8.3 collective-permute-done.14
  761.2 4.1 collective-permute-start.15
  768.0 38.8 %collective-permute-done.19 = bf16[2,2,2,64,2048]{4,3,1,0,2:T(8,128)(2,1)} collective-permute-done((bf16[2,2,2,64,2048]{4,3,1,0,2:T(8,128)(2,1)}, bf16[2,2,2,64,2048]{4,3,1,0,2:T(8,128)(2,1)}, u32[]{:S(2)}, u32[]{:S(2)}) %collective-permute-start.19) | collective-permute-done | bytes 2097184 | tf_op jit(solution)/shard_map/ppermute | solution.py:65
  806.7 2.5 bitcast_add_fusion.1
  812.0 3.0 collective-permute-done.13
  816.9 4.1 collective-permute-start.17
  824.3 11.4 %collective-permute-done.17 = bf16[4,128,512]{2,1,0:T(8,128)(2,1)S(1)} collective-permute-done((bf16[4,128,512]{2,1,0:T(8,128)(2,1)S(1)}, bf16[4,128,512]{2,1,0:T(8,128)(2,1)S(1)}, u32[]{:S(2)}, u32[]{:S(2)}) %collective-permute-start.17) | collective-permute-done | bytes 524320 | tf_op jit(solution)/shard_map/ppermute | solution.py:65
  838.1 4.3 all-to-all-start.2
  849.2 2.5 all-to-all-done.2
  851.7 3.6 all-to-all-start.5
  855.4 4.9 collective-permute-done.21
  863.2 2.5 collective-permute-start.22
  869.3 8.6 collective-permute-done.22
  (264 shorter events, 115.9 us)
Async XLA Ops:
  7.2 5.6 copy-start.25
  7.2 329.8 %all-gather.2.cloned.1.call-start = ((), (), s32[]{:S(2)}) async-start(), calls=%async_computation.6 | async-start | bytes 8650752 | tf_op jit(solution)/shard_map/all_gather | solution.py:923
  203.9 64.0 %collective-permute-start.1 = (bf16[4,128,1024]{2,1,0:T(8,128)(2,1)}, bf16[4,128,1024]{2,1,0:T(8,128)(2,1)}, u32[]{:S(2)}, u32[]{:S(2)}) collective-permute-start(bf16[4,128,1024]{2,1,0:T(8,128)(2,1)} %get-tuple-element.63.refs_8_), channel_id=1, source_target_pairs={{0,2},{2,0},{1,3},{3,1},{4,6},{6,4},{5,7},{7,5},{8,10},{10,8},{9,1... | collective-permute-start | bytes 3145736 | tf_op jit(solution)/shard_map/ppermute | solution.py:65
  206.0 12.7 %copy-start.9 = (f32[1,2048]{1,0:T(1,128)}, f32[1,2048]{1,0:T(1,128)S(1)}, u32[]{:S(2)}) copy-start(f32[1,2048]{1,0:T(1,128)S(1)} %reshape.239.gain_ref) | copy-start | bytes 24580
  218.7 13.7 %copy-start = (f32[2048,256]{1,0:T(8,128)}, f32[2048,256]{1,0:T(8,128)S(1)}, u32[]{:S(2)}) copy-start(f32[2048,256]{1,0:T(8,128)S(1)} %get-tuple-element.133.cos_ref) | copy-start | bytes 6291460
  218.7 13.7 %copy-start.1 = (f32[2048,256]{1,0:T(8,128)}, f32[2048,256]{1,0:T(8,128)S(1)}, u32[]{:S(2)}) copy-start(f32[2048,256]{1,0:T(8,128)S(1)} %get-tuple-element.134.sin_ref) | copy-start | bytes 6291460
  234.5 15.0 %collective-permute-start = (bf16[4,512,128]{2,1,0:T(8,128)(2,1)}, bf16[4,512,128]{2,1,0:T(8,128)(2,1)S(1)}, u32[]{:S(2)}, u32[]{:S(2)}) collective-permute-start(bf16[4,512,128]{2,1,0:T(8,128)(2,1)} %slice.128), channel_id=1, source_target_pairs={{0,2},{1,3},{4,6},{5,7},{8,10},{9,11},{12,14},{13,15},{16,18},{17,... | collective-permute-start | bytes 1572872 | tf_op jit(solution)/shard_map/ppermute | solution.py:938
  269.2 44.9 %copy-start.18 = (bf16[4,128,1024]{2,1,0:T(8,128)(2,1)S(1)}, bf16[4,128,1024]{2,1,0:T(8,128)(2,1)}, u32[]{:S(2)}) copy-start(bf16[4,128,1024]{2,1,0:T(8,128)(2,1)} %copy-done.17) | copy-start | bytes 3145732
  269.2 67.8 %all-to-all-start = ((bf16[8,256,256]{1,2,0:T(8,128)(2,1)}), bf16[8,256,256]{1,2,0:T(8,128)(2,1)}, u32[]{:S(2)}, u32[]{:S(2)}) async-start(bf16[8,256,256]{1,2,0:T(8,128)(2,1)} %copy.99), calls=%async_computation | async-start | bytes 2097152 | tf_op jit(solution)/shard_map/all_to_all | solution.py:945
  314.2 30.6 %collective-permute-start.2 = (bf16[4,128,1024]{2,1,0:T(8,128)(2,1)S(1)}, bf16[4,128,1024]{2,1,0:T(8,128)(2,1)}, u32[]{:S(2)}, u32[]{:S(2)}) collective-permute-start(bf16[4,128,1024]{2,1,0:T(8,128)(2,1)S(1)} %copy-done.18), channel_id=1, source_target_pairs={{0,16},{16,0},{1,17},{17,1},{2,18},{18,2},{3,19},{19,3},{4,20},{20... | collective-permute-start | bytes 3145736 | tf_op jit(solution)/shard_map/ppermute | solution.py:65
  315.2 47.1 %collective-permute-start.3 = (bf16[4,128,1024]{2,1,0:T(8,128)(2,1)}, bf16[4,128,1024]{2,1,0:T(8,128)(2,1)}, u32[]{:S(2)}, u32[]{:S(2)}) collective-permute-start(bf16[4,128,1024]{2,1,0:T(8,128)(2,1)} %collective-permute-done.1.refs_10_), channel_id=1, source_target_pairs={{0,16},{16,0},{1,17},{17,1},{2,18},{18,2},{3,19},{19,3},{4,20},{20... | collective-permute-start | bytes 3145736 | tf_op jit(solution)/shard_map/ppermute | solution.py:65
  470.2 10.0 %copy-start.49 = (bf16[1,256,2048]{2,1,0:T(8,128)(2,1)S(1)}, bf16[1,256,2048]{2,1,0:T(8,128)(2,1)}, u32[]{:S(2)}) copy-start(bf16[1,256,2048]{2,1,0:T(8,128)(2,1)} %param.25) | copy-start | bytes 3145732
  475.0 33.0 %collective-permute-start.4 = (bf16[2,2,256,2048]{3,2,1,0:T(8,128)(2,1)}, bf16[2,2,256,2048]{3,2,1,0:T(8,128)(2,1)}, u32[]{:S(2)}, u32[]{:S(2)}) collective-permute-start(bf16[2,2,256,2048]{3,2,1,0:T(8,128)(2,1)} %slice_bitcast_fusion), channel_id=1, source_target_pairs={{0,4},{4,0},{1,5},{5,1},{2,6},{6,2},{3,7},{7,3},{8,12},{12,8},{9,1... | collective-permute-start | bytes 12582920 | tf_op jit(solution)/shard_map/ppermute | solution.py:65
  481.3 6.5 copy-start.28
  488.9 26.4 %all-to-all-start.1 = ((bf16[8,256,256]{2,1,0:T(8,128)(2,1)}), bf16[8,256,256]{2,1,0:T(8,128)(2,1)S(1)}, u32[]{:S(2)}, u32[]{:S(2)}) async-start(bf16[8,256,256]{2,1,0:T(8,128)(2,1)} %bitcast.234), calls=%async_computation.1 | async-start | bytes 2097152 | tf_op jit(solution)/shard_map/all_to_all | solution.py:963
  494.0 4.7 copy-start.29
  494.0 14.1 %slice-start.2 = ((s8[8388608]{0:T(1024)(128)(4,1)}), s8[4194304]{0:T(1024)(128)(4,1)S(1)}, s32[]{:S(2)}) async-start(s8[8388608]{0:T(1024)(128)(4,1)} %bitcast.230), calls=%async_computation.9 | async-start | bytes 8388608
  497.2 8.5 copy-start.51
  497.2 10.8 %slice-start.3 = ((s8[8388608]{0:T(1024)(128)(4,1)}), s8[4194304]{0:T(1024)(128)(4,1)S(1)}, s32[]{:S(2)}) async-start(s8[8388608]{0:T(1024)(128)(4,1)} %bitcast.230), calls=%async_computation.10 | async-start | bytes 8388608
  497.2 62.0 %collective-permute-start.23 = (bf16[4,2,128,1024]{3,2,1,0:T(8,128)(2,1)}, bf16[4,2,128,1024]{3,2,1,0:T(8,128)(2,1)}, u32[]{:S(2)}, u32[]{:S(2)}) collective-permute-start(bf16[4,2,128,1024]{3,2,1,0:T(8,128)(2,1)} %dynamic-slice_bitcast_fusion.1), channel_id=1, source_target_pairs={{0,16},{16,0},{1,17},{17,1},{2,18},{18,2},{3,19},{19,3},{4,20},{20... | collective-permute-start | bytes 6291464 | tf_op jit(solution)/shard_map/ppermute | solution.py:65
  507.4 139.8 %collective-permute-start.9 = (bf16[4,2,128,1024]{3,2,1,0:T(8,128)(2,1)}, bf16[4,2,128,1024]{3,2,1,0:T(8,128)(2,1)}, u32[]{:S(2)}, u32[]{:S(2)}) collective-permute-start(bf16[4,2,128,1024]{3,2,1,0:T(8,128)(2,1)} %dynamic-slice_bitcast_fusion.2), channel_id=1, source_target_pairs={{0,16},{16,0},{1,17},{17,1},{2,18},{18,2},{3,19},{19,3},{4,20},{20... | collective-permute-start | bytes 6291464 | tf_op jit(solution)/shard_map/ppermute | solution.py:65
  551.1 50.1 %collective-permute-start.7 = (bf16[4,512,128]{2,1,0:T(8,128)(2,1)S(1)}, bf16[4,512,128]{2,1,0:T(8,128)(2,1)S(1)}, u32[]{:S(2)}, u32[]{:S(2)}) collective-permute-start(bf16[4,512,128]{2,1,0:T(8,128)(2,1)S(1)} %get-tuple-element.83), channel_id=1, source_target_pairs={{2,0},{3,1},{6,4},{7,5},{10,8},{11,9},{14,12},{15,13},{18,16},{19,... | collective-permute-start | bytes 1572872 | tf_op jit(solution)/shard_map/ppermute | solution.py:980
  561.6 113.0 %collective-permute-start.18 = (bf16[2,2,2,2,64,2048]{5,4,2,0,3,1:T(8,128)(2,1)}, bf16[2,2,2,2,64,2048]{5,4,2,0,3,1:T(8,128)(2,1)}, u32[]{:S(2)}, u32[]{:S(2)}) collective-permute-start(bf16[2,2,2,2,64,2048]{5,4,2,0,3,1:T(8,128)(2,1)} %bitcast.209), channel_id=1, source_target_pairs={{0,4},{4,0},{1,5},{5,1},{2,6},{6,2},{3,7},{7,3},{8,12},{12,8},{9,1... | collective-permute-start | bytes 12582920 | tf_op jit(solution)/shard_map/ppermute | solution.py:65
  565.3 35.9 %copy-start.34 = (f32[4,2,128,1024]{3,2,1,0:T(8,128)}, f32[4,2,128,1024]{3,2,1,0:T(8,128)S(1)}, u32[]{:S(2)}) copy-start(f32[4,2,128,1024]{3,2,1,0:T(8,128)S(1)} %convert_add_fusion.3) | copy-start | bytes 12582916
  602.5 29.4 %collective-permute-start.24 = (bf16[4,128,1024]{2,1,0:T(8,128)(2,1)}, bf16[4,128,1024]{2,1,0:T(8,128)(2,1)}, u32[]{:S(2)}, u32[]{:S(2)}) collective-permute-start(bf16[4,128,1024]{2,1,0:T(8,128)(2,1)} %fusion.20), channel_id=1, source_target_pairs={{0,2},{2,0},{1,3},{3,1},{4,6},{6,4},{5,7},{7,5},{8,10},{10,8},{9,1... | collective-permute-start | bytes 3145736 | tf_op jit(solution)/shard_map/ppermute | solution.py:65
  615.9 10.5 %copy-start.21 = (f32[2048,2048]{1,0:T(8,128)}, f32[2048,2048]{1,0:T(8,128)S(1)}, u32[]{:S(2)}) copy-start(f32[2048,2048]{1,0:T(8,128)S(1)} %get-tuple-element.132) | copy-start | bytes 50331652
  615.9 5.2 copy-start.50
  618.6 55.9 %collective-permute-start.8 = (bf16[2,2,256,2048]{3,2,1,0:T(8,128)(2,1)}, bf16[2,2,256,2048]{3,2,1,0:T(8,128)(2,1)}, u32[]{:S(2)}, u32[]{:S(2)}) collective-permute-start(bf16[2,2,256,2048]{3,2,1,0:T(8,128)(2,1)} %fusion), channel_id=1, source_target_pairs={{0,4},{4,0},{1,5},{5,1},{2,6},{6,2},{3,7},{7,3},{8,12},{12,8},{9,1... | collective-permute-start | bytes 12582920 | tf_op jit(solution)/shard_map/ppermute | solution.py:65
  621.1 12.4 %copy-start.35 = (f32[4,2,128,1024]{3,2,1,0:T(8,128)S(1)}, f32[4,2,128,1024]{3,2,1,0:T(8,128)}, u32[]{:S(2)}) copy-start(f32[4,2,128,1024]{3,2,1,0:T(8,128)} %copy-done.34) | copy-start | bytes 12582916
  629.1 27.7 %collective-permute-start.5 = (bf16[2,256,1024]{2,1,0:T(8,128)(2,1)}, bf16[2,256,1024]{2,1,0:T(8,128)(2,1)}, u32[]{:S(2)}, u32[]{:S(2)}) collective-permute-start(bf16[2,256,1024]{2,1,0:T(8,128)(2,1)} %slice_bitcast_fusion.5), channel_id=1, source_target_pairs={{0,1},{1,0},{2,3},{3,2},{4,5},{5,4},{6,7},{7,6},{8,9},{9,8},{10,11... | collective-permute-start | bytes 3145736 | tf_op jit(solution)/shard_map/ppermute | solution.py:65
  631.8 31.1 %collective-permute-start.11 = (bf16[2,256,1024]{2,1,0:T(8,128)(2,1)}, bf16[2,256,1024]{2,1,0:T(8,128)(2,1)}, u32[]{:S(2)}, u32[]{:S(2)}) collective-permute-start(bf16[2,256,1024]{2,1,0:T(8,128)(2,1)} %slice_bitcast_fusion.3), channel_id=1, source_target_pairs={{0,8},{8,0},{1,9},{9,1},{2,10},{10,2},{3,11},{11,3},{4,12},{12,4},... | collective-permute-start | bytes 3145736 | tf_op jit(solution)/shard_map/ppermute | solution.py:65
  636.1 36.8 %all-to-all-start.3 = ((bf16[8,64,1024]{2,1,0:T(8,128)(2,1)}), bf16[8,64,1024]{2,1,0:T(8,128)(2,1)S(1)}, u32[]{:S(2)}, u32[]{:S(2)}) async-start(bf16[8,64,1024]{2,1,0:T(8,128)(2,1)} %bitcast.233), calls=%async_computation.3 | async-start | bytes 2097152 | tf_op jit(solution)/shard_map/all_to_all | solution.py:106
  640.2 8.4 copy-start.10
  647.2 91.3 %collective-permute-start.26 = (bf16[4,2,128,1024]{3,2,1,0:T(8,128)(2,1)}, bf16[4,2,128,1024]{3,2,1,0:T(8,128)(2,1)}, u32[]{:S(2)}, u32[]{:S(2)}) collective-permute-start(bf16[4,2,128,1024]{3,2,1,0:T(8,128)(2,1)} %dynamic-slice_bitcast_fusion), channel_id=1, source_target_pairs={{0,16},{16,0},{1,17},{17,1},{2,18},{18,2},{3,19},{19,3},{4,20},{20... | collective-permute-start | bytes 6291464 | tf_op jit(solution)/shard_map/ppermute | solution.py:65
  666.4 4.8 copy-start.42
  667.3 72.7 %collective-permute-start.12 = (bf16[256,1024]{1,0:T(8,128)(2,1)}, bf16[256,1024]{1,0:T(8,128)(2,1)S(1)}, u32[]{:S(2)}, u32[]{:S(2)}) collective-permute-start(bf16[256,1024]{1,0:T(8,128)(2,1)} %fusion.34), channel_id=1, source_target_pairs={{0,1},{1,0},{2,3},{3,2},{4,5},{5,4},{6,7},{7,6},{8,9},{9,8},{10,11... | collective-permute-start | bytes 1572872 | tf_op jit(solution)/shard_map/ppermute | solution.py:65
  671.2 68.9 %collective-permute-start.6 = (bf16[256,1024]{1,0:T(8,128)(2,1)}, bf16[256,1024]{1,0:T(8,128)(2,1)}, u32[]{:S(2)}, u32[]{:S(2)}) collective-permute-start(bf16[256,1024]{1,0:T(8,128)(2,1)} %fusion.33), channel_id=1, source_target_pairs={{0,8},{8,0},{1,9},{9,1},{2,10},{10,2},{3,11},{11,3},{4,12},{12,4},... | collective-permute-start | bytes 1572872 | tf_op jit(solution)/shard_map/ppermute | solution.py:65
  683.5 8.3 copy-start.37
  683.5 8.8 copy-start.31
  687.8 47.3 %collective-permute-start.25 = (bf16[4,128,1024]{2,1,0:T(8,128)(2,1)}, bf16[4,128,1024]{2,1,0:T(8,128)(2,1)}, u32[]{:S(2)}, u32[]{:S(2)}) collective-permute-start(bf16[4,128,1024]{2,1,0:T(8,128)(2,1)} %fusion.21), channel_id=1, source_target_pairs={{0,2},{2,0},{1,3},{3,1},{4,6},{6,4},{5,7},{7,5},{8,10},{10,8},{9,1... | collective-permute-start | bytes 3145736 | tf_op jit(solution)/shard_map/ppermute | solution.py:65
  691.9 39.4 %collective-permute-start.10 = (bf16[2,256,1024]{2,1,0:T(8,128)(2,1)}, bf16[2,256,1024]{2,1,0:T(8,128)(2,1)}, u32[]{:S(2)}, u32[]{:S(2)}) collective-permute-start(bf16[2,256,1024]{2,1,0:T(8,128)(2,1)} %fusion.17), channel_id=1, source_target_pairs={{0,1},{1,0},{2,3},{3,2},{4,5},{5,4},{6,7},{7,6},{8,9},{9,8},{10,11... | collective-permute-start | bytes 3145736 | tf_op jit(solution)/shard_map/ppermute | solution.py:65
  715.6 20.1 %copy-start.32 = (f32[4,2,128,1024]{3,2,1,0:T(8,128)S(1)}, f32[4,2,128,1024]{3,2,1,0:T(8,128)}, u32[]{:S(2)}) copy-start(f32[4,2,128,1024]{3,2,1,0:T(8,128)} %convert_add_fusion.4) | copy-start | bytes 12582916
  731.3 28.1 %collective-permute-start.14 = (bf16[2,256,1024]{2,1,0:T(8,128)(2,1)S(1)}, bf16[2,256,1024]{2,1,0:T(8,128)(2,1)}, u32[]{:S(2)}, u32[]{:S(2)}) collective-permute-start(bf16[2,256,1024]{2,1,0:T(8,128)(2,1)S(1)} %fusion.18), channel_id=1, source_target_pairs={{0,8},{8,0},{1,9},{9,1},{2,10},{10,2},{3,11},{11,3},{4,12},{12,4},... | collective-permute-start | bytes 3145736 | tf_op jit(solution)/shard_map/ppermute | solution.py:65
  735.1 71.6 %collective-permute-start.19 = (bf16[2,2,2,64,2048]{4,3,1,0,2:T(8,128)(2,1)}, bf16[2,2,2,64,2048]{4,3,1,0,2:T(8,128)(2,1)}, u32[]{:S(2)}, u32[]{:S(2)}) collective-permute-start(bf16[2,2,2,64,2048]{4,3,1,0,2:T(8,128)(2,1)} %fusion.10), channel_id=1, source_target_pairs={{0,8},{8,0},{1,9},{9,1},{2,10},{10,2},{3,11},{11,3},{4,12},{12,4},... | collective-permute-start | bytes 6291464 | tf_op jit(solution)/shard_map/ppermute | solution.py:65
  738.5 76.7 %collective-permute-start.16 = (bf16[4,2,128,512]{3,2,0,1:T(8,128)(2,1)}, bf16[4,2,128,512]{3,2,0,1:T(8,128)(2,1)}, u32[]{:S(2)}, u32[]{:S(2)}) collective-permute-start(bf16[4,2,128,512]{3,2,0,1:T(8,128)(2,1)} %bitcast.56), channel_id=1, source_target_pairs={{0,16},{16,0},{1,17},{17,1},{2,18},{18,2},{3,19},{19,3},{4,20},{20... | collective-permute-start | bytes 3145736 | tf_op jit(solution)/shard_map/ppermute | solution.py:65
  740.1 98.0 %all-to-all-start.4 = ((bf16[8,64,1024]{2,1,0:T(8,128)(2,1)}), bf16[8,64,1024]{2,1,0:T(8,128)(2,1)S(1)}, u32[]{:S(2)}, u32[]{:S(2)}) async-start(bf16[8,64,1024]{2,1,0:T(8,128)(2,1)} %bitcast.81), calls=%async_computation.4 | async-start | bytes 2097152 | tf_op jit(solution)/shard_map/all_to_all | solution.py:106
  743.6 71.4 %collective-permute-start.13 = (bf16[256,1024]{1,0:T(8,128)(2,1)S(1)}, bf16[256,1024]{1,0:T(8,128)(2,1)S(1)}, u32[]{:S(2)}, u32[]{:S(2)}) collective-permute-start(bf16[256,1024]{1,0:T(8,128)(2,1)S(1)} %fusion.29), channel_id=1, source_target_pairs={{0,8},{8,0},{1,9},{9,1},{2,10},{10,2},{3,11},{11,3},{4,12},{12,4},... | collective-permute-start | bytes 1572872 | tf_op jit(solution)/shard_map/ppermute | solution.py:65
  745.6 13.8 %copy-start.36 = (f32[2,2,256,1024]{3,2,1,0:T(8,128)S(1)}, f32[2,2,256,1024]{3,2,1,0:T(8,128)}, u32[]{:S(2)}) copy-start(f32[2,2,256,1024]{3,2,1,0:T(8,128)} %get-tuple-element.111) | copy-start | bytes 12582916
  748.9 57.8 %slice-start = ((s8[8388608]{0:T(1024)(128)(4,1)}), s8[4194304]{0:T(1024)(128)(4,1)S(1)}, s32[]{:S(2)}) async-start(s8[8388608]{0:T(1024)(128)(4,1)} %bitcast.227), calls=%async_computation.7 | async-start | bytes 8388608
  749.1 16.2 %copy-start.43 = (f32[2,256,1024]{2,1,0:T(8,128)S(1)}, f32[2,256,1024]{2,1,0:T(8,128)}, u32[]{:S(2)}) copy-start(f32[2,256,1024]{2,1,0:T(8,128)} %copy-done.42) | copy-start | bytes 6291460
  749.1 87.6 %collective-permute-start.27 = (bf16[4,128,1024]{2,1,0:T(8,128)(2,1)S(1)}, bf16[4,128,1024]{2,1,0:T(8,128)(2,1)S(1)}, u32[]{:S(2)}, u32[]{:S(2)}) collective-permute-start(bf16[4,128,1024]{2,1,0:T(8,128)(2,1)S(1)} %fusion.22), channel_id=1, source_target_pairs={{0,2},{2,0},{1,3},{3,1},{4,6},{6,4},{5,7},{7,5},{8,10},{10,8},{9,1... | collective-permute-start | bytes 3145736 | tf_op jit(solution)/shard_map/ppermute | solution.py:65
  761.2 5.5 copy-start.24
  761.2 45.6 %slice-start.1 = ((s8[8388608]{0:T(1024)(128)(4,1)}), s8[4194304]{0:T(1024)(128)(4,1)S(1)}, s32[]{:S(2)}) async-start(s8[8388608]{0:T(1024)(128)(4,1)} %bitcast.227), calls=%async_computation.8 | async-start | bytes 8388608
  761.2 59.8 %collective-permute-start.15 = (bf16[256,1024]{1,0:T(8,128)(2,1)S(1)}, bf16[256,1024]{1,0:T(8,128)(2,1)S(1)}, u32[]{:S(2)}, u32[]{:S(2)}) collective-permute-start(bf16[256,1024]{1,0:T(8,128)(2,1)S(1)} %fusion.30), channel_id=1, source_target_pairs={{0,1},{1,0},{2,3},{3,2},{4,5},{5,4},{6,7},{7,6},{8,9},{9,8},{10,11... | collective-permute-start | bytes 1572872 | tf_op jit(solution)/shard_map/ppermute | solution.py:65
  809.2 6.0 copy-start.33
  809.2 5.8 copy-start.45
  809.3 6.0 copy-start.54
  810.4 32.1 %collective-permute-start.20 = (bf16[2,2,64,2048]{3,2,1,0:T(8,128)(2,1)}, bf16[2,2,64,2048]{3,2,1,0:T(8,128)(2,1)}, u32[]{:S(2)}, u32[]{:S(2)}) collective-permute-start(bf16[2,2,64,2048]{3,2,1,0:T(8,128)(2,1)} %fusion.19), channel_id=1, source_target_pairs={{0,1},{1,0},{2,3},{3,2},{4,5},{5,4},{6,7},{7,6},{8,9},{9,8},{10,11... | collective-permute-start | bytes 3145736 | tf_op jit(solution)/shard_map/ppermute | solution.py:65
  816.9 18.9 %collective-permute-start.17 = (bf16[4,128,512]{2,1,0:T(8,128)(2,1)S(1)}, bf16[4,128,512]{2,1,0:T(8,128)(2,1)S(1)}, u32[]{:S(2)}, u32[]{:S(2)}) collective-permute-start(bf16[4,128,512]{2,1,0:T(8,128)(2,1)S(1)} %fusion.31), channel_id=1, source_target_pairs={{0,2},{2,0},{1,3},{3,1},{4,6},{6,4},{5,7},{7,5},{8,10},{10,8},{9,1... | collective-permute-start | bytes 1572872 | tf_op jit(solution)/shard_map/ppermute | solution.py:65
  838.1 13.6 %all-to-all-start.2 = ((bf16[8,64,512]{2,1,0:T(8,128)(2,1)}), bf16[8,64,512]{2,1,0:T(8,128)(2,1)S(1)}, u32[]{:S(2)}, u32[]{:S(2)}) async-start(bf16[8,64,512]{2,1,0:T(8,128)(2,1)} %bitcast.59), calls=%async_computation.2 | async-start | bytes 1048576 | tf_op jit(solution)/shard_map/all_to_all | solution.py:106
  846.0 14.4 %collective-permute-start.21 = (bf16[2,64,2048]{2,1,0:T(8,128)(2,1)S(1)}, bf16[2,64,2048]{2,1,0:T(8,128)(2,1)}, u32[]{:S(2)}, u32[]{:S(2)}) collective-permute-start(bf16[2,64,2048]{2,1,0:T(8,128)(2,1)S(1)} %fusion.32), channel_id=1, source_target_pairs={{0,16},{16,0},{1,17},{17,1},{2,18},{18,2},{3,19},{19,3},{4,20},{20... | collective-permute-start | bytes 1572872 | tf_op jit(solution)/shard_map/ppermute | solution.py:65
  851.7 28.1 %all-to-all-start.5 = ((bf16[8,64,1024]{2,1,0:T(8,128)(2,1)}), bf16[8,64,1024]{2,1,0:T(8,128)(2,1)S(1)}, u32[]{:S(2)}, u32[]{:S(2)}) async-start(bf16[8,64,1024]{2,1,0:T(8,128)(2,1)} %bitcast.88), calls=%async_computation.5 | async-start | bytes 2097152 | tf_op jit(solution)/shard_map/all_to_all | solution.py:106
  855.3 5.1 copy-start.47
  863.2 14.7 %collective-permute-start.22 = (bf16[64,2048]{1,0:T(8,128)(2,1)}, bf16[64,2048]{1,0:T(8,128)(2,1)S(1)}, u32[]{:S(2)}, u32[]{:S(2)}) collective-permute-start(bf16[64,2048]{1,0:T(8,128)(2,1)} %fusion.37), channel_id=1, source_target_pairs={{0,2},{2,0},{1,3},{3,1},{4,6},{6,4},{5,7},{7,5},{8,10},{10,8},{9,1... | collective-permute-start | bytes 786440 | tf_op jit(solution)/shard_map/ppermute | solution.py:65
  (32 other events, 68.4 us)
Sparse Core Ops, SparseCore 0:
  204.0 126.9 all-gather.1
